TPU v7x, 512 devices: a whole 4x8x8 slice. The times are simulated.
512 devices in a mesh: head: 8 (over y), blk: 64 (over z, x, core).
Axes of the slice: x: 4, y: 8, z: 8, core: 2. Of those that a mesh axis runs over, the one named last changes fastest.
Arguments:
- residual: bfloat16 [12288, 2048], P('blk'), may hold values from -100 to 100
- lengths: int32 [64, 6], P('blk'), may hold values from 1 to 96, 192 in all within a row
- token_adapter_index: int32 [12288, 1], P('blk'), may hold values from 0 to 63; in each aligned block of 192 rows (0 to 191, 192 to 383, ...) at most 6 rows name the same one
- attention_norm_gain: float32 [2048], replicated, may hold values from 0.1 to 1.9
- query_key_weight: bfloat16 [2048, 4096], P('blk', 'head'), may hold values from -8 to 8
- value_weight: bfloat16 [2048, 2048], P('blk', 'head'), may hold values from -0.125 to 0.125
- head_second_weight: float32 [8], P('head'), may hold values from 0.2 to 0.8
- output_weight: bfloat16 [2048, 2048], P('blk', 'head'), may hold values from -0.125 to 0.125
- adapter_down_maps: bfloat16 [64, 2048, 16], P('blk', 'head'), may hold values from -0.125 to 0.125
- adapter_up_maps: bfloat16 [64, 16, 2048], P('blk'), may hold values from -1.5 to 1.5
- feedforward_norm_gain: float32 [2048], replicated, may hold values from 0.1 to 1.9
- gate_weight: bfloat16 [2048, 5632], P('blk', 'head'), may hold values from -0.125 to 0.125
- up_weight: bfloat16 [2048, 5632], P('blk', 'head'), may hold values from -0.125 to 0.125
- down_weight: bfloat16 [2048, 5632], P('blk', 'head'), may hold values from -0.078125 to 0.078125
Outputs:
- layer_out: bfloat16 [12288, 2048], P('blk', 'head')
Inputs may be any that keep to these rules, and one draw needn't show every extreme that they name: `lengths`: each row sums to 192, and its largest entry is 96. `token_adapter_index`: among the 192 tokens of one block no adapter is named more than 6 times, a bound that some block reaches.
All inputs are finite; a program needn't handle non-finite values.
Results may differ from a plain program's by a relative error of at most 0.011.
Values may be sent and summed in bfloat16 or wider, within the bound.
No kernel may reach another device: no remote copies, remote signals or barrier semaphores. Data moves between devices by JAX's collectives and lax.ppermute only.
A program may use at most 64 MiB of HBM per device.

v0:
```python
import jax
import jax.numpy as jnp
from jax import lax
from jax.sharding import PartitionSpec as P

HD = 128


adapter_scaling = 2.0
head_shrink = 0.8
neg_large = -1e30


def rms_scale(values, epsilon):
    return values * lax.rsqrt(jnp.mean(values * values, axis=-1, keepdims=True) + epsilon)


def masked_softmax(scores, allowed):
    scores = jnp.where(allowed, scores, neg_large)
    row_peak = jnp.max(scores, axis=-1, keepdims=True)
    raised = jnp.where(allowed, jnp.exp(scores - row_peak), 0.0)
    return raised / jnp.sum(raised, axis=-1, keepdims=True)


def request_mask(lengths_row, length_total):
    ends_at = jnp.cumsum(lengths_row)
    position = jnp.arange(length_total, dtype=jnp.int32)
    request = jnp.sum((position[:, None] >= ends_at[None, :]).astype(jnp.int32), axis=1)
    return (request[:, None] == request[None, :]) & (position[None, :] <= position[:, None])


def diff_head(qk_head, value_head, allowed, lambda_value):
    score_scale = 1.0 / qk_head.shape[-1] ** 0.5
    first_scores = (
        jnp.dot(qk_head[:, 0], qk_head[:, 2].T, precision=lax.Precision.HIGHEST) * score_scale
    )
    second_scores = (
        jnp.dot(qk_head[:, 1], qk_head[:, 3].T, precision=lax.Precision.HIGHEST) * score_scale
    )
    mixed = (
        masked_softmax(first_scores, allowed)
        - lambda_value * masked_softmax(second_scores, allowed)
    ).astype(jnp.bfloat16)
    attended = jnp.dot(mixed, value_head, preferred_element_type=jnp.float32)
    return (rms_scale(attended, 1e-05) * head_shrink).astype(jnp.bfloat16)


def weight_fold(leading, trailing, combine, initial):
    return combine(
        initial,
        (
            lax.all_gather(leading, "blk", axis=0, tiled=True),
            lax.all_gather(trailing, "blk", axis=0, tiled=True),
        ),
        jnp.int32(0),
    )


def head_total(partial_value):
    return lax.psum_scatter(
        partial_value.astype(jnp.bfloat16), "head", scatter_dimension=1, tiled=True
    ).astype(jnp.float32)


def row_products(source):

    def add_rows(totals, pieces, offset):
        return (
            jnp.dot(source, pieces[0], preferred_element_type=jnp.float32),
            jnp.dot(source, pieces[1], preferred_element_type=jnp.float32),
        )

    return add_rows


def per_device(
    residual,
    lengths,
    token_adapter_index,
    attention_norm_gain,
    query_key_weight,
    value_weight,
    head_second_weight,
    output_weight,
    adapter_down_maps,
    adapter_up_maps,
    feedforward_norm_gain,
    gate_weight,
    up_weight,
    down_weight,
):
    tokens = residual.shape[0]
    width = residual.shape[1]
    owners = lax.axis_size("blk")
    capacity = 2 * tokens // owners
    own_width = width // lax.axis_size("head")
    own_begin = lax.axis_index("head") * own_width
    inputs = residual.astype(jnp.float32)
    normed = (rms_scale(inputs, 1e-06) * attention_norm_gain).astype(jnp.bfloat16)
    qk_start = jnp.zeros((tokens, query_key_weight.shape[1]), jnp.float32)
    value_start = jnp.zeros((tokens, value_weight.shape[1]), jnp.float32)
    qk_local, value_local = weight_fold(
        query_key_weight, value_weight, row_products(normed), (qk_start, value_start)
    )
    qk_head = qk_local.reshape(tokens, 4, HD)
    value_head = value_local.astype(jnp.bfloat16)
    allowed = request_mask(lengths[0], tokens)
    head_out = diff_head(qk_head, value_head, allowed, head_second_weight[0])
    chosen = token_adapter_index[:, 0]
    owner_ids = jnp.arange(owners, dtype=jnp.int32)
    member = (chosen[:, None] == owner_ids[None, :]).astype(jnp.int32)
    earlier = jnp.cumsum(member, axis=0) - member
    within = jnp.sum(earlier * member, axis=1)
    target = chosen * capacity + within
    slot_ids = jnp.arange(owners * capacity, dtype=jnp.int32)
    dispatch = (slot_ids[:, None] == target[None, :]).astype(jnp.bfloat16)
    outgoing = jnp.dot(dispatch, head_out, preferred_element_type=jnp.float32).astype(jnp.bfloat16)
    outgoing = outgoing.reshape(owners, capacity, head_out.shape[1])
    received = lax.all_to_all(outgoing, "blk", split_axis=0, concat_axis=0, tiled=True)
    sources = received.shape[0]
    slot_count = received.shape[1]
    flat_heads_output = received.reshape(sources * slot_count, received.shape[2])
    reduced_rank_part = jnp.dot(
        flat_heads_output, adapter_down_maps[0], preferred_element_type=jnp.float32
    )
    reduced_rank_state = lax.psum(reduced_rank_part, "head").astype(jnp.bfloat16)
    adapter_delta = (
        adapter_scaling
        * jnp.dot(reduced_rank_state, adapter_up_maps[0], preferred_element_type=jnp.float32)
    ).astype(jnp.bfloat16)
    returned = lax.all_to_all(
        adapter_delta.reshape(sources, slot_count, width),
        "blk",
        split_axis=0,
        concat_axis=0,
        tiled=True,
    )
    delta_rows = lax.dot_general(
        dispatch,
        returned.reshape(owners * capacity, returned.shape[2]),
        (((0,), (0,)), ((), ())),
        preferred_element_type=jnp.float32,
    )
    delta_own = lax.dynamic_slice_in_dim(delta_rows, own_begin, own_width, 1)
    unit_count = down_weight.shape[1]

    def place_columns(totals, pieces, offset):
        columns = lax.dot_general(
            head_out, pieces[0], (((1,), (1,)), ((), ())), preferred_element_type=jnp.float32
        )
        return (columns, pieces[1])

    projected_start = jnp.zeros((tokens, width), jnp.float32)
    down_start = jnp.zeros((width, unit_count), jnp.bfloat16)
    projected, down_full = weight_fold(
        output_weight, down_weight, place_columns, (projected_start, down_start)
    )
    own_mid = (
        lax.dynamic_slice_in_dim(inputs, own_begin, own_width, 1)
        + head_total(projected)
        + delta_own
    )
    mid_full = lax.all_gather(own_mid.astype(jnp.bfloat16), "head", axis=1, tiled=True)
    ffn_in = (rms_scale(mid_full.astype(jnp.float32), 1e-06) * feedforward_norm_gain).astype(
        jnp.bfloat16
    )
    gate_start = jnp.zeros((tokens, gate_weight.shape[1]), jnp.float32)
    up_start = jnp.zeros((tokens, up_weight.shape[1]), jnp.float32)
    gate_act, upward = weight_fold(
        gate_weight, up_weight, row_products(ffn_in), (gate_start, up_start)
    )
    hidden_units = (jax.nn.silu(gate_act) * upward).astype(jnp.bfloat16)
    ffn_part = lax.dot_general(
        hidden_units, down_full, (((1,), (1,)), ((), ())), preferred_element_type=jnp.float32
    )
    return (own_mid + head_total(ffn_part)).astype(jnp.bfloat16)


def solution(mesh):
    return jax.shard_map(
        per_device,
        mesh=mesh,
        in_specs=(
            P("blk", None),
            P("blk", None),
            P("blk", None),
            P(),
            P("blk", "head"),
            P("blk", "head"),
            P("head"),
            P("blk", "head"),
            P("blk", "head", None),
            P("blk", None, None),
            P(),
            P("blk", "head"),
            P("blk", "head"),
            P("blk", "head"),
        ),
        out_specs=P("blk", "head"),
        check_vma=False,
    )
```

profile of v0, /device:TPU:1, one launch (start us, length us, event | category | flops | bytes accessed | tf_op | source)
XLA Modules:
  0.0 615.9 jit_solution(7784527970061427897)
XLA Ops:
  6.5 0.7 all-gather.7.cloned.1.call-update
  7.3 0.7 all-gather.9.cloned.1.call-update
  8.1 0.7 all-gather.11.cloned.1.call-update
  8.7 0.0 reduce-scatter.3.cloned.1.call-start
  8.8 0.8 reduce-window.18
  9.6 0.1 convert_reduce_fusion
  10.4 1.4 multiply_reduce_fusion
  11.7 88.2 %all-gather.7.cloned.1.call-done = bf16[2048,512]{1,0:T(8,128)(2,1)} async-done(((bf16[32,512]{1,0:T(8,128)(2,1)}), bf16[2048,512]{1,0:T(8,128)(2,1)}) %all-gather.7.cloned.1.call-update) | async-done | bytes 2097168 | tf_op jit(solution)/shard_map/all_gather | solution.py:52
  100.0 2.5 fusion.14
  102.5 0.1 reshape.92
  102.6 0.3 fusion.40
  102.9 0.4 fusion.42
  103.3 0.4 fusion.41
  103.7 0.1 fusion.22
  103.8 79.3 %all-gather.9.cloned.1.call-done = bf16[2048,256]{1,0:T(8,128)(2,1)} async-done(((bf16[32,256]{1,0:T(8,128)(2,1)}), bf16[2048,256]{1,0:T(8,128)(2,1)}) %all-gather.9.cloned.1.call-update) | async-done | bytes 1048592 | tf_op jit(solution)/shard_map/all_gather | solution.py:53
  183.1 2.0 multiply_reduce_fusion.1
  185.1 81.1 %all-gather.11.cloned.1.call-done = bf16[2048,256]{1,0:T(8,128)(2,1)} async-done(((bf16[32,256]{1,0:T(8,128)(2,1)}), bf16[2048,256]{1,0:T(8,128)(2,1)}) %all-gather.11.cloned.1.call-update) | async-done | bytes 1048592 | tf_op jit(solution)/shard_map/all_gather | solution.py:52
  266.2 2.7 convolution_convert_fusion.1
  268.9 0.0 all-gather.13.cloned.1.call-start
  269.0 0.5 all-gather.13.cloned.1.call-update
  269.5 0.5 all-gather.15.cloned.1.call-update
  270.1 0.7 all-gather.17.cloned.1.call-update
  270.9 0.6 reduce-window.19
  271.5 0.2 slice_reduce_fusion
  271.7 0.1 bitcast_bitcast_fusion
  271.9 0.3 convolution_convert_fusion.2
  272.1 0.1 reshape.95
  272.2 19.5 %all_to_all.10 = bf16[64,6,256]{2,1,0:T(8,128)(2,1)S(1)} all-to-all(bf16[64,6,256]{2,1,0:T(8,128)(2,1)S(1)} %reshape.95), channel_id=1, replica_groups=mesh['head'=8,'blk'=64] {'blk'}, dimensions={0} | all-to-all | bytes 393216 | tf_op jit(solution)/shard_map/all_to_all | solution.py:119
  291.7 0.1 reshape.96
  291.8 0.2 fusion.35
  292.0 23.2 %psum.7 = bf16[384,16]{0,1:T(8,128)(2,1)S(1)} all-reduce(f32[384,16]{0,1:T(8,128)S(1)} %fusion.35), channel_id=1, replica_groups=mesh['head'=8,'blk'=64] {'head'}, use_global_device_ids=true, to_apply=%region_12.13 | all-reduce | flops 6144 | bytes 36864 | tf_op jit(solution)/shard_map/psum | solution.py:126
  315.2 0.6 multiply_convert_fusion
  315.8 1.6 reshape.97
  317.4 11.3 %all-to-all-start.1 = ((bf16[64,6,2048]{2,1,0:T(8,128)(2,1)}), bf16[64,6,2048]{2,1,0:T(8,128)(2,1)S(1)}, u32[]{:S(2)}, u32[]{:S(2)}) async-start(bf16[64,6,2048]{2,1,0:T(8,128)(2,1)} %reshape.97), calls=%async_computation.2 | async-start | bytes 4194304 | tf_op jit(solution)/shard_map/all_to_all | solution.py:131
  328.7 0.0 reduce-scatter.5.cloned.1.call-start
  328.7 1.4 convert_element_type.59
  330.1 52.8 %all-to-all-done.1 = bf16[64,6,2048]{2,1,0:T(8,128)(2,1)S(1)} async-done(((bf16[64,6,2048]{2,1,0:T(8,128)(2,1)}), bf16[64,6,2048]{2,1,0:T(8,128)(2,1)S(1)}, u32[]{:S(2)}, u32[]{:S(2)}) %all-to-all-start.1) | async-done | bytes 1572896 | tf_op jit(solution)/shard_map/all_to_all | solution.py:131
  382.9 1.4 reshape.98
  384.3 2.0 fusion.12
  386.4 1.0 fusion.37
  387.4 20.7 %all_gather.24 = bf16[192,2048]{1,0:T(8,128)(2,1)S(1)} all-gather(bf16[192,256]{1,0:T(8,128)(2,1)S(1)} %fusion.37), channel_id=1, replica_groups=mesh['head'=8,'blk'=64] {'head'}, dimensions={1}, use_global_device_ids=true | all-gather | bytes 884736 | tf_op jit(solution)/shard_map/all_gather | solution.py:163
  408.1 0.2 fusion
  408.4 2.7 fusion.17
  411.1 73.2 %all-gather.15.cloned.1.call-done = bf16[2048,704]{1,0:T(8,128)(2,1)} async-done(((bf16[32,704]{1,0:T(8,128)(2,1)}), bf16[2048,704]{1,0:T(8,128)(2,1)}) %all-gather.15.cloned.1.call-update) | async-done | bytes 2883600 | tf_op jit(solution)/shard_map/all_gather | solution.py:53
  484.3 85.3 %all-gather.17.cloned.1.call-done = bf16[2048,704]{1,0:T(8,128)(2,1)} async-done(((bf16[32,704]{1,0:T(8,128)(2,1)}), bf16[2048,704]{1,0:T(8,128)(2,1)}) %all-gather.17.cloned.1.call-update) | async-done | bytes 2883600 | tf_op jit(solution)/shard_map/all_gather | solution.py:53
  569.6 5.8 convolution_convert_fusion
  575.4 32.0 %reduce-scatter.5.cloned.1.call-done = bf16[192,256]{1,0:T(8,128)(2,1)} async-done(((bf16[192,2048]{1,0:T(8,128)(2,1)}), bf16[192,256]{1,0:T(8,128)(2,1)}) %reduce-scatter.5.cloned.1.call-update) | async-done | bytes 98320 | tf_op jit(solution)/shard_map/reduce_scatter | solution.py:60
  607.4 1.7 add_convert_fusion
  (32 shorter events, 0.4 us)
Async XLA Ops:
  6.5 308.7 %copy-start = (bf16[1,16,2048]{2,1,0:T(8,128)(2,1)S(1)}, bf16[1,16,2048]{2,1,0:T(8,128)(2,1)}, u32[]{:S(2)}) copy-start(bf16[1,16,2048]{2,1,0:T(8,128)(2,1)} %param.23) | copy-start | bytes 196612
  6.5 93.4 %all-gather.7.cloned.1.call-start = ((), (), s32[]{:S(2)}) async-start(), calls=%async_computation.4 | async-start | bytes 2129920 | tf_op jit(solution)/shard_map/all_gather | solution.py:52
  7.3 175.8 %all-gather.9.cloned.1.call-start = ((), (), s32[]{:S(2)}) async-start(), calls=%async_computation.5 | async-start | bytes 1064960 | tf_op jit(solution)/shard_map/all_gather | solution.py:53
  8.0 258.2 %all-gather.11.cloned.1.call-start = ((), (), s32[]{:S(2)}) async-start(), calls=%async_computation.6 | async-start | bytes 1064960 | tf_op jit(solution)/shard_map/all_gather | solution.py:52
  8.7 377.6 %reduce-scatter.3.cloned.1.call-start = ((), (), s32[]{:S(2)}) async-start(), calls=%async_computation.7 | async-start | bytes 884736 | tf_op jit(solution)/shard_map/reduce_scatter | solution.py:60
  102.5 80.6 %copy-start.1 = (bf16[192,2048]{1,0:T(8,128)(2,1)S(1)}, bf16[192,2048]{1,0:T(8,128)(2,1)}, u32[]{:S(2)}) copy-start(bf16[192,2048]{1,0:T(8,128)(2,1)} %param.14) | copy-start | bytes 2359300
  102.5 80.6 %copy-start.5 = (f32[2048]{0:T(1024)S(1)}, f32[2048]{0:T(1024)}, u32[]{:S(2)}) copy-start(f32[2048]{0:T(1024)} %param.17) | copy-start | bytes 24580
  185.1 85.8 %copy-start.3 = (s32[192,1]{0,1:T(1,128)S(1)}, s32[192,1]{0,1:T(1,128)}, u32[]{:S(2)}) copy-start(s32[192,1]{0,1:T(1,128)} %param.16) | copy-start | bytes 2308
  268.9 22.9 %copy-start.4 = (bf16[1,256,16]{1,2,0:T(8,128)(2,1)S(1)}, bf16[1,256,16]{1,2,0:T(8,128)(2,1)}, u32[]{:S(2)}) copy-start(bf16[1,256,16]{1,2,0:T(8,128)(2,1)} %param.22) | copy-start | bytes 24580
  268.9 139.4 %all-gather.13.cloned.1.call-start = ((), (), s32[]{:S(2)}) async-start(), calls=%async_computation.8 | async-start | bytes 3194880 | tf_op jit(solution)/shard_map/all_gather | solution.py:52
  269.5 214.8 %all-gather.15.cloned.1.call-start = ((), (), s32[]{:S(2)}) async-start(), calls=%async_computation.9 | async-start | bytes 3194880 | tf_op jit(solution)/shard_map/all_gather | solution.py:53
  270.1 299.5 %all-gather.17.cloned.1.call-start = ((), (), s32[]{:S(2)}) async-start(), calls=%async_computation.10 | async-start | bytes 3194880 | tf_op jit(solution)/shard_map/all_gather | solution.py:53
  317.4 65.5 %all-to-all-start.1 = ((bf16[64,6,2048]{2,1,0:T(8,128)(2,1)}), bf16[64,6,2048]{2,1,0:T(8,128)(2,1)S(1)}, u32[]{:S(2)}, u32[]{:S(2)}) async-start(bf16[64,6,2048]{2,1,0:T(8,128)(2,1)} %reshape.97), calls=%async_computation.2 | async-start | bytes 4194304 | tf_op jit(solution)/shard_map/all_to_all | solution.py:131
  328.7 278.7 %reduce-scatter.5.cloned.1.call-start = ((), (), s32[]{:S(2)}) async-start(), calls=%async_computation.11 | async-start | bytes 884736 | tf_op jit(solution)/shard_map/reduce_scatter | solution.py:60
  386.3 22.0 %copy-start.6 = (f32[2048]{0:T(1024)S(1)}, f32[2048]{0:T(1024)}, u32[]{:S(2)}) copy-start(f32[2048]{0:T(1024)} %param.24) | copy-start | bytes 24580
  411.1 196.3 %copy-start.2 = (bf16[192,256]{1,0:T(8,128)(2,1)S(1)}, bf16[192,256]{1,0:T(8,128)(2,1)}, u32[]{:S(2)}) copy-start(bf16[192,256]{1,0:T(8,128)(2,1)} %reduce-scatter.3.cloned.1.call-done) | copy-start | bytes 294916
Sparse Core Ops, SparseCore 0:
  10.7 89.2 all-gather.6
  103.3 79.7 all-gather.8
  186.4 79.7 all-gather.10
  269.0 32.9 reduce-scatter.2
  305.8 92.7 all-gather.12
  402.3 81.9 all-gather.14
  488.2 81.3 all-gather.16
  575.5 31.8 reduce-scatter.4
where the time goes:
time: 620 us; the launch traced here: 616 us
  waiting for transfers between devices  496 us (80%)
  blocking collectives  63.4 us (10%)
  matrix products  19.3 us (3%)
  between operations  14.4 us (2%)
  starting transfers between devices  11.5 us (2%)
  other arithmetic  7.53 us (1%)
    all_gather x3, waiting for transfers between devices, weight_fold(): lax.all_gather(trailing, 'blk', axis=0, tiled=True)  238 us
    all_gather x3, waiting for transfers between devices, weight_fold(): lax.all_gather(leading, 'blk', axis=0, tiled=True)  169 us
    all_to_all x1, waiting for transfers between devices, per_device(): lax.all_to_all(adapter_delta.reshape(sources, slot_count, width), 'blk',...  52.8 us
    reduce_scatter x2, waiting for transfers between devices, head_total(): lax.psum_scatter(partial_value.astype(jnp.bfloat16), 'head', scatter_dime...  32 us
    psum x1, blocking collectives, per_device(): lax.psum(reduced_rank_part, 'head').astype(jnp.bfloat16)  23.2 us
    all_gather x1, blocking collectives, per_device(): lax.all_gather(own_mid.astype(jnp.bfloat16), 'head', axis=1, tiled=True)  20.7 us
    all_to_all x1, blocking collectives, per_device(): lax.all_to_all(outgoing, 'blk', split_axis=0, concat_axis=0, tiled=True)  19.5 us
  transfers between devices with their start and end apart: 9, of which 7 were waited for; matrix products, arithmetic and copies ran while one was open for 3% of the time, Pallas kernels for 0%

commit v1 on v0

v1 whole, which is shorter than its diff:
```python
import jax
import jax.numpy as jnp
from jax import lax
from jax.sharding import Mesh
from jax.sharding import PartitionSpec as P

HD = 128
RANK = 16

adapter_scaling = 2.0
head_shrink = 0.8
neg_large = -1e30

BLK = ("z", "x", "core")


def rms_scale(values, epsilon):
    return values * lax.rsqrt(jnp.mean(values * values, axis=-1, keepdims=True) + epsilon)


def masked_softmax(scores, allowed):
    scores = jnp.where(allowed, scores, neg_large)
    row_peak = jnp.max(scores, axis=-1, keepdims=True)
    raised = jnp.where(allowed, jnp.exp(scores - row_peak), 0.0)
    return raised / jnp.sum(raised, axis=-1, keepdims=True)


def request_mask(lengths_row, length_total):
    count = lengths_row.shape[0]
    order = jnp.arange(count, dtype=jnp.int32)
    ends_at = jnp.sum(jnp.where(order[None, :] <= order[:, None], lengths_row[None, :], 0), axis=1)
    position = jnp.arange(length_total, dtype=jnp.int32)
    request = jnp.sum((position[:, None] >= ends_at[None, :]).astype(jnp.int32), axis=1)
    return (request[:, None] == request[None, :]) & (position[None, :] <= position[:, None])


def diff_head(qk_head, value_head, allowed, lambda_value):
    score_scale = 1.0 / HD**0.5
    parts = [qk_head[:, i * HD : (i + 1) * HD] for i in range(4)]

    def scores(left, right):
        return (
            lax.dot_general(left, right, (((1,), (1,)), ((), ())), precision=lax.Precision.HIGHEST)
            * score_scale
        )

    mixed = (
        masked_softmax(scores(parts[0], parts[2]), allowed)
        - lambda_value * masked_softmax(scores(parts[1], parts[3]), allowed)
    ).astype(jnp.bfloat16)
    attended = jnp.dot(mixed, value_head, preferred_element_type=jnp.float32)
    return (rms_scale(attended, 1e-05) * head_shrink).astype(jnp.bfloat16)


def exchange(blocks, axis):
    return lax.all_to_all(blocks, axis, split_axis=0, concat_axis=0, tiled=True)


def spread(block, axis):
    return exchange(jnp.broadcast_to(block[None], (lax.axis_size(axis), *block.shape)), axis)


def sibling(block):
    return lax.ppermute(block, "core", [(0, 1), (1, 0)])


def fold_map(rank_rows):
    half = rank_rows.shape[1] // 2
    return jnp.concatenate([rank_rows[:, :half], rank_rows[:, half:]], axis=0)


def unfold_map(folded, owners):
    stacked = folded.reshape(owners, 2, RANK, folded.shape[1])
    return [stacked[:, i].reshape(owners * RANK, folded.shape[1]) for i in range(2)]


def per_device(
    residual,
    lengths,
    token_adapter_index,
    attention_norm_gain,
    query_key_weight,
    value_weight,
    head_second_weight,
    output_weight,
    adapter_down_maps,
    adapter_up_maps,
    feedforward_norm_gain,
    gate_weight,
    up_weight,
    down_weight,
):
    tokens, width = residual.shape
    groups = lax.axis_size("head")
    owners = lax.axis_size(BLK)
    own_width = width // groups
    own_begin = lax.axis_index("head") * own_width
    units = gate_weight.shape[1]
    qk_width = query_key_weight.shape[1]
    value_width = value_weight.shape[1]

    down_map = fold_map(adapter_down_maps[0].T)
    up_map = fold_map(lax.dynamic_slice_in_dim(adapter_up_maps[0], own_begin, own_width, 1))

    late = lax.all_gather(
        jnp.concatenate([gate_weight, up_weight, up_map, down_weight], axis=1),
        BLK,
        axis=0,
        tiled=True,
    )

    early = jnp.concatenate([query_key_weight, value_weight, output_weight, down_map], axis=1)
    early_width = early.shape[1]
    mine = spread(spread(early, "z"), "x")
    other = sibling(mine)
    first = lax.axis_index("core") == 0
    both = jnp.stack([jnp.where(first, mine, other), jnp.where(first, other, mine)], axis=2)
    both = both.transpose(1, 0, 2, 3, 4).reshape(width, early_width)
    qk_full = both[:, :qk_width]
    value_full = both[:, qk_width : qk_width + value_width]
    out_full = both[:, qk_width + value_width : qk_width + 2 * value_width]
    down_maps = unfold_map(both[:, qk_width + 2 * value_width :], owners)

    inputs = residual.astype(jnp.float32)
    normed = (rms_scale(inputs, 1e-06) * attention_norm_gain).astype(jnp.bfloat16)
    qk_head = jnp.dot(normed, qk_full, preferred_element_type=jnp.float32)
    value_head = jnp.dot(normed, value_full, preferred_element_type=jnp.float32).astype(jnp.bfloat16)
    allowed = request_mask(lengths[0], tokens)
    head_out = diff_head(qk_head, value_head, allowed, head_second_weight[0])

    coordinate = jnp.arange(owners * RANK, dtype=jnp.int32)
    chosen = coordinate[None, :] // RANK == token_adapter_index
    lift = (jnp.arange(RANK, dtype=jnp.int32)[:, None] == coordinate[None, :] % RANK)
    half = value_width // 2
    all_coordinates = sum(
        lax.dot_general(
            head_out[:, i * half : (i + 1) * half],
            down_maps[i],
            (((1,), (1,)), ((), ())),
            preferred_element_type=jnp.float32,
        )
        for i in range(2)
    )
    low_part = lax.dot_general(
        lift.astype(jnp.float32),
        jnp.where(chosen, all_coordinates, 0.0),
        (((1,), (1,)), ((), ())),
        precision=lax.Precision.HIGHEST,
    )
    low_high = lax.reduce_precision(low_part, 8, 7)
    low_rows = jnp.concatenate([low_high, low_part - low_high], axis=0).astype(jnp.bfloat16)
    low_rows = jnp.pad(low_rows, ((0, 0), (0, own_width - tokens)))

    share = lax.dot_general(
        head_out, out_full, (((1,), (1,)), ((), ())), preferred_element_type=jnp.float32
    ).astype(jnp.bfloat16)
    share = share.reshape(tokens, groups, own_width).transpose(1, 0, 2)
    sent = jnp.concatenate(
        [share, jnp.broadcast_to(low_rows[None], (groups, *low_rows.shape))], axis=1
    )
    total = jnp.sum(exchange(sent, "head").astype(jnp.float32), axis=0)
    low_rank = (total[tokens : tokens + RANK, :tokens] + total[tokens + RANK :, :tokens]).astype(
        jnp.bfloat16
    )
    lifted = lax.dot_general(
        low_rank,
        lift.astype(jnp.bfloat16),
        (((0,), (0,)), ((), ())),
        preferred_element_type=jnp.float32,
    )
    routed = jnp.where(chosen, lifted, 0.0).astype(jnp.bfloat16)
    up_maps = unfold_map(late[:, 2 * units : 2 * units + own_width // 2], owners)
    delta_own = (
        adapter_scaling
        * jnp.concatenate(
            [jnp.dot(routed, part, preferred_element_type=jnp.float32) for part in up_maps], axis=1
        )
    ).astype(jnp.bfloat16)
    own_mid = (
        lax.dynamic_slice_in_dim(inputs, own_begin, own_width, 1)
        + total[:tokens]
        + delta_own.astype(jnp.float32)
    )
    mid_full = spread(own_mid.astype(jnp.bfloat16), "head").transpose(1, 0, 2).reshape(tokens, width)
    ffn_in = (rms_scale(mid_full.astype(jnp.float32), 1e-06) * feedforward_norm_gain).astype(
        jnp.bfloat16
    )
    both_acts = jnp.dot(ffn_in, late[:, : 2 * units], preferred_element_type=jnp.float32)
    hidden_units = (jax.nn.silu(both_acts[:, :units]) * both_acts[:, units:]).astype(jnp.bfloat16)
    piece = lax.dot_general(
        hidden_units,
        late[:, 2 * units + own_width // 2 :],
        (((1,), (1,)), ((), ())),
        preferred_element_type=jnp.float32,
    ).astype(jnp.bfloat16)
    piece = piece.reshape(tokens, groups, own_width).transpose(1, 0, 2)
    return (own_mid + jnp.sum(exchange(piece, "head").astype(jnp.float32), axis=0)).astype(
        jnp.bfloat16
    )


def solution(mesh):
    fine = Mesh(mesh.devices.reshape(mesh.devices.shape[0], 8, 4, 2), ("head", *BLK))
    return jax.shard_map(
        per_device,
        mesh=fine,
        in_specs=(
            P(BLK, None),
            P(BLK, None),
            P(BLK, None),
            P(),
            P(BLK, "head"),
            P(BLK, "head"),
            P("head"),
            P(BLK, "head"),
            P(BLK, "head", None),
            P(BLK, None, None),
            P(),
            P(BLK, "head"),
            P(BLK, "head"),
            P(BLK, "head"),
        ),
        out_specs=P(BLK, "head"),
        check_vma=False,
    )
```

time: 620 us -> 193 us (0.31)
  waiting for transfers between devices: 496 us -> 28.4 us
  blocking collectives: 63.4 us -> 109 us
  matrix products: 19.3 us -> 9.57 us
    all_gather x6 -> x1, waiting for transfers between devices: 407 us -> 0.02 us  [per_device(): lax.all_gather(jnp.concatenate([gate_weight, up_weight, up_map, down_weig...]
    all_to_all x1 -> x4, blocking collectives: 19.5 us -> 109 us  [exchange(): return lax.all_to_all(blocks, axis, split_axis=0, concat_axis=0, tiled=True)]
    reduce_scatter x2 -> x0, waiting for transfers between devices: 32 us -> none  [head_total(): lax.psum_scatter(partial_value.astype(jnp.bfloat16), 'head', scatter_dime...]
    all_to_all x1, waiting for transfers between devices: 52.8 us -> 25 us  [exchange(): return lax.all_to_all(blocks, axis, split_axis=0, concat_axis=0, tiled=True)]
    psum x1 -> x0, blocking collectives: 23.2 us -> none  [per_device(): lax.psum(reduced_rank_part, 'head').astype(jnp.bfloat16)]
    all_gather x1 -> x0, blocking collectives: 20.7 us -> none  [per_device(): lax.all_gather(own_mid.astype(jnp.bfloat16), 'head', axis=1, tiled=True)]
    dot_general x10 -> x12, matrix products: 17.4 us -> 7.61 us  [the longest x1 1.82 us: per_device(): lax.dot_general(head_out, out_full, (((1,), (1,)), ((), ())), preferred_e...]
  transfers between devices with their start and end apart: 9 -> 3, of which waited for: 7 -> 2; matrix products, arithmetic and copies ran while one was open for 3% -> 8% of each run, Pallas kernels for 0% -> 0%
where the time goes in v1:
time: 193 us; the launch traced here: 192 us
  blocking collectives  109 us (56%)
  waiting for transfers between devices  28.4 us (15%)
  between operations  14.3 us (7%)
  starting transfers between devices  13.1 us (7%)
  matrix products  9.57 us (5%)
  other arithmetic  8.94 us (5%)
  local copies, waits for them, and re-layouts  8.7 us (5%)
    all_to_all x4, blocking collectives, exchange(): return lax.all_to_all(blocks, axis, split_axis=0, concat_axis=0, tiled=True)  109 us
    all_to_all x1, waiting for transfers between devices, exchange(): return lax.all_to_all(blocks, axis, split_axis=0, concat_axis=0, tiled=True)  25 us
    all_to_all x1, starting transfers between devices, exchange(): return lax.all_to_all(blocks, axis, split_axis=0, concat_axis=0, tiled=True)  7.28 us
    ppermute x1, starting transfers between devices, sibling(): return lax.ppermute(block, 'core', [(0, 1), (1, 0)])  5.85 us
  transfers between devices with their start and end apart: 3, of which 2 were waited for; matrix products, arithmetic and copies ran while one was open for 8% of the time, Pallas kernels for 0%

profile of v1, /device:TPU:1, one launch (start us, length us, event | category | flops | bytes accessed | tf_op | source)
XLA Modules:
  0.0 192.2 jit_solution(13659659492032525438)
XLA Ops:
  6.5 0.8 copy-done
  7.4 1.6 concatenate.27
  9.0 0.7 fusion.63
  9.7 0.8 maximum_maximum_fusion
  10.6 28.0 %all_to_all.25 = bf16[8,32,1152]{2,1,0:T(8,128)(2,1)S(1)} all-to-all(bf16[8,32,1152]{2,1,0:T(8,128)(2,1)S(1)} %broadcast_in_dim.39), channel_id=1, replica_groups=mesh['head'=8,'z'=8,'x'=4,'core'=2] {'z'}, dimensions={0} | all-to-all | bytes 1179648 | tf_op jit(solution)/shard_map/all_to_all | solution.py:56
  38.6 0.2 broadcast_in_dim.40
  38.8 30.5 %all_to_all.26 = bf16[4,8,32,1152]{3,2,1,0:T(8,128)(2,1)S(1)} all-to-all(bf16[4,8,32,1152]{3,2,1,0:T(8,128)(2,1)S(1)} %broadcast_in_dim.40), channel_id=1, replica_groups=mesh['head'=8,'z'=8,'x'=4,'core'=2] {'x'}, dimensions={0} | all-to-all | bytes 4718592 | tf_op jit(solution)/shard_map/all_to_all | solution.py:56
  69.3 1.7 copy.24
  71.0 5.8 %collective-permute-start = (bf16[4,8,32,1152]{3,2,0,1:T(8,128)(2,1)}, bf16[4,8,32,1152]{3,2,0,1:T(8,128)(2,1)}, u32[]{:S(2)}, u32[]{:S(2)}) collective-permute-start(bf16[4,8,32,1152]{3,2,0,1:T(8,128)(2,1)} %copy.24), channel_id=1, source_target_pairs={{0,1},{1,0},{2,3},{3,2},{4,5},{5,4},{6,7},{7,6},{8,9},{9,8},{10,11... | collective-permute-start | bytes 7077896 | tf_op jit(solution)/shard_map/ppermute | solution.py:64
  77.5 0.1 select_reduce_fusion
  77.6 0.1 convert_reduce_fusion.2
  77.7 0.2 multiply_reduce_fusion
  78.0 3.4 %collective-permute-done = bf16[4,8,32,1152]{3,2,0,1:T(8,128)(2,1)} collective-permute-done((bf16[4,8,32,1152]{3,2,0,1:T(8,128)(2,1)}, bf16[4,8,32,1152]{3,2,0,1:T(8,128)(2,1)}, u32[]{:S(2)}, u32[]{:S(2)}) %collective-permute-start) | collective-permute-done | bytes 2359328 | tf_op jit(solution)/shard_map/ppermute | solution.py:64
  81.3 2.2 %select_bitcast_fusion.1 = (bf16[4,8,1,32,1152]{4,3,2,0,1:T(8,128)(2,1)S(1)}, bf16[4,8,1,32,1152]{4,3,2,0,1:T(8,128)(2,1)S(1)}) fusion(bf16[4,8,32,1152]{3,2,0,1:T(8,128)(2,1)} %collective-permute-done, pred[]{:T(512)S(6)} %eq.55, bf16[4,8,32,1152]{3,2,1,0:T(8,128)(2,1)S(1)} %all_to_all.26), kind=kLoop, calls=%fused_computation.8 | loop fusion | flops 2359296 | bytes 9437185 | tf_op jit(solution)/shard_map/stack | solution.py:117
  83.5 0.5 pad_maximum_fusion
  84.1 0.2 copy-done.5
  84.2 0.6 fusion.7
  84.9 1.4 copy-done.1
  86.3 0.4 fusion.64
  86.6 0.4 fusion.65
  87.0 0.1 fusion.26
  87.1 2.0 %multiply_reduce_fusion.1 = (f32[192]{0:T(256)S(1)}, f32[192,256]{1,0:T(8,128)S(1)}) fusion(bf16[2048,1152]{1,0:T(8,128)(2,1)} %bitcast.52, f32[2048]{0:T(1024)S(1)} %copy-done.5, f32[192]{0:T(256)S(1)} %add_rsqrt_fusion.2, bf16[192,2048]{1,0:T(8,128)(2,1)S(1)} %copy-done.2, f32[192,192]{0,1:T(8,128)S(1)} %get-tuple-element.22, ...), kind=kOutput, calls=%fused_computation.45 | convolution fusion | flops 222363456 | bytes 2441472 | tf_op jit(solution)/shard_map/dot_general | solution.py:51
  89.1 0.1 multiply_convert_fusion.6
  89.2 1.8 convolution_convert_fusion
  91.2 0.3 fusion.41
  91.4 0.3 copy-done.4
  91.7 0.3 fusion.10
  92.0 0.5 reduce-precision_convert_fusion
  92.5 1.0 pad_maximum_fusion.1
  93.5 7.3 %all-to-all-start.2 = ((bf16[8,224,256]{2,1,0:T(8,128)(2,1)}), bf16[8,224,256]{2,1,0:T(8,128)(2,1)S(1)}, u32[]{:S(2)}, u32[]{:S(2)}) async-start(bf16[8,224,256]{2,1,0:T(8,128)(2,1)} %pad_maximum_fusion.1), calls=%async_computation.2 | async-start | bytes 1835008 | tf_op jit(solution)/shard_map/all_to_all | solution.py:56
  100.8 1.3 convert_element_type.72
  102.1 25.0 %all-to-all-done.2 = bf16[8,224,256]{2,1,0:T(8,128)(2,1)S(1)} async-done(((bf16[8,224,256]{2,1,0:T(8,128)(2,1)}), bf16[8,224,256]{2,1,0:T(8,128)(2,1)S(1)}, u32[]{:S(2)}, u32[]{:S(2)}) %all-to-all-start.2) | async-done | bytes 917536 | tf_op jit(solution)/shard_map/all_to_all | solution.py:56
  127.2 0.1 convert_reduce_fusion
  127.3 0.3 fusion.11
  127.6 1.1 slice.123
  128.8 0.3 fusion.69
  129.0 0.3 fusion.68
  129.3 1.1 fusion.58
  130.5 26.1 %all_to_all.27 = bf16[8,192,256]{2,1,0:T(8,128)(2,1)S(1)} all-to-all(bf16[8,192,256]{2,1,0:T(8,128)(2,1)S(1)} %broadcast_in_dim.45), channel_id=1, replica_groups=mesh['head'=8,'z'=8,'x'=4,'core'=2] {'head'}, dimensions={0} | all-to-all | bytes 1572864 | tf_op jit(solution)/shard_map/all_to_all | solution.py:56
  156.6 0.1 convert_bitcast_fusion
  156.8 0.2 copy.32
  156.9 0.2 fusion.9
  157.2 0.3 copy-done.6
  157.5 1.4 fusion
  158.9 1.2 fusion.4
  160.2 24.5 %all_to_all.28 = bf16[8,192,256]{2,1,0:T(8,128)(2,1)S(1)} all-to-all(bf16[8,192,256]{2,1,0:T(8,128)(2,1)S(1)} %bitcast.55), channel_id=1, replica_groups=mesh['head'=8,'z'=8,'x'=4,'core'=2] {'head'}, dimensions={0} | all-to-all | bytes 1572864 | tf_op jit(solution)/shard_map/all_to_all | solution.py:56
  184.6 0.1 convert_reduce_fusion.1
  184.7 0.7 add_convert_fusion
  (30 shorter events, 0.4 us)
Async XLA Ops:
  6.5 0.8 copy-start
  6.5 121.1 %all-gather.2.cloned.1.call-start = ((), (), s32[]{:S(2)}) async-start(), calls=%async_computation.5 | async-start | bytes 9584640 | tf_op jit(solution)/shard_map/all_gather | solution.py:105
  69.3 8.2 %copy-start.7 = (s32[1,6]{1,0:T(1,128)S(1)}, s32[1,6]{1,0:T(1,128)}, u32[]{:S(2)}) copy-start(s32[1,6]{1,0:T(1,128)} %param.15) | copy-start | bytes 76
  69.3 8.4 %copy-start.2 = (bf16[192,2048]{1,0:T(8,128)(2,1)S(1)}, bf16[192,2048]{1,0:T(8,128)(2,1)}, u32[]{:S(2)}) copy-start(bf16[192,2048]{1,0:T(8,128)(2,1)} %param.14) | copy-start | bytes 2359300
  71.0 10.3 %collective-permute-start = (bf16[4,8,32,1152]{3,2,0,1:T(8,128)(2,1)}, bf16[4,8,32,1152]{3,2,0,1:T(8,128)(2,1)}, u32[]{:S(2)}, u32[]{:S(2)}) collective-permute-start(bf16[4,8,32,1152]{3,2,0,1:T(8,128)(2,1)} %copy.24), channel_id=1, source_target_pairs={{0,1},{1,0},{2,3},{3,2},{4,5},{5,4},{6,7},{7,6},{8,9},{9,8},{10,11... | collective-permute-start | bytes 7077896 | tf_op jit(solution)/shard_map/ppermute | solution.py:64
  83.5 0.7 copy-start.5
  84.0 2.2 %copy-start.1 = (bf16[4,8,2,32,1152]{4,3,2,0,1:T(8,128)(2,1)}, bf16[4,8,2,32,1152]{4,3,2,0,1:T(8,128)(2,1)S(1)}, u32[]{:S(2)}) copy-start(bf16[4,8,2,32,1152]{4,3,2,0,1:T(8,128)(2,1)S(1)} %pad_maximum_fusion) | copy-start | bytes 14155780
  91.0 0.7 copy-start.4
  93.5 33.7 %all-to-all-start.2 = ((bf16[8,224,256]{2,1,0:T(8,128)(2,1)}), bf16[8,224,256]{2,1,0:T(8,128)(2,1)S(1)}, u32[]{:S(2)}, u32[]{:S(2)}) async-start(bf16[8,224,256]{2,1,0:T(8,128)(2,1)} %pad_maximum_fusion.1), calls=%async_computation.2 | async-start | bytes 1835008 | tf_op jit(solution)/shard_map/all_to_all | solution.py:56
  129.3 27.9 %copy-start.3 = (bf16[2048,2240]{1,0:T(8,128)(2,1)S(1)}, bf16[2048,2240]{1,0:T(8,128)(2,1)}, u32[]{:S(2)}) copy-start(bf16[2048,2240]{1,0:T(8,128)(2,1)} %all-gather.2.cloned.1.call-done) | copy-start | bytes 27525124
  156.8 0.7 copy-start.6
Sparse Core Ops, SparseCore 0:
  10.7 97.2 all-gather.1

commit v2 on v1

--- a/solution.py
+++ b/solution.py
@@ -102,8 +102,19 @@
     down_map = fold_map(adapter_down_maps[0].T)
     up_map = fold_map(lax.dynamic_slice_in_dim(adapter_up_maps[0], own_begin, own_width, 1))
 
+    acts_local = jnp.concatenate([gate_weight, up_weight, down_weight], axis=1)
+    acts_paired = lax.ppermute(acts_local, "head", [(i, i ^ 1) for i in range(groups)])
     late = lax.all_gather(
-        jnp.concatenate([gate_weight, up_weight, up_map, down_weight], axis=1),
+        jnp.concatenate(
+            [
+                acts_local[:, : 2 * units],
+                acts_paired[:, : 2 * units],
+                up_map,
+                acts_local[:, 2 * units :],
+                acts_paired[:, 2 * units :],
+            ],
+            axis=1,
+        ),
         BLK,
         axis=0,
         tiled=True,
@@ -169,7 +180,7 @@
         preferred_element_type=jnp.float32,
     )
     routed = jnp.where(chosen, lifted, 0.0).astype(jnp.bfloat16)
-    up_maps = unfold_map(late[:, 2 * units : 2 * units + own_width // 2], owners)
+    up_maps = unfold_map(late[:, 4 * units : 4 * units + own_width // 2], owners)
     delta_own = (
         adapter_scaling
         * jnp.concatenate(
@@ -181,22 +192,32 @@
         + total[:tokens]
         + delta_own.astype(jnp.float32)
     )
-    mid_full = spread(own_mid.astype(jnp.bfloat16), "head").transpose(1, 0, 2).reshape(tokens, width)
+    part = tokens // 2
+    halves = own_mid.astype(jnp.bfloat16).reshape(1, 2, part, own_width)
+    halves = jnp.broadcast_to(halves, (groups // 2, 2, part, own_width))
+    mid_full = exchange(halves.reshape(groups, part, own_width), "head")
+    mid_full = mid_full.transpose(1, 0, 2).reshape(part, width)
     ffn_in = (rms_scale(mid_full.astype(jnp.float32), 1e-06) * feedforward_norm_gain).astype(
         jnp.bfloat16
     )
-    both_acts = jnp.dot(ffn_in, late[:, : 2 * units], preferred_element_type=jnp.float32)
-    hidden_units = (jax.nn.silu(both_acts[:, :units]) * both_acts[:, units:]).astype(jnp.bfloat16)
+    acts = jnp.dot(ffn_in, late[:, : 4 * units], preferred_element_type=jnp.float32)
+    hidden_units = jnp.concatenate(
+        [
+            jax.nn.silu(acts[:, i * units : (i + 1) * units])
+            * acts[:, (i + 1) * units : (i + 2) * units]
+            for i in (0, 2)
+        ],
+        axis=1,
+    ).astype(jnp.bfloat16)
     piece = lax.dot_general(
         hidden_units,
-        late[:, 2 * units + own_width // 2 :],
+        late[:, 4 * units + own_width // 2 :],
         (((1,), (1,)), ((), ())),
         preferred_element_type=jnp.float32,
     ).astype(jnp.bfloat16)
-    piece = piece.reshape(tokens, groups, own_width).transpose(1, 0, 2)
-    return (own_mid + jnp.sum(exchange(piece, "head").astype(jnp.float32), axis=0)).astype(
-        jnp.bfloat16
-    )
+    piece = piece.reshape(part, groups, own_width).transpose(1, 0, 2)
+    pieces = exchange(piece, "head").reshape(groups // 2, tokens, own_width)
+    return (own_mid + jnp.sum(pieces.astype(jnp.float32), axis=0)).astype(jnp.bfloat16)
 
 
 def solution(mesh):

time: 193 us -> 190 us (0.984)
  blocking collectives: 109 us -> 91.5 us
  matrix products: 9.57 us -> 17 us
  starting transfers between devices: 13.1 us -> 18 us
  waiting for transfers between devices: 28.4 us -> 30.8 us
    all_to_all x4, blocking collectives: 109 us -> 91.5 us  [exchange(): return lax.all_to_all(blocks, axis, split_axis=0, concat_axis=0, tiled=True)]
    dot_general x2, matrix products: 2.62 us -> 10.1 us  [the longest x1 5.51 us: per_device(): jnp.dot(ffn_in, late[:, :4 * units], preferred_element_type=jnp.float32)]
    ppermute x0 -> x1, starting transfers between devices: none -> 4.03 us  [per_device(): lax.ppermute(acts_local, 'head', [(i, i ^ 1) for i in range(groups)])]
    ppermute x0 -> x1, waiting for transfers between devices: none -> 2.37 us  [per_device(): lax.ppermute(acts_local, 'head', [(i, i ^ 1) for i in range(groups)])]
  transfers between devices with their start and end apart: 3 -> 4, of which waited for: 2 -> 3; matrix products, arithmetic and copies ran while one was open for 8% -> 8% of each run, Pallas kernels for 0% -> 0%
where the time goes in v2:
time: 190 us; the launch traced here: 189 us
  blocking collectives  91.5 us (48%)
  waiting for transfers between devices  30.8 us (16%)
  starting transfers between devices  18 us (9%)
  matrix products  17 us (9%)
  between operations  14.4 us (8%)
  other arithmetic  8.75 us (5%)
  local copies, waits for them, and re-layouts  8.2 us (4%)
    all_to_all x4, blocking collectives, exchange(): return lax.all_to_all(blocks, axis, split_axis=0, concat_axis=0, tiled=True)  91.5 us
    all_to_all x1, waiting for transfers between devices, exchange(): return lax.all_to_all(blocks, axis, split_axis=0, concat_axis=0, tiled=True)  25 us
    ppermute x1, starting transfers between devices, sibling(): return lax.ppermute(block, 'core', [(0, 1), (1, 0)])  7.27 us
    all_to_all x1, starting transfers between devices, exchange(): return lax.all_to_all(blocks, axis, split_axis=0, concat_axis=0, tiled=True)  6.74 us
    dot_general x1, matrix products, per_device(): jnp.dot(ffn_in, late[:, :4 * units], preferred_element_type=jnp.float32)  5.51 us
    dot_general x1, matrix products, per_device(): lax.dot_general(hidden_units, late[:, 4 * units + own_width // 2:], (((1,...  4.54 us
    ppermute x1, starting transfers between devices, per_device(): lax.ppermute(acts_local, 'head', [(i, i ^ 1) for i in range(groups)])  4.03 us
  transfers between devices with their start and end apart: 4, of which 3 were waited for; matrix products, arithmetic and copies ran while one was open for 8% of the time, Pallas kernels for 0%

profile of v2, /device:TPU:1, one launch (start us, length us, event | category | flops | bytes accessed | tf_op | source)
XLA Modules:
  0.0 188.7 jit_solution(10127732111160247094)
XLA Ops:
  6.5 1.0 concatenate.35
  7.5 4.0 %collective-permute-start.1 = (bf16[32,2112]{1,0:T(8,128)(2,1)S(1)}, bf16[32,2112]{1,0:T(8,128)(2,1)S(1)}, u32[]{:S(2)}, u32[]{:S(2)}) collective-permute-start(bf16[32,2112]{1,0:T(8,128)(2,1)S(1)} %concatenate.35), channel_id=1, source_target_pairs={{0,64},{64,0},{128,192},{192,128},{256,320},{320,256},{384,448},{4... | collective-permute-start | bytes 405512 | tf_op jit(solution)/shard_map/ppermute | solution.py:106
  11.6 2.4 %collective-permute-done.1 = bf16[32,2112]{1,0:T(8,128)(2,1)S(1)} collective-permute-done((bf16[32,2112]{1,0:T(8,128)(2,1)S(1)}, bf16[32,2112]{1,0:T(8,128)(2,1)S(1)}, u32[]{:S(2)}, u32[]{:S(2)}) %collective-permute-start.1) | collective-permute-done | bytes 135200 | tf_op jit(solution)/shard_map/ppermute | solution.py:106
  14.0 1.7 concatenate.37
  15.7 0.7 fusion.65
  16.5 0.8 maximum_maximum_fusion
  17.3 26.5 %all_to_all.25 = bf16[8,32,1152]{2,1,0:T(8,128)(2,1)S(1)} all-to-all(bf16[8,32,1152]{2,1,0:T(8,128)(2,1)S(1)} %broadcast_in_dim.41), channel_id=1, replica_groups=mesh['head'=8,'z'=8,'x'=4,'core'=2] {'z'}, dimensions={0} | all-to-all | bytes 1179648 | tf_op jit(solution)/shard_map/all_to_all | solution.py:56
  43.8 0.2 broadcast_in_dim.42
  44.0 30.0 %all_to_all.26 = bf16[4,8,32,1152]{3,2,1,0:T(8,128)(2,1)S(1)} all-to-all(bf16[4,8,32,1152]{3,2,1,0:T(8,128)(2,1)S(1)} %broadcast_in_dim.42), channel_id=1, replica_groups=mesh['head'=8,'z'=8,'x'=4,'core'=2] {'x'}, dimensions={0} | all-to-all | bytes 4718592 | tf_op jit(solution)/shard_map/all_to_all | solution.py:56
  74.1 1.7 copy.26
  75.7 7.3 %collective-permute-start = (bf16[4,8,32,1152]{3,2,0,1:T(8,128)(2,1)}, bf16[4,8,32,1152]{3,2,0,1:T(8,128)(2,1)}, u32[]{:S(2)}, u32[]{:S(2)}) collective-permute-start(bf16[4,8,32,1152]{3,2,0,1:T(8,128)(2,1)} %copy.26), channel_id=1, source_target_pairs={{0,1},{1,0},{2,3},{3,2},{4,5},{5,4},{6,7},{7,6},{8,9},{9,8},{10,11... | collective-permute-start | bytes 7077896 | tf_op jit(solution)/shard_map/ppermute | solution.py:64
  83.7 0.1 select_reduce_fusion
  83.8 0.1 convert_reduce_fusion.2
  83.9 0.2 multiply_reduce_fusion
  84.1 3.4 %collective-permute-done = bf16[4,8,32,1152]{3,2,0,1:T(8,128)(2,1)} collective-permute-done((bf16[4,8,32,1152]{3,2,0,1:T(8,128)(2,1)}, bf16[4,8,32,1152]{3,2,0,1:T(8,128)(2,1)}, u32[]{:S(2)}, u32[]{:S(2)}) %collective-permute-start) | collective-permute-done | bytes 2359328 | tf_op jit(solution)/shard_map/ppermute | solution.py:64
  87.5 2.1 %select_bitcast_fusion.1 = (bf16[4,8,1,32,1152]{4,3,2,0,1:T(8,128)(2,1)S(1)}, bf16[4,8,1,32,1152]{4,3,2,0,1:T(8,128)(2,1)S(1)}) fusion(bf16[4,8,32,1152]{3,2,0,1:T(8,128)(2,1)} %collective-permute-done, pred[]{:T(512)S(6)} %eq.55, bf16[4,8,32,1152]{3,2,1,0:T(8,128)(2,1)S(1)} %all_to_all.26), kind=kLoop, calls=%fused_computation.7 | loop fusion | flops 2359296 | bytes 9437185 | tf_op jit(solution)/shard_map/stack | solution.py:128
  89.6 0.5 pad_maximum_fusion
  90.2 0.2 copy-done.4
  90.3 0.6 fusion.7
  91.0 1.3 copy-done.1
  92.3 0.4 fusion.66
  92.6 0.4 fusion.67
  93.0 0.1 fusion.28
  93.1 2.0 %multiply_reduce_fusion.1 = (f32[192]{0:T(256)S(1)}, f32[192,256]{1,0:T(8,128)S(1)}) fusion(bf16[2048,1152]{1,0:T(8,128)(2,1)} %bitcast.58, f32[2048]{0:T(1024)S(1)} %copy-done.4, f32[192]{0:T(256)S(1)} %add_rsqrt_fusion.1, bf16[192,2048]{1,0:T(8,128)(2,1)S(1)} %copy-done.2, f32[192,192]{0,1:T(8,128)S(1)} %get-tuple-element.24, ...), kind=kOutput, calls=%fused_computation.49 | convolution fusion | flops 222363456 | bytes 2441472 | tf_op jit(solution)/shard_map/dot_general | solution.py:51
  95.1 0.1 multiply_convert_fusion.6
  95.2 1.8 convolution_convert_fusion
  97.2 0.3 fusion.43
  97.5 0.3 fusion.9
  97.7 0.5 reduce-precision_convert_fusion
  98.3 1.0 pad_maximum_fusion.1
  99.3 6.7 %all-to-all-start.2 = ((bf16[8,224,256]{2,1,0:T(8,128)(2,1)}), bf16[8,224,256]{2,1,0:T(8,128)(2,1)S(1)}, u32[]{:S(2)}, u32[]{:S(2)}) async-start(bf16[8,224,256]{2,1,0:T(8,128)(2,1)} %pad_maximum_fusion.1), calls=%async_computation.2 | async-start | bytes 1835008 | tf_op jit(solution)/shard_map/all_to_all | solution.py:56
  106.0 1.4 convert_element_type.73
  107.4 25.0 %all-to-all-done.2 = bf16[8,224,256]{2,1,0:T(8,128)(2,1)S(1)} async-done(((bf16[8,224,256]{2,1,0:T(8,128)(2,1)}), bf16[8,224,256]{2,1,0:T(8,128)(2,1)S(1)}, u32[]{:S(2)}, u32[]{:S(2)}) %all-to-all-start.2) | async-done | bytes 917536 | tf_op jit(solution)/shard_map/all_to_all | solution.py:56
  132.4 0.1 convert_reduce_fusion
  132.5 0.3 fusion.10
  132.8 1.1 slice.143
  134.0 0.3 fusion.70
  134.2 0.3 fusion.71
  134.5 1.0 fusion.60
  135.5 19.5 %all_to_all.27 = bf16[8,96,256]{2,1,0:T(8,128)(2,1)S(1)} all-to-all(bf16[8,96,256]{2,1,0:T(8,128)(2,1)S(1)} %bitcast.66), channel_id=1, replica_groups=mesh['head'=8,'z'=8,'x'=4,'core'=2] {'head'}, dimensions={0} | all-to-all | bytes 786432 | tf_op jit(solution)/shard_map/all_to_all | solution.py:56
  155.0 0.1 convert_bitcast_fusion
  155.1 0.1 copy.34
  155.1 0.2 fusion.17
  155.3 5.5 %fusion = f32[96,2816]{1,0:T(8,128)S(1)} fusion(bf16[2048,4352]{1,0:T(8,128)(2,1)} %all-gather.2.cloned.1.call-done, f32[96,2048]{1,0:T(8,128)S(1)} %bitcast.71, f32[2048]{0:T(1024)S(1)} %copy-done.5, f32[96]{0:T(128)S(1)} %add_rsqrt_fusion.2), kind=kOutput, calls=%fused_computation | convolution fusion | flops 1107886080 | bytes 13410688 | tf_op jit(solution)/shard_map/dot_general | solution.py:203
  160.8 0.2 fusion.21
  161.1 4.5 %fusion.4 = bf16[96,2048]{1,0:T(8,128)(2,1)S(1)} fusion(bf16[2048,4352]{1,0:T(8,128)(2,1)} %all-gather.2.cloned.1.call-done, bf16[96,704]{1,0:T(8,128)(2,1)S(1)} %get-tuple-element.12, bf16[96,704]{1,0:T(8,128)(2,1)S(1)} %get-tuple-element.11), kind=kOutput, calls=%fused_computation.8 | convolution fusion | flops 554385408 | bytes 6430720 | tf_op jit(solution)/shard_map/dot_general | solution.py:212
  165.7 15.5 %all_to_all.28 = bf16[8,96,256]{2,1,0:T(8,128)(2,1)S(1)} all-to-all(bf16[8,96,256]{2,1,0:T(8,128)(2,1)S(1)} %bitcast.64), channel_id=1, replica_groups=mesh['head'=8,'z'=8,'x'=4,'core'=2] {'head'}, dimensions={0} | all-to-all | bytes 786432 | tf_op jit(solution)/shard_map/all_to_all | solution.py:56
  181.2 0.7 add_convert_fusion
  (34 shorter events, 0.5 us)
Async XLA Ops:
  6.5 5.0 %copy-start = (bf16[1,16,2048]{2,1,0:T(8,128)(2,1)S(1)}, bf16[1,16,2048]{2,1,0:T(8,128)(2,1)}, u32[]{:S(2)}) copy-start(bf16[1,16,2048]{2,1,0:T(8,128)(2,1)} %param.23) | copy-start | bytes 196612
  6.5 126.3 %all-gather.2.cloned.1.call-start = ((), (), s32[]{:S(2)}) async-start(), calls=%async_computation.5 | async-start | bytes 18104320 | tf_op jit(solution)/shard_map/all_gather | solution.py:107
  7.5 6.5 %collective-permute-start.1 = (bf16[32,2112]{1,0:T(8,128)(2,1)S(1)}, bf16[32,2112]{1,0:T(8,128)(2,1)S(1)}, u32[]{:S(2)}, u32[]{:S(2)}) collective-permute-start(bf16[32,2112]{1,0:T(8,128)(2,1)S(1)} %concatenate.35), channel_id=1, source_target_pairs={{0,64},{64,0},{128,192},{192,128},{256,320},{320,256},{384,448},{4... | collective-permute-start | bytes 405512 | tf_op jit(solution)/shard_map/ppermute | solution.py:106
  74.1 9.6 %copy-start.6 = (s32[1,6]{1,0:T(1,128)S(1)}, s32[1,6]{1,0:T(1,128)}, u32[]{:S(2)}) copy-start(s32[1,6]{1,0:T(1,128)} %param.15) | copy-start | bytes 76
  74.1 9.8 %copy-start.2 = (bf16[192,2048]{1,0:T(8,128)(2,1)S(1)}, bf16[192,2048]{1,0:T(8,128)(2,1)}, u32[]{:S(2)}) copy-start(bf16[192,2048]{1,0:T(8,128)(2,1)} %param.14) | copy-start | bytes 2359300
  75.7 11.8 %collective-permute-start = (bf16[4,8,32,1152]{3,2,0,1:T(8,128)(2,1)}, bf16[4,8,32,1152]{3,2,0,1:T(8,128)(2,1)}, u32[]{:S(2)}, u32[]{:S(2)}) collective-permute-start(bf16[4,8,32,1152]{3,2,0,1:T(8,128)(2,1)} %copy.26), channel_id=1, source_target_pairs={{0,1},{1,0},{2,3},{3,2},{4,5},{5,4},{6,7},{7,6},{8,9},{9,8},{10,11... | collective-permute-start | bytes 7077896 | tf_op jit(solution)/shard_map/ppermute | solution.py:64
  89.6 0.7 copy-start.4
  90.1 2.2 %copy-start.1 = (bf16[4,8,2,32,1152]{4,3,2,0,1:T(8,128)(2,1)}, bf16[4,8,2,32,1152]{4,3,2,0,1:T(8,128)(2,1)S(1)}, u32[]{:S(2)}) copy-start(bf16[4,8,2,32,1152]{4,3,2,0,1:T(8,128)(2,1)S(1)} %pad_maximum_fusion) | copy-start | bytes 14155780
  95.2 2.2 %copy-start.3 = (s32[192,1]{0,1:T(1,128)S(1)}, s32[192,1]{0,1:T(1,128)}, u32[]{:S(2)}) copy-start(s32[192,1]{0,1:T(1,128)} %param.16) | copy-start | bytes 2308
  99.3 33.1 %all-to-all-start.2 = ((bf16[8,224,256]{2,1,0:T(8,128)(2,1)}), bf16[8,224,256]{2,1,0:T(8,128)(2,1)S(1)}, u32[]{:S(2)}, u32[]{:S(2)}) async-start(bf16[8,224,256]{2,1,0:T(8,128)(2,1)} %pad_maximum_fusion.1), calls=%async_computation.2 | async-start | bytes 1835008 | tf_op jit(solution)/shard_map/all_to_all | solution.py:56
  135.5 19.8 %copy-start.5 = (f32[2048]{0:T(1024)S(1)}, f32[2048]{0:T(1024)}, u32[]{:S(2)}) copy-start(f32[2048]{0:T(1024)} %param.24) | copy-start | bytes 24580
Sparse Core Ops, SparseCore 0:
  15.9 115.9 all-gather.1

commit v3 on v1

v3 whole, which is shorter than its diff:
```python
import jax
import jax.numpy as jnp
from jax import lax
from jax.experimental import pallas as pl
from jax.experimental.pallas import tpu as pltpu
from jax.sharding import Mesh
from jax.sharding import PartitionSpec as P

HD = 128
RANK = 16

adapter_scaling = 2.0
head_shrink = 0.8
neg_large = -1e30

BLK = ("z", "x", "core")


def rms_scale(values, epsilon):
    return values * lax.rsqrt(jnp.mean(values * values, axis=-1, keepdims=True) + epsilon)


def nt_dot(left, right, precision=None):
    return lax.dot_general(
        left,
        right,
        (((1,), (1,)), ((), ())),
        precision=precision,
        preferred_element_type=jnp.float32,
    )


def masked_softmax(scores, allowed):
    scores = jnp.where(allowed, scores, neg_large)
    row_peak = jnp.max(scores, axis=-1, keepdims=True)
    raised = jnp.where(allowed, jnp.exp(scores - row_peak), 0.0)
    return raised / jnp.sum(raised, axis=-1, keepdims=True)


def attention_kernel(
    lengths_ref, lambda_ref, core_ref, residual_ref, gain_ref, chosen_ref, mine_ref, other_ref, sent_ref
):
    slabs_x, slabs_z, rows, width = mine_ref.shape
    tokens = residual_ref.shape[0]
    value_width = 2 * HD
    qkv_width = 4 * HD + value_width
    out_end = qkv_width + value_width
    adapters = 2 * slabs_x * slabs_z

    def body(even_ref, odd_ref):
        def gather(z, begin, end, first_row=0, last_row=rows):
            return jnp.concatenate(
                [
                    ref[x, z, first_row:last_row, begin:end]
                    for x in range(slabs_x)
                    for ref in (even_ref, odd_ref)
                ],
                axis=0,
            )

        slab = 2 * slabs_x * rows
        normed = (rms_scale(residual_ref[...].astype(jnp.float32), 1e-06) * gain_ref[...]).astype(
            jnp.bfloat16
        )
        qkv = jnp.zeros((tokens, qkv_width), jnp.float32)
        for z in range(slabs_z):
            qkv = qkv + jnp.dot(
                normed[:, z * slab : (z + 1) * slab],
                gather(z, 0, qkv_width),
                preferred_element_type=jnp.float32,
            )
        row_at = lax.broadcasted_iota(jnp.int32, (tokens, tokens), 0)
        column_at = lax.broadcasted_iota(jnp.int32, (tokens, tokens), 1)
        row_request = jnp.zeros((tokens, tokens), jnp.int32)
        column_request = jnp.zeros((tokens, tokens), jnp.int32)
        end = jnp.int32(0)
        for i in range(lengths_ref.shape[1]):
            end = end + lengths_ref[0, i]
            row_request = row_request + jnp.where(row_at >= end, 1, 0)
            column_request = column_request + jnp.where(column_at >= end, 1, 0)
        allowed = (row_request == column_request) & (column_at <= row_at)
        parts = [qkv[:, i * HD : (i + 1) * HD] for i in range(4)]
        scale = 1.0 / HD**0.5
        probs = [
            masked_softmax(nt_dot(parts[i], parts[i + 2], lax.Precision.HIGHEST) * scale, allowed)
            for i in range(2)
        ]
        mixed = (probs[0] - lambda_ref[0] * probs[1]).astype(jnp.bfloat16)
        attended = jnp.dot(
            mixed, qkv[:, 4 * HD :].astype(jnp.bfloat16), preferred_element_type=jnp.float32
        )
        head_out = (rms_scale(attended, 1e-05) * head_shrink).astype(jnp.bfloat16)

        coordinates = jnp.zeros((tokens, adapters * RANK), jnp.float32)
        for half in range(2):
            maps = jnp.concatenate(
                [
                    gather(z, out_end, width, half * RANK, (half + 1) * RANK)
                    for z in range(slabs_z)
                ],
                axis=0,
            )
            coordinates = coordinates + nt_dot(head_out[:, half * HD : (half + 1) * HD], maps)
        owner = lax.broadcasted_iota(jnp.int32, coordinates.shape, 1) // RANK
        kept = jnp.where(owner == chosen_ref[...], coordinates, 0.0)
        room = jnp.zeros((value_width - tokens, adapters * RANK), jnp.float32)
        kept = jnp.concatenate([kept, room], axis=0)
        high = kept.astype(jnp.bfloat16)
        low = (kept - high.astype(jnp.float32)).astype(jnp.bfloat16)
        lift_shape = (RANK, adapters * RANK)
        lift = jnp.where(
            lax.broadcasted_iota(jnp.int32, lift_shape, 1) % RANK
            == lax.broadcasted_iota(jnp.int32, lift_shape, 0),
            1.0,
            0.0,
        ).astype(jnp.bfloat16)
        low_rows = jnp.concatenate([nt_dot(lift, high), nt_dot(lift, low)], axis=0).astype(
            jnp.bfloat16
        )
        for z in range(slabs_z):
            sent_ref[z, :tokens, :] = nt_dot(head_out, gather(z, qkv_width, out_end)).astype(
                jnp.bfloat16
            )
            sent_ref[z, tokens:, :] = low_rows

    @pl.when(core_ref[0] == 0)
    def _():
        body(mine_ref, other_ref)

    @pl.when(core_ref[0] != 0)
    def _():
        body(other_ref, mine_ref)


def attention(lengths, second_weight, core, residual, gain, chosen, mine, other):
    tokens = residual.shape[0]
    groups = mine.shape[1]
    smem = pl.BlockSpec(memory_space=pltpu.SMEM)
    vmem = pl.BlockSpec(memory_space=pltpu.VMEM)
    return pl.pallas_call(
        attention_kernel,
        out_shape=jax.ShapeDtypeStruct((groups, tokens + 2 * RANK, 2 * HD), jnp.bfloat16),
        in_specs=[smem] * 3 + [vmem] * 5,
        out_specs=vmem,
        compiler_params=pltpu.CompilerParams(vmem_limit_bytes=48 * 1024 * 1024),
        cost_estimate=pl.CostEstimate(
            flops=1_200_000_000, bytes_accessed=8_000_000, transcendentals=80_000
        ),
    )(lengths, second_weight, core, residual, gain.reshape(1, -1), chosen, mine, other)


def exchange(blocks, axis):
    return lax.all_to_all(blocks, axis, split_axis=0, concat_axis=0, tiled=True)


def spread(block, axis):
    return exchange(jnp.broadcast_to(block[None], (lax.axis_size(axis), *block.shape)), axis)


def sibling(block):
    return lax.ppermute(block, "core", [(0, 1), (1, 0)])


def fold_map(rank_rows):
    half = rank_rows.shape[1] // 2
    return jnp.concatenate([rank_rows[:, :half], rank_rows[:, half:]], axis=0)


def unfold_map(folded, owners):
    stacked = folded.reshape(owners, 2, RANK, folded.shape[1])
    return [stacked[:, i].reshape(owners * RANK, folded.shape[1]) for i in range(2)]


def per_device(
    residual,
    lengths,
    token_adapter_index,
    attention_norm_gain,
    query_key_weight,
    value_weight,
    head_second_weight,
    output_weight,
    adapter_down_maps,
    adapter_up_maps,
    feedforward_norm_gain,
    gate_weight,
    up_weight,
    down_weight,
):
    tokens, width = residual.shape
    groups = lax.axis_size("head")
    owners = lax.axis_size(BLK)
    own_width = width // groups
    own_begin = lax.axis_index("head") * own_width
    units = gate_weight.shape[1]

    down_map = fold_map(adapter_down_maps[0].T)
    up_map = fold_map(lax.dynamic_slice_in_dim(adapter_up_maps[0], own_begin, own_width, 1))

    early = jnp.concatenate([query_key_weight, value_weight, output_weight, down_map], axis=1)
    columns = spread(early, "z")
    late_rows = jnp.concatenate([gate_weight, up_weight, up_map, down_weight], axis=1)
    columns, late_rows = lax.optimization_barrier((columns, late_rows))
    late = lax.all_gather(late_rows, BLK, axis=0, tiled=True)
    mine = spread(columns, "x")
    other = sibling(mine)
    core = lax.axis_index("core").astype(jnp.int32).reshape(1)
    sent = attention(
        lengths,
        head_second_weight,
        core,
        residual,
        attention_norm_gain,
        token_adapter_index,
        mine,
        other,
    )

    inputs = residual.astype(jnp.float32)
    coordinate = jnp.arange(owners * RANK, dtype=jnp.int32)
    chosen = coordinate[None, :] // RANK == token_adapter_index
    lift = (jnp.arange(RANK, dtype=jnp.int32)[:, None] == coordinate[None, :] % RANK)
    total = jnp.sum(exchange(sent, "head").astype(jnp.float32), axis=0)
    low_rank = (total[tokens : tokens + RANK, :tokens] + total[tokens + RANK :, :tokens]).astype(
        jnp.bfloat16
    )
    lifted = lax.dot_general(
        low_rank,
        lift.astype(jnp.bfloat16),
        (((0,), (0,)), ((), ())),
        preferred_element_type=jnp.float32,
    )
    routed = jnp.where(chosen, lifted, 0.0).astype(jnp.bfloat16)
    up_maps = unfold_map(late[:, 2 * units : 2 * units + own_width // 2], owners)
    delta_own = (
        adapter_scaling
        * jnp.concatenate(
            [jnp.dot(routed, part, preferred_element_type=jnp.float32) for part in up_maps], axis=1
        )
    ).astype(jnp.bfloat16)
    own_mid = (
        lax.dynamic_slice_in_dim(inputs, own_begin, own_width, 1)
        + total[:tokens]
        + delta_own.astype(jnp.float32)
    )
    mid_full = spread(own_mid.astype(jnp.bfloat16), "head").transpose(1, 0, 2).reshape(tokens, width)
    ffn_in = (rms_scale(mid_full.astype(jnp.float32), 1e-06) * feedforward_norm_gain).astype(
        jnp.bfloat16
    )
    both_acts = jnp.dot(ffn_in, late[:, : 2 * units], preferred_element_type=jnp.float32)
    hidden_units = (jax.nn.silu(both_acts[:, :units]) * both_acts[:, units:]).astype(jnp.bfloat16)
    piece = lax.dot_general(
        hidden_units,
        late[:, 2 * units + own_width // 2 :],
        (((1,), (1,)), ((), ())),
        preferred_element_type=jnp.float32,
    ).astype(jnp.bfloat16)
    piece = piece.reshape(tokens, groups, own_width).transpose(1, 0, 2)
    return (own_mid + jnp.sum(exchange(piece, "head").astype(jnp.float32), axis=0)).astype(
        jnp.bfloat16
    )


def solution(mesh):
    fine = Mesh(mesh.devices.reshape(mesh.devices.shape[0], 8, 4, 2), ("head", *BLK))
    return jax.shard_map(
        per_device,
        mesh=fine,
        in_specs=(
            P(BLK, None),
            P(BLK, None),
            P(BLK, None),
            P(),
            P(BLK, "head"),
            P(BLK, "head"),
            P("head"),
            P(BLK, "head"),
            P(BLK, "head", None),
            P(BLK, None, None),
            P(),
            P(BLK, "head"),
            P(BLK, "head"),
            P(BLK, "head"),
        ),
        out_specs=P(BLK, "head"),
        check_vma=False,
    )
```

time: 193 us -> 194 us (level)
  waiting for transfers between devices: 28.4 us -> 53.9 us
  blocking collectives: 109 us -> 88.5 us
  starting transfers between devices: 13.1 us -> 21.5 us
  other arithmetic: 8.94 us -> 2.17 us
  matrix products: 9.57 us -> 3.42 us
  Pallas kernels: 0 us -> 5.8 us
  local copies, waits for them, and re-layouts: 8.7 us -> 4.37 us
    all_to_all x4 -> x3, blocking collectives: 109 us -> 88.5 us  [exchange(): return lax.all_to_all(blocks, axis, split_axis=0, concat_axis=0, tiled=True)]
    all_to_all x1 -> x2, waiting for transfers between devices: 25 us -> 44.8 us  [exchange(): return lax.all_to_all(blocks, axis, split_axis=0, concat_axis=0, tiled=True)]
    all_to_all x1 -> x2, starting transfers between devices: 7.28 us -> 17.7 us  [exchange(): return lax.all_to_all(blocks, axis, split_axis=0, concat_axis=0, tiled=True)]
    dot_general x8 -> x0, matrix products: 6.16 us -> none  [the longest x1 1.96 us: diff_head(): attended = jnp.dot(mixed, value_head, preferred_element_type=jnp.float32)]
    pallas_call x0 -> x1, Pallas kernels: none -> 5.8 us  [attention(): pl.pallas_call(attention_kernel, out_shape=jax.ShapeDtypeStruct((groups,...]
    all_gather x1, waiting for transfers between devices: 0.02 us -> 5.57 us  [per_device(): late = lax.all_gather(late_rows, BLK, axis=0, tiled=True)]
    another operation x2 -> x0, other arithmetic: 2.68 us -> none  [per_device(): jnp.stack([jnp.where(first, mine, other), jnp.where(first, other, mine)],...]
    unnamed x16 -> x21, local copies, waits for them, and re-layouts: 2.95 us -> 0.43 us
  transfers between devices with their start and end apart: 3 -> 4, of which waited for: 2 -> 4; matrix products, arithmetic and copies ran while one was open for 8% -> 1% of each run, Pallas kernels for 0% -> 3%
where the time goes in v3:
time: 194 us
  blocking collectives  88.5 us (46%)
  waiting for transfers between devices  53.9 us (28%)
  starting transfers between devices  21.5 us (11%)
  between operations  14.3 us (7%)
  Pallas kernels  5.8 us (3%)
  local copies, waits for them, and re-layouts  4.37 us (2%)
  matrix products  3.42 us (2%)
  other arithmetic  2.17 us (1%)
    all_to_all x3, blocking collectives, exchange(): return lax.all_to_all(blocks, axis, split_axis=0, concat_axis=0, tiled=True)  88.5 us
    all_to_all x2, waiting for transfers between devices, exchange(): return lax.all_to_all(blocks, axis, split_axis=0, concat_axis=0, tiled=True)  44.8 us
    all_to_all x2, starting transfers between devices, exchange(): return lax.all_to_all(blocks, axis, split_axis=0, concat_axis=0, tiled=True)  17.7 us
    pallas_call x1, Pallas kernels, attention(): pl.pallas_call(attention_kernel, out_shape=jax.ShapeDtypeStruct((groups,...  5.8 us
    all_gather x1, waiting for transfers between devices, per_device(): late = lax.all_gather(late_rows, BLK, axis=0, tiled=True)  5.57 us
  transfers between devices with their start and end apart: 4, of which 4 were waited for; matrix products, arithmetic and copies ran while one was open for 1% of the time, Pallas kernels for 3%

profile of v3, /device:TPU:1, one launch (start us, length us, event | category | flops | bytes accessed | tf_op | source)
XLA Modules:
  0.0 193.9 jit_solution(2682758049774777981)
XLA Ops:
  6.5 0.0 copy-start
  6.5 0.7 fusion.30
  7.3 0.8 maximum_maximum_fusion
  8.1 0.9 broadcast_in_dim.9
  8.9 10.9 %all-to-all-start = ((bf16[8,32,1152]{2,1,0:T(8,128)(2,1)}), bf16[8,32,1152]{2,1,0:T(8,128)(2,1)S(1)}, u32[]{:S(2)}, u32[]{:S(2)}) async-start(bf16[8,32,1152]{2,1,0:T(8,128)(2,1)} %broadcast_in_dim.9), calls=%async_computation | async-start | bytes 1179648 | tf_op jit(solution)/shard_map/all_to_all | solution.py:153
  19.8 0.0 all-gather.2.cloned.1.call-start
  19.9 0.0 copy-done
  19.9 0.0 copy-done.4
  19.9 0.0 copy-done.5
  19.9 0.0 copy-done.6
  19.9 0.8 concatenate.18
  20.7 18.5 %all-to-all-done = bf16[8,32,1152]{2,1,0:T(8,128)(2,1)S(1)} async-done(((bf16[8,32,1152]{2,1,0:T(8,128)(2,1)}), bf16[8,32,1152]{2,1,0:T(8,128)(2,1)S(1)}, u32[]{:S(2)}, u32[]{:S(2)}) %all-to-all-start) | async-done | bytes 589856 | tf_op jit(solution)/shard_map/all_to_all | solution.py:153
  39.2 0.0 all-gather.2.cloned.1.call-update
  39.2 0.2 broadcast_in_dim.10
  39.4 0.0 copy-start.8
  39.4 0.0 copy-start.1
  39.4 0.0 copy-start.2
  39.4 0.0 copy-start.3
  39.4 34.6 %all_to_all.25.mine_ref = bf16[4,8,32,1152]{3,2,1,0:T(8,128)(2,1)S(1)} all-to-all(bf16[4,8,32,1152]{3,2,1,0:T(8,128)(2,1)S(1)} %broadcast_in_dim.10), channel_id=1, replica_groups=mesh['head'=8,'z'=8,'x'=4,'core'=2] {'x'}, dimensions={0} | all-to-all | bytes 4718592 | tf_op jit(solution)/shard_map/all_to_all | solution.py:153
  74.0 3.8 %collective-permute-start = (bf16[4,8,32,1152]{3,2,1,0:T(8,128)(2,1)S(1)}, bf16[4,8,32,1152]{3,2,1,0:T(8,128)(2,1)}, u32[]{:S(2)}, u32[]{:S(2)}) collective-permute-start(bf16[4,8,32,1152]{3,2,1,0:T(8,128)(2,1)S(1)} %all_to_all.25.mine_ref), channel_id=1, source_target_pairs={{0,1},{1,0},{2,3},{3,2},{4,5},{5,4},{6,7},{7,6},{8,9},{9,8},{10,11... | collective-permute-start | bytes 7077896 | tf_op jit(solution)/shard_map/ppermute | solution.py:161
  77.8 0.0 copy-done.8
  77.8 0.1 copy.17.chosen_ref
  78.6 3.5 %collective-permute-done.other_ref = bf16[4,8,32,1152]{3,2,1,0:T(8,128)(2,1)} collective-permute-done((bf16[4,8,32,1152]{3,2,1,0:T(8,128)(2,1)S(1)}, bf16[4,8,32,1152]{3,2,1,0:T(8,128)(2,1)}, u32[]{:S(2)}, u32[]{:S(2)}) %collective-permute-start) | collective-permute-done | bytes 2359328 | tf_op jit(solution)/shard_map/ppermute | solution.py:161
  82.1 0.0 copy-done.1
  82.1 0.0 copy-done.2
  82.1 5.8 %shard_map.136 = bf16[8,224,256]{2,1,0:T(8,128)(2,1)} custom-call(s32[1,6]{1,0:T(1,128)S(1)} %copy-done.3, f32[1]{0:T(128)S(6)} %copy.24.lambda_ref, s32[1]{0:T(128)} %bitcast.core_ref, bf16[192,2048]{1,0:T(8,128)(2,1)S(1)} %copy-done.1, f32[1,2048]{1,0:T(1,128)S(1)} %bitcast.26, s32[192,1]{1,0:T(8,128)S(1)} %copy.17.chosen_ref, ...), custom_call_target="tpu_custom_call" | custom-call | flops 1200000000 | bytes 8000000 | tf_op jit(solution)/shard_map/pallas_call | solution.py:140
  87.9 6.8 %all-to-all-start.2 = ((bf16[8,224,256]{2,1,0:T(8,128)(2,1)}), bf16[8,224,256]{2,1,0:T(8,128)(2,1)S(1)}, u32[]{:S(2)}, u32[]{:S(2)}) async-start(bf16[8,224,256]{2,1,0:T(8,128)(2,1)} %shard_map.136), calls=%async_computation.2 | async-start | bytes 1835008 | tf_op jit(solution)/shard_map/all_to_all | solution.py:153
  94.7 26.4 %all-to-all-done.2 = bf16[8,224,256]{2,1,0:T(8,128)(2,1)S(1)} async-done(((bf16[8,224,256]{2,1,0:T(8,128)(2,1)}), bf16[8,224,256]{2,1,0:T(8,128)(2,1)S(1)}, u32[]{:S(2)}, u32[]{:S(2)}) %all-to-all-start.2) | async-done | bytes 917536 | tf_op jit(solution)/shard_map/all_to_all | solution.py:153
  121.0 0.1 convert_reduce_fusion
  121.2 0.3 fusion.8
  121.5 5.6 %all-gather.2.cloned.1.call-done = bf16[2048,2240]{1,0:T(8,128)(2,1)} async-done(((bf16[32,2240]{1,0:T(8,128)(2,1)}), bf16[2048,2240]{1,0:T(8,128)(2,1)}) %all-gather.2.cloned.1.call-update) | async-done | bytes 9175056 | tf_op jit(solution)/shard_map/all_gather | solution.py:204
  127.0 1.1 slice.63
  128.2 0.3 fusion.31
  128.4 0.3 fusion.32
  128.7 0.1 broadcast_in_dim.13
  128.8 29.7 %all_to_all.26 = bf16[8,192,256]{2,1,0:T(8,128)(2,1)S(1)} all-to-all(bf16[8,192,256]{2,1,0:T(8,128)(2,1)S(1)} %broadcast_in_dim.13), channel_id=1, replica_groups=mesh['head'=8,'z'=8,'x'=4,'core'=2] {'head'}, dimensions={0} | all-to-all | bytes 1572864 | tf_op jit(solution)/shard_map/all_to_all | solution.py:153
  158.5 0.1 convert_bitcast_fusion
  158.7 0.0 copy-start.9
  158.7 0.2 copy.21
  158.8 0.2 fusion.7
  159.1 0.0 copy-done.7
  159.1 0.3 copy-done.9
  159.4 1.4 fusion
  160.8 1.2 fusion.4
  162.0 0.1 copy.23
  162.1 24.2 %all_to_all.27 = bf16[8,192,256]{2,1,0:T(8,128)(2,1)S(1)} all-to-all(bf16[8,192,256]{2,1,0:T(8,128)(2,1)S(1)} %bitcast.27), channel_id=1, replica_groups=mesh['head'=8,'z'=8,'x'=4,'core'=2] {'head'}, dimensions={0} | all-to-all | bytes 1572864 | tf_op jit(solution)/shard_map/all_to_all | solution.py:153
  186.3 0.1 convert_reduce_fusion.1
  186.4 0.7 add_convert_fusion
  (12 shorter events, 0.1 us)
Async XLA Ops:
  6.5 13.3 %copy-start = (bf16[1,16,2048]{2,1,0:T(8,128)(2,1)S(1)}, bf16[1,16,2048]{2,1,0:T(8,128)(2,1)}, u32[]{:S(2)}) copy-start(bf16[1,16,2048]{2,1,0:T(8,128)(2,1)} %param.23) | copy-start | bytes 196612
  6.5 13.4 %copy-start.4 = (bf16[32,704]{1,0:T(8,128)(2,1)S(1)}, bf16[32,704]{1,0:T(8,128)(2,1)}, u32[]{:S(2)}) copy-start(bf16[32,704]{1,0:T(8,128)(2,1)} %param.25) | copy-start | bytes 135172
  6.5 13.4 %copy-start.5 = (bf16[32,704]{1,0:T(8,128)(2,1)S(1)}, bf16[32,704]{1,0:T(8,128)(2,1)}, u32[]{:S(2)}) copy-start(bf16[32,704]{1,0:T(8,128)(2,1)} %param.26) | copy-start | bytes 135172
  6.5 13.4 %copy-start.6 = (bf16[32,704]{1,0:T(8,128)(2,1)S(1)}, bf16[32,704]{1,0:T(8,128)(2,1)}, u32[]{:S(2)}) copy-start(bf16[32,704]{1,0:T(8,128)(2,1)} %param.27) | copy-start | bytes 135172
  8.9 30.2 %all-to-all-start = ((bf16[8,32,1152]{2,1,0:T(8,128)(2,1)}), bf16[8,32,1152]{2,1,0:T(8,128)(2,1)S(1)}, u32[]{:S(2)}, u32[]{:S(2)}) async-start(bf16[8,32,1152]{2,1,0:T(8,128)(2,1)} %broadcast_in_dim.9), calls=%async_computation | async-start | bytes 1179648 | tf_op jit(solution)/shard_map/all_to_all | solution.py:153
  19.8 107.2 %all-gather.2.cloned.1.call-start = ((), (), s32[]{:S(2)}) async-start(), calls=%async_computation.5 | async-start | bytes 9584640 | tf_op jit(solution)/shard_map/all_gather | solution.py:204
  39.4 38.4 %copy-start.8 = (s32[192,1]{0,1:T(1,128)S(1)}, s32[192,1]{0,1:T(1,128)}, u32[]{:S(2)}) copy-start(s32[192,1]{0,1:T(1,128)} %param.16) | copy-start | bytes 2308
  39.4 42.7 %copy-start.1 = (bf16[192,2048]{1,0:T(8,128)(2,1)S(1)}, bf16[192,2048]{1,0:T(8,128)(2,1)}, u32[]{:S(2)}) copy-start(bf16[192,2048]{1,0:T(8,128)(2,1)} %residual_ref.1) | copy-start | bytes 2359300
  39.4 42.6 %copy-start.2 = (f32[2048]{0:T(1024)S(1)}, f32[2048]{0:T(1024)}, u32[]{:S(2)}) copy-start(f32[2048]{0:T(1024)} %param.17) | copy-start | bytes 24580
  39.4 42.6 %copy-start.3 = (s32[1,6]{1,0:T(1,128)S(1)}, s32[1,6]{1,0:T(1,128)}, u32[]{:S(2)}) copy-start(s32[1,6]{1,0:T(1,128)} %lengths_ref.1) | copy-start | bytes 76
  74.0 8.1 %collective-permute-start = (bf16[4,8,32,1152]{3,2,1,0:T(8,128)(2,1)S(1)}, bf16[4,8,32,1152]{3,2,1,0:T(8,128)(2,1)}, u32[]{:S(2)}, u32[]{:S(2)}) collective-permute-start(bf16[4,8,32,1152]{3,2,1,0:T(8,128)(2,1)S(1)} %all_to_all.25.mine_ref), channel_id=1, source_target_pairs={{0,1},{1,0},{2,3},{3,2},{4,5},{5,4},{6,7},{7,6},{8,9},{9,8},{10,11... | collective-permute-start | bytes 7077896 | tf_op jit(solution)/shard_map/ppermute | solution.py:161
  87.9 33.2 %all-to-all-start.2 = ((bf16[8,224,256]{2,1,0:T(8,128)(2,1)}), bf16[8,224,256]{2,1,0:T(8,128)(2,1)S(1)}, u32[]{:S(2)}, u32[]{:S(2)}) async-start(bf16[8,224,256]{2,1,0:T(8,128)(2,1)} %shard_map.136), calls=%async_computation.2 | async-start | bytes 1835008 | tf_op jit(solution)/shard_map/all_to_all | solution.py:153
  128.4 30.7 %copy-start.7 = (bf16[2048,2240]{1,0:T(8,128)(2,1)S(1)}, bf16[2048,2240]{1,0:T(8,128)(2,1)}, u32[]{:S(2)}) copy-start(bf16[2048,2240]{1,0:T(8,128)(2,1)} %all-gather.2.cloned.1.call-done) | copy-start | bytes 27525124
  158.7 0.7 copy-start.9
Sparse Core Ops, SparseCore 0:
  39.3 87.6 all-gather.1

commit v4 on v3

--- a/solution.py
+++ b/solution.py
@@ -198,11 +198,9 @@
     up_map = fold_map(lax.dynamic_slice_in_dim(adapter_up_maps[0], own_begin, own_width, 1))
 
     early = jnp.concatenate([query_key_weight, value_weight, output_weight, down_map], axis=1)
-    columns = spread(early, "z")
     late_rows = jnp.concatenate([gate_weight, up_weight, up_map, down_weight], axis=1)
-    columns, late_rows = lax.optimization_barrier((columns, late_rows))
     late = lax.all_gather(late_rows, BLK, axis=0, tiled=True)
-    mine = spread(columns, "x")
+    mine = spread(spread(early, "z"), "x")
     other = sibling(mine)
     core = lax.axis_index("core").astype(jnp.int32).reshape(1)
     sent = attention(

time: 194 us -> 183 us (0.943)
  waiting for transfers between devices: 53.9 us -> 29.9 us
  blocking collectives: 88.5 us -> 109 us
  starting transfers between devices: 21.5 us -> 12.7 us
    all_to_all x3 -> x4, blocking collectives: 88.5 us -> 109 us  [exchange(): return lax.all_to_all(blocks, axis, split_axis=0, concat_axis=0, tiled=True)]
    all_to_all x2 -> x1, waiting for transfers between devices: 44.8 us -> 26.4 us  [exchange(): return lax.all_to_all(blocks, axis, split_axis=0, concat_axis=0, tiled=True)]
    all_to_all x2 -> x1, starting transfers between devices: 17.7 us -> 6.77 us  [exchange(): return lax.all_to_all(blocks, axis, split_axis=0, concat_axis=0, tiled=True)]
    all_gather x1, waiting for transfers between devices: 5.57 us -> 0.02 us  [per_device(): late = lax.all_gather(late_rows, BLK, axis=0, tiled=True)]
    ppermute x1, starting transfers between devices: 3.78 us -> 5.94 us  [sibling(): return lax.ppermute(block, 'core', [(0, 1), (1, 0)])]
  transfers between devices with their start and end apart: 4 -> 3, of which waited for: 4 -> 2; matrix products, arithmetic and copies ran while one was open for 1% -> 1% of each run, Pallas kernels for 3% -> 3%
where the time goes in v4:
time: 183 us; the launch traced here: 182 us
  blocking collectives  109 us (60%)
  waiting for transfers between devices  29.9 us (16%)
  between operations  14.2 us (8%)
  starting transfers between devices  12.7 us (7%)
  Pallas kernels  5.89 us (3%)
  local copies, waits for them, and re-layouts  5.19 us (3%)
  matrix products  3.42 us (2%)
  other arithmetic  2.17 us (1%)
    all_to_all x4, blocking collectives, exchange(): return lax.all_to_all(blocks, axis, split_axis=0, concat_axis=0, tiled=True)  109 us
    all_to_all x1, waiting for transfers between devices, exchange(): return lax.all_to_all(blocks, axis, split_axis=0, concat_axis=0, tiled=True)  26.4 us
    all_to_all x1, starting transfers between devices, exchange(): return lax.all_to_all(blocks, axis, split_axis=0, concat_axis=0, tiled=True)  6.77 us
    ppermute x1, starting transfers between devices, sibling(): return lax.ppermute(block, 'core', [(0, 1), (1, 0)])  5.94 us
    pallas_call x1, Pallas kernels, attention(): pl.pallas_call(attention_kernel, out_shape=jax.ShapeDtypeStruct((groups,...  5.89 us
  transfers between devices with their start and end apart: 3, of which 2 were waited for; matrix products, arithmetic and copies ran while one was open for 1% of the time, Pallas kernels for 3%

profile of v4, /device:TPU:1, one launch (start us, length us, event | category | flops | bytes accessed | tf_op | source)
XLA Modules:
  0.0 182.5 jit_solution(12324142007223024483)
XLA Ops:
  6.5 0.0 copy-start
  6.5 0.0 all-gather.2.cloned.1.call-start
  6.5 0.8 copy-done
  7.4 1.6 concatenate.18
  9.0 0.0 all-gather.2.cloned.1.call-update
  9.0 0.7 fusion.29
  9.7 0.8 maximum_maximum_fusion
  10.6 28.0 %all_to_all.25 = bf16[8,32,1152]{2,1,0:T(8,128)(2,1)S(1)} all-to-all(bf16[8,32,1152]{2,1,0:T(8,128)(2,1)S(1)} %broadcast_in_dim.9), channel_id=1, replica_groups=mesh['head'=8,'z'=8,'x'=4,'core'=2] {'z'}, dimensions={0} | all-to-all | bytes 1179648 | tf_op jit(solution)/shard_map/all_to_all | solution.py:153
  38.6 0.2 broadcast_in_dim.10
  38.8 0.0 copy-start.5
  38.8 0.0 copy-start.1
  38.8 0.0 copy-start.2
  38.8 0.0 copy-start.3
  38.8 30.5 %all_to_all.26.mine_ref = bf16[4,8,32,1152]{3,2,1,0:T(8,128)(2,1)S(1)} all-to-all(bf16[4,8,32,1152]{3,2,1,0:T(8,128)(2,1)S(1)} %broadcast_in_dim.10), channel_id=1, replica_groups=mesh['head'=8,'z'=8,'x'=4,'core'=2] {'x'}, dimensions={0} | all-to-all | bytes 4718592 | tf_op jit(solution)/shard_map/all_to_all | solution.py:153
  69.3 5.9 %collective-permute-start = (bf16[4,8,32,1152]{3,2,1,0:T(8,128)(2,1)S(1)}, bf16[4,8,32,1152]{3,2,1,0:T(8,128)(2,1)}, u32[]{:S(2)}, u32[]{:S(2)}) collective-permute-start(bf16[4,8,32,1152]{3,2,1,0:T(8,128)(2,1)S(1)} %all_to_all.26.mine_ref), channel_id=1, source_target_pairs={{0,1},{1,0},{2,3},{3,2},{4,5},{5,4},{6,7},{7,6},{8,9},{9,8},{10,11... | collective-permute-start | bytes 7077896 | tf_op jit(solution)/shard_map/ppermute | solution.py:161
  75.9 0.0 copy-done.5
  75.9 0.1 copy.17.chosen_ref
  76.0 3.5 %collective-permute-done.other_ref = bf16[4,8,32,1152]{3,2,1,0:T(8,128)(2,1)} collective-permute-done((bf16[4,8,32,1152]{3,2,1,0:T(8,128)(2,1)S(1)}, bf16[4,8,32,1152]{3,2,1,0:T(8,128)(2,1)}, u32[]{:S(2)}, u32[]{:S(2)}) %collective-permute-start) | collective-permute-done | bytes 2359328 | tf_op jit(solution)/shard_map/ppermute | solution.py:161
  79.5 0.0 copy-done.1
  79.5 0.0 copy-done.2
  79.5 0.0 copy-done.3
  79.5 5.9 %shard_map.136 = bf16[8,224,256]{2,1,0:T(8,128)(2,1)} custom-call(s32[1,6]{1,0:T(1,128)S(1)} %copy-done.3, f32[1]{0:T(128)S(6)} %copy.24.lambda_ref, s32[1]{0:T(128)} %bitcast.core_ref, bf16[192,2048]{1,0:T(8,128)(2,1)S(1)} %copy-done.1, f32[1,2048]{1,0:T(1,128)S(1)} %bitcast.26, s32[192,1]{1,0:T(8,128)S(1)} %copy.17.chosen_ref, ...), custom_call_target="tpu_custom_call" | custom-call | flops 1200000000 | bytes 8000000 | tf_op jit(solution)/shard_map/pallas_call | solution.py:140
  85.4 6.8 %all-to-all-start.2 = ((bf16[8,224,256]{2,1,0:T(8,128)(2,1)}), bf16[8,224,256]{2,1,0:T(8,128)(2,1)S(1)}, u32[]{:S(2)}, u32[]{:S(2)}) async-start(bf16[8,224,256]{2,1,0:T(8,128)(2,1)} %shard_map.136), calls=%async_computation.2 | async-start | bytes 1835008 | tf_op jit(solution)/shard_map/all_to_all | solution.py:153
  92.2 26.4 %all-to-all-done.2 = bf16[8,224,256]{2,1,0:T(8,128)(2,1)S(1)} async-done(((bf16[8,224,256]{2,1,0:T(8,128)(2,1)}), bf16[8,224,256]{2,1,0:T(8,128)(2,1)S(1)}, u32[]{:S(2)}, u32[]{:S(2)}) %all-to-all-start.2) | async-done | bytes 917536 | tf_op jit(solution)/shard_map/all_to_all | solution.py:153
  118.6 0.1 convert_reduce_fusion
  118.7 0.3 fusion.8
  119.0 0.0 all-gather.2.cloned.1.call-done
  119.0 1.1 slice.63
  120.1 0.3 fusion.32
  120.4 0.0 copy-start.4
  120.4 0.3 fusion.31
  120.7 0.1 broadcast_in_dim.13
  120.8 26.1 %all_to_all.27 = bf16[8,192,256]{2,1,0:T(8,128)(2,1)S(1)} all-to-all(bf16[8,192,256]{2,1,0:T(8,128)(2,1)S(1)} %broadcast_in_dim.13), channel_id=1, replica_groups=mesh['head'=8,'z'=8,'x'=4,'core'=2] {'head'}, dimensions={0} | all-to-all | bytes 1572864 | tf_op jit(solution)/shard_map/all_to_all | solution.py:153
  146.9 0.1 convert_bitcast_fusion
  147.0 0.0 copy-start.6
  147.0 0.2 copy.21
  147.2 0.2 fusion.7
  147.5 0.0 copy-done.4
  147.5 0.3 copy-done.6
  147.7 1.4 fusion
  149.2 1.2 fusion.4
  150.4 0.1 copy.23
  150.4 24.4 %all_to_all.28 = bf16[8,192,256]{2,1,0:T(8,128)(2,1)S(1)} all-to-all(bf16[8,192,256]{2,1,0:T(8,128)(2,1)S(1)} %bitcast.27), channel_id=1, replica_groups=mesh['head'=8,'z'=8,'x'=4,'core'=2] {'head'}, dimensions={0} | all-to-all | bytes 1572864 | tf_op jit(solution)/shard_map/all_to_all | solution.py:153
  174.8 0.1 convert_reduce_fusion.1
  174.9 0.7 add_convert_fusion
  (8 shorter events, 0.2 us)
Async XLA Ops:
  6.5 0.8 copy-start
  6.5 112.5 %all-gather.2.cloned.1.call-start = ((), (), s32[]{:S(2)}) async-start(), calls=%async_computation.5 | async-start | bytes 9584640 | tf_op jit(solution)/shard_map/all_gather | solution.py:202
  38.8 37.1 %copy-start.5 = (s32[192,1]{0,1:T(1,128)S(1)}, s32[192,1]{0,1:T(1,128)}, u32[]{:S(2)}) copy-start(s32[192,1]{0,1:T(1,128)} %param.16) | copy-start | bytes 2308
  38.8 40.7 %copy-start.1 = (bf16[192,2048]{1,0:T(8,128)(2,1)S(1)}, bf16[192,2048]{1,0:T(8,128)(2,1)}, u32[]{:S(2)}) copy-start(bf16[192,2048]{1,0:T(8,128)(2,1)} %residual_ref.1) | copy-start | bytes 2359300
  38.8 40.7 %copy-start.2 = (f32[2048]{0:T(1024)S(1)}, f32[2048]{0:T(1024)}, u32[]{:S(2)}) copy-start(f32[2048]{0:T(1024)} %param.17) | copy-start | bytes 24580
  38.8 40.7 %copy-start.3 = (s32[1,6]{1,0:T(1,128)S(1)}, s32[1,6]{1,0:T(1,128)}, u32[]{:S(2)}) copy-start(s32[1,6]{1,0:T(1,128)} %lengths_ref.1) | copy-start | bytes 76
  69.3 10.2 %collective-permute-start = (bf16[4,8,32,1152]{3,2,1,0:T(8,128)(2,1)S(1)}, bf16[4,8,32,1152]{3,2,1,0:T(8,128)(2,1)}, u32[]{:S(2)}, u32[]{:S(2)}) collective-permute-start(bf16[4,8,32,1152]{3,2,1,0:T(8,128)(2,1)S(1)} %all_to_all.26.mine_ref), channel_id=1, source_target_pairs={{0,1},{1,0},{2,3},{3,2},{4,5},{5,4},{6,7},{7,6},{8,9},{9,8},{10,11... | collective-permute-start | bytes 7077896 | tf_op jit(solution)/shard_map/ppermute | solution.py:161
  85.4 33.2 %all-to-all-start.2 = ((bf16[8,224,256]{2,1,0:T(8,128)(2,1)}), bf16[8,224,256]{2,1,0:T(8,128)(2,1)S(1)}, u32[]{:S(2)}, u32[]{:S(2)}) async-start(bf16[8,224,256]{2,1,0:T(8,128)(2,1)} %shard_map.136), calls=%async_computation.2 | async-start | bytes 1835008 | tf_op jit(solution)/shard_map/all_to_all | solution.py:153
  120.4 27.1 %copy-start.4 = (bf16[2048,2240]{1,0:T(8,128)(2,1)S(1)}, bf16[2048,2240]{1,0:T(8,128)(2,1)}, u32[]{:S(2)}) copy-start(bf16[2048,2240]{1,0:T(8,128)(2,1)} %all-gather.2.cloned.1.call-done) | copy-start | bytes 27525124
  147.0 0.7 copy-start.6
Sparse Core Ops, SparseCore 0:
  10.7 97.2 all-gather.1

commit v5 on v4

--- a/solution.py
+++ b/solution.py
@@ -38,9 +38,9 @@
 
 
 def attention_kernel(
-    lengths_ref, lambda_ref, core_ref, residual_ref, gain_ref, chosen_ref, mine_ref, other_ref, sent_ref
+    lengths_ref, lambda_ref, core_ref, residual_ref, gain_ref, chosen_ref, mine_ref, other_ref, sent_ref, up_ref
 ):
-    slabs_x, slabs_z, rows, width = mine_ref.shape
+    slabs_x, slabs_z, rows, _ = mine_ref.shape
     tokens = residual_ref.shape[0]
     value_width = 2 * HD
     qkv_width = 4 * HD + value_width
@@ -93,13 +93,15 @@
 
         coordinates = jnp.zeros((tokens, adapters * RANK), jnp.float32)
         for half in range(2):
+            folded_rows = (half * RANK, (half + 1) * RANK)
             maps = jnp.concatenate(
-                [
-                    gather(z, out_end, width, half * RANK, (half + 1) * RANK)
-                    for z in range(slabs_z)
-                ],
-                axis=0,
-            )
+                [gather(z, out_end, out_end + HD, *folded_rows) for z in range(slabs_z)], axis=0
+            )
+            for z in range(slabs_z):
+                piece = gather(z, out_end + HD, out_end + 2 * HD, *folded_rows)
+                up_ref[z * piece.shape[0] : (z + 1) * piece.shape[0], half * HD : (half + 1) * HD] = (
+                    piece
+                )
             coordinates = coordinates + nt_dot(head_out[:, half * HD : (half + 1) * HD], maps)
         owner = lax.broadcasted_iota(jnp.int32, coordinates.shape, 1) // RANK
         kept = jnp.where(owner == chosen_ref[...], coordinates, 0.0)
@@ -139,9 +141,12 @@
     vmem = pl.BlockSpec(memory_space=pltpu.VMEM)
     return pl.pallas_call(
         attention_kernel,
-        out_shape=jax.ShapeDtypeStruct((groups, tokens + 2 * RANK, 2 * HD), jnp.bfloat16),
+        out_shape=[
+            jax.ShapeDtypeStruct((groups, tokens + 2 * RANK, 2 * HD), jnp.bfloat16),
+            jax.ShapeDtypeStruct((2 * mine.shape[0] * groups * RANK, 2 * HD), jnp.bfloat16),
+        ],
         in_specs=[smem] * 3 + [vmem] * 5,
-        out_specs=vmem,
+        out_specs=[vmem] * 2,
         compiler_params=pltpu.CompilerParams(vmem_limit_bytes=48 * 1024 * 1024),
         cost_estimate=pl.CostEstimate(
             flops=1_200_000_000, bytes_accessed=8_000_000, transcendentals=80_000
@@ -149,6 +154,92 @@
     )(lengths, second_weight, core, residual, gain.reshape(1, -1), chosen, mine, other)
 
 
+def feed_forward_kernel(mid_ref, gain_ref, weights_ref, out_ref, normed_ref, acts_ref, hidden_ref):
+    phase, step = pl.program_id(0), pl.program_id(1)
+    groups, _, slab = mid_ref.shape
+    pairs = weights_ref.shape[1]
+    per_step = weights_ref.shape[0] // slab
+
+    @pl.when((phase == 0) & (step == 0))
+    def _():
+        mid = mid_ref[...].astype(jnp.float32)
+        square = jnp.sum(jnp.sum(mid * mid, axis=0), axis=-1, keepdims=True) / (groups * slab)
+        scaled = mid * lax.rsqrt(square + 1e-06)[None] * gain_ref[...]
+        normed_ref[...] = scaled.astype(jnp.bfloat16)
+
+    @pl.when(phase < 2)
+    def _():
+        product = sum(
+            jnp.dot(
+                normed_ref[step * per_step + i],
+                weights_ref[i * slab : (i + 1) * slab, :],
+                preferred_element_type=jnp.float32,
+            )
+            for i in range(per_step)
+        )
+
+        @pl.when(step == 0)
+        def _():
+            acts_ref[...] = product
+
+        @pl.when(step > 0)
+        def _():
+            acts_ref[...] += product
+
+    last = step == pl.num_programs(1) - 1
+
+    @pl.when(last & (phase == 0))
+    def _():
+        acts = acts_ref[...]
+        hidden_ref[...] = jax.nn.silu(acts) * pltpu.roll(acts, pairs // 2, 1)
+
+    @pl.when(last & (phase == 1))
+    def _():
+        acts = acts_ref[...]
+        lane = lax.broadcasted_iota(jnp.int32, acts.shape, 1)
+        hidden_ref[...] = jnp.where(
+            lane < pairs // 2,
+            hidden_ref[...],
+            jax.nn.silu(pltpu.roll(acts, pairs // 2, 1)) * acts,
+        )
+
+    @pl.when(phase == 2)
+    def _():
+        hidden = hidden_ref[...].astype(jnp.bfloat16)
+        for i in range(per_step):
+            out_ref[i] = nt_dot(hidden, weights_ref[i * slab : (i + 1) * slab, :]).astype(jnp.bfloat16)
+
+
+def feed_forward(mid, gain, weights):
+    groups, part, slab = mid.shape
+    width, columns = weights.shape
+    pairs = columns // 3
+    steps = 4
+    return pl.pallas_call(
+        feed_forward_kernel,
+        grid=(3, steps),
+        out_shape=jax.ShapeDtypeStruct(mid.shape, jnp.bfloat16),
+        in_specs=[
+            pl.BlockSpec(mid.shape, lambda phase, step: (0, 0, 0)),
+            pl.BlockSpec((groups, 1, slab), lambda phase, step: (0, 0, 0)),
+            pl.BlockSpec((width // steps, pairs), lambda phase, step: (step, phase)),
+        ],
+        out_specs=pl.BlockSpec(
+            (groups // steps, part, slab),
+            lambda phase, step: (jnp.where(phase == 2, step, 0), 0, 0),
+        ),
+        scratch_shapes=[
+            pltpu.VMEM(mid.shape, jnp.bfloat16),
+            pltpu.VMEM((part, pairs), jnp.float32),
+            pltpu.VMEM((part, pairs), jnp.float32),
+        ],
+        compiler_params=pltpu.CompilerParams(vmem_limit_bytes=40 * 1024 * 1024),
+        cost_estimate=pl.CostEstimate(
+            flops=1_700_000_000, bytes_accessed=18_000_000, transcendentals=300_000
+        ),
+    )(mid, gain.reshape(groups, 1, slab), weights)
+
+
 def exchange(blocks, axis):
     return lax.all_to_all(blocks, axis, split_axis=0, concat_axis=0, tiled=True)
 
@@ -164,11 +255,6 @@
 def fold_map(rank_rows):
     half = rank_rows.shape[1] // 2
     return jnp.concatenate([rank_rows[:, :half], rank_rows[:, half:]], axis=0)
-
-
-def unfold_map(folded, owners):
-    stacked = folded.reshape(owners, 2, RANK, folded.shape[1])
-    return [stacked[:, i].reshape(owners * RANK, folded.shape[1]) for i in range(2)]
 
 
 def per_device(
@@ -197,13 +283,27 @@
     down_map = fold_map(adapter_down_maps[0].T)
     up_map = fold_map(lax.dynamic_slice_in_dim(adapter_up_maps[0], own_begin, own_width, 1))
 
-    early = jnp.concatenate([query_key_weight, value_weight, output_weight, down_map], axis=1)
-    late_rows = jnp.concatenate([gate_weight, up_weight, up_map, down_weight], axis=1)
-    late = lax.all_gather(late_rows, BLK, axis=0, tiled=True)
+    early = jnp.concatenate([query_key_weight, value_weight, output_weight, down_map, up_map], axis=1)
+    acts_own = jnp.concatenate([gate_weight, up_weight, down_weight], axis=1)
+    acts_pair = lax.ppermute(acts_own, "head", [(i, i ^ 1) for i in range(groups)])
+    late = lax.all_gather(
+        jnp.concatenate(
+            [
+                acts_own[:, : 2 * units],
+                acts_pair[:, : 2 * units],
+                acts_own[:, 2 * units :],
+                acts_pair[:, 2 * units :],
+            ],
+            axis=1,
+        ),
+        BLK,
+        axis=0,
+        tiled=True,
+    )
     mine = spread(spread(early, "z"), "x")
     other = sibling(mine)
     core = lax.axis_index("core").astype(jnp.int32).reshape(1)
-    sent = attention(
+    sent, up_maps = attention(
         lengths,
         head_second_weight,
         core,
@@ -229,34 +329,21 @@
         preferred_element_type=jnp.float32,
     )
     routed = jnp.where(chosen, lifted, 0.0).astype(jnp.bfloat16)
-    up_maps = unfold_map(late[:, 2 * units : 2 * units + own_width // 2], owners)
     delta_own = (
-        adapter_scaling
-        * jnp.concatenate(
-            [jnp.dot(routed, part, preferred_element_type=jnp.float32) for part in up_maps], axis=1
-        )
+        adapter_scaling * jnp.dot(routed, up_maps, preferred_element_type=jnp.float32)
     ).astype(jnp.bfloat16)
     own_mid = (
         lax.dynamic_slice_in_dim(inputs, own_begin, own_width, 1)
         + total[:tokens]
         + delta_own.astype(jnp.float32)
     )
-    mid_full = spread(own_mid.astype(jnp.bfloat16), "head").transpose(1, 0, 2).reshape(tokens, width)
-    ffn_in = (rms_scale(mid_full.astype(jnp.float32), 1e-06) * feedforward_norm_gain).astype(
-        jnp.bfloat16
-    )
-    both_acts = jnp.dot(ffn_in, late[:, : 2 * units], preferred_element_type=jnp.float32)
-    hidden_units = (jax.nn.silu(both_acts[:, :units]) * both_acts[:, units:]).astype(jnp.bfloat16)
-    piece = lax.dot_general(
-        hidden_units,
-        late[:, 2 * units + own_width // 2 :],
-        (((1,), (1,)), ((), ())),
-        preferred_element_type=jnp.float32,
-    ).astype(jnp.bfloat16)
-    piece = piece.reshape(tokens, groups, own_width).transpose(1, 0, 2)
-    return (own_mid + jnp.sum(exchange(piece, "head").astype(jnp.float32), axis=0)).astype(
-        jnp.bfloat16
-    )
+    part = tokens // 2
+    halves = own_mid.astype(jnp.bfloat16).reshape(1, 2, part, own_width)
+    halves = jnp.broadcast_to(halves, (groups // 2, 2, part, own_width))
+    mid_full = exchange(halves.reshape(groups, part, own_width), "head")
+    piece = feed_forward(mid_full, feedforward_norm_gain, late)
+    pieces = exchange(piece, "head").reshape(groups // 2, tokens, own_width)
+    return (own_mid + jnp.sum(pieces.astype(jnp.float32), axis=0)).astype(jnp.bfloat16)
 
 
 def solution(mesh):

time: 183 us -> 192 us (1.049)
  blocking collectives: 109 us -> 92.8 us
  Pallas kernels: 5.89 us -> 17.6 us
  starting transfers between devices: 12.7 us -> 22.7 us
  local copies, waits for them, and re-layouts: 5.19 us -> 9.36 us
  matrix products: 3.42 us -> 0.52 us
  waiting for transfers between devices: 29.9 us -> 32.1 us
    all_to_all x4, blocking collectives: 109 us -> 92.8 us  [exchange(): return lax.all_to_all(blocks, axis, split_axis=0, concat_axis=0, tiled=True)]
    pallas_call x1 -> x2, Pallas kernels: 5.89 us -> 17.6 us  [the longest x1 12.7 us: feed_forward(): pl.pallas_call(feed_forward_kernel, grid=(3, steps), out_shape=jax.ShapeD...]
    ppermute x1, starting transfers between devices: 5.94 us -> 10.8 us  [sibling(): return lax.ppermute(block, 'core', [(0, 1), (1, 0)])]
    unnamed x15 -> x24, local copies, waits for them, and re-layouts: 1.25 us -> 5.62 us
    ppermute x0 -> x1, starting transfers between devices: none -> 4.03 us  [per_device(): lax.ppermute(acts_own, 'head', [(i, i ^ 1) for i in range(groups)])]
    dot_general x5 -> x1, matrix products: 3.42 us -> 0.52 us  [per_device(): jnp.dot(routed, up_maps, preferred_element_type=jnp.float32)]
    ppermute x0 -> x1, waiting for transfers between devices: none -> 2.43 us  [per_device(): lax.ppermute(acts_own, 'head', [(i, i ^ 1) for i in range(groups)])]
  transfers between devices with their start and end apart: 3 -> 4, of which waited for: 2 -> 3; matrix products, arithmetic and copies ran while one was open for 1% -> 2% of each run, Pallas kernels for 3% -> 3%
where the time goes in v5:
time: 192 us; the launch traced here: 190 us
  blocking collectives  92.8 us (48%)
  waiting for transfers between devices  32.1 us (17%)
  starting transfers between devices  22.7 us (12%)
  Pallas kernels  17.6 us (9%)
  between operations  14.2 us (7%)
  local copies, waits for them, and re-layouts  9.36 us (5%)
    all_to_all x4, blocking collectives, exchange(): return lax.all_to_all(blocks, axis, split_axis=0, concat_axis=0, tiled=True)  92.8 us
    all_to_all x1, waiting for transfers between devices, exchange(): return lax.all_to_all(blocks, axis, split_axis=0, concat_axis=0, tiled=True)  26.4 us
    pallas_call x1, Pallas kernels, feed_forward(): pl.pallas_call(feed_forward_kernel, grid=(3, steps), out_shape=jax.ShapeD...  12.7 us
    ppermute x1, starting transfers between devices, sibling(): return lax.ppermute(block, 'core', [(0, 1), (1, 0)])  10.8 us
    all_to_all x1, starting transfers between devices, exchange(): return lax.all_to_all(blocks, axis, split_axis=0, concat_axis=0, tiled=True)  7.88 us
    unnamed x24, local copies, waits for them, and re-layouts  5.62 us
    pallas_call x1, Pallas kernels, attention(): pl.pallas_call(attention_kernel, out_shape=[jax.ShapeDtypeStruct((groups,...  4.92 us
    ppermute x1, starting transfers between devices, per_device(): lax.ppermute(acts_own, 'head', [(i, i ^ 1) for i in range(groups)])  4.03 us
  transfers between devices with their start and end apart: 4, of which 3 were waited for; matrix products, arithmetic and copies ran while one was open for 2% of the time, Pallas kernels for 3%

profile of v5, /device:TPU:1, one launch (start us, length us, event | category | flops | bytes accessed | tf_op | source)
XLA Modules:
  0.0 190.1 jit_solution(11465135489832693688)
XLA Ops:
  6.5 0.0 copy-start
  6.5 0.0 all-gather.2.cloned.1.call-start
  6.5 1.0 concatenate.20
  7.5 4.0 %collective-permute-start.1 = (bf16[32,2112]{1,0:T(8,128)(2,1)S(1)}, bf16[32,2112]{1,0:T(8,128)(2,1)S(1)}, u32[]{:S(2)}, u32[]{:S(2)}) collective-permute-start(bf16[32,2112]{1,0:T(8,128)(2,1)S(1)} %concatenate.20), channel_id=1, source_target_pairs={{0,64},{64,0},{128,192},{192,128},{256,320},{320,256},{384,448},{4... | collective-permute-start | bytes 405512 | tf_op jit(solution)/shard_map/ppermute | solution.py:288
  11.6 2.4 %collective-permute-done.1 = bf16[32,2112]{1,0:T(8,128)(2,1)S(1)} collective-permute-done((bf16[32,2112]{1,0:T(8,128)(2,1)S(1)}, bf16[32,2112]{1,0:T(8,128)(2,1)S(1)}, u32[]{:S(2)}, u32[]{:S(2)}) %collective-permute-start.1) | collective-permute-done | bytes 135200 | tf_op jit(solution)/shard_map/ppermute | solution.py:288
  14.0 1.7 concatenate.21
  15.7 0.0 all-gather.2.cloned.1.call-update
  15.7 0.0 copy-done
  15.8 0.8 constant_dynamic-update-slice_fusion.4
  16.5 0.7 constant_dynamic-update-slice_fusion.3
  17.2 0.7 constant_dynamic-update-slice_fusion.2
  18.0 0.7 fusion.24
  18.7 29.5 %all_to_all.25 = bf16[8,32,1280]{2,1,0:T(8,128)(2,1)S(1)} all-to-all(bf16[8,32,1280]{2,1,0:T(8,128)(2,1)S(1)} %broadcast_in_dim.11), channel_id=1, replica_groups=mesh['head'=8,'z'=8,'x'=4,'core'=2] {'z'}, dimensions={0} | all-to-all | bytes 1310720 | tf_op jit(solution)/shard_map/all_to_all | solution.py:244
  48.3 0.3 broadcast_in_dim.13
  48.5 0.0 copy-start.9
  48.6 0.0 copy-start.2
  48.6 0.0 copy-start.4
  48.6 0.0 copy-start.6
  48.6 31.0 %all_to_all.26.mine_ref = bf16[4,8,32,1280]{3,2,1,0:T(8,128)(2,1)S(1)} all-to-all(bf16[4,8,32,1280]{3,2,1,0:T(8,128)(2,1)S(1)} %broadcast_in_dim.13), channel_id=1, replica_groups=mesh['head'=8,'z'=8,'x'=4,'core'=2] {'x'}, dimensions={0} | all-to-all | bytes 5242880 | tf_op jit(solution)/shard_map/all_to_all | solution.py:244
  79.6 10.8 %collective-permute-start = (bf16[4,8,32,1280]{3,2,1,0:T(8,128)(2,1)S(1)}, bf16[4,8,32,1280]{3,2,1,0:T(8,128)(2,1)}, u32[]{:S(2)}, u32[]{:S(2)}) collective-permute-start(bf16[4,8,32,1280]{3,2,1,0:T(8,128)(2,1)S(1)} %all_to_all.26.mine_ref), channel_id=1, source_target_pairs={{0,1},{1,0},{2,3},{3,2},{4,5},{5,4},{6,7},{7,6},{8,9},{9,8},{10,11... | collective-permute-start | bytes 7864328 | tf_op jit(solution)/shard_map/ppermute | solution.py:252
  91.1 0.0 copy-done.9
  91.1 0.8 copy.15.chosen_ref
  91.8 3.2 %collective-permute-done.other_ref = bf16[4,8,32,1280]{3,2,1,0:T(8,128)(2,1)} collective-permute-done((bf16[4,8,32,1280]{3,2,1,0:T(8,128)(2,1)S(1)}, bf16[4,8,32,1280]{3,2,1,0:T(8,128)(2,1)}, u32[]{:S(2)}, u32[]{:S(2)}) %collective-permute-start) | collective-permute-done | bytes 2621472 | tf_op jit(solution)/shard_map/ppermute | solution.py:252
  95.1 0.0 copy-done.2
  95.1 0.0 copy-done.4
  95.1 0.0 copy-done.6
  95.1 0.0 copy-start.3
  95.1 0.9 copy-done.3
  96.0 4.9 %shard_map.136 = (bf16[8,224,256]{2,1,0:T(8,128)(2,1)S(1)}, bf16[1024,256]{1,0:T(8,128)(2,1)S(1)}) custom-call(s32[1,6]{1,0:T(1,128)S(1)} %copy-done.6, f32[1]{0:T(128)S(6)} %copy.20.lambda_ref, s32[1]{0:T(128)} %bitcast.core_ref, bf16[192,2048]{1,0:T(8,128)(2,1)S(1)} %copy-done.2, f32[1,2048]{1,0:T(1,128)S(1)} %bitcast.16, s32[192,1]{1,0:T(8,128)S(1)} %copy-done.3, ...), custom_call_target="tpu_custom_call" | custom-call | flops 1200000000 | bytes 8000000 | tf_op jit(solution)/shard_map/pallas_call | solution.py:142
  100.9 0.0 copy-start.1
  100.9 0.9 copy-done.1
  101.8 0.0 copy-start.7
  101.8 0.8 copy-done.7
  102.6 0.0 copy-start.8
  102.6 0.0 copy-start.5
  102.6 7.9 %all-to-all-start.2 = ((bf16[8,224,256]{2,1,0:T(8,128)(2,1)}), bf16[8,224,256]{2,1,0:T(8,128)(2,1)S(1)}, u32[]{:S(2)}, u32[]{:S(2)}) async-start(bf16[8,224,256]{2,1,0:T(8,128)(2,1)} %copy-done.1), calls=%async_computation.2 | async-start | bytes 1835008 | tf_op jit(solution)/shard_map/all_to_all | solution.py:244
  110.5 26.4 %all-to-all-done.2 = bf16[8,224,256]{2,1,0:T(8,128)(2,1)S(1)} async-done(((bf16[8,224,256]{2,1,0:T(8,128)(2,1)}), bf16[8,224,256]{2,1,0:T(8,128)(2,1)S(1)}, u32[]{:S(2)}, u32[]{:S(2)}) %all-to-all-start.2) | async-done | bytes 917536 | tf_op jit(solution)/shard_map/all_to_all | solution.py:244
  136.9 0.1 convert_reduce_fusion
  137.0 0.0 copy-done.8
  137.0 0.5 fusion.25
  137.6 16.7 %all_to_all.27.mid_ref = bf16[8,96,256]{2,1,0:T(8,128)(2,1)S(1)} all-to-all(bf16[8,96,256]{2,1,0:T(8,128)(2,1)S(1)} %bitcast.19), channel_id=1, replica_groups=mesh['head'=8,'z'=8,'x'=4,'core'=2] {'head'}, dimensions={0} | all-to-all | bytes 786432 | tf_op jit(solution)/shard_map/all_to_all | solution.py:244
  154.3 0.0 all-gather.2.cloned.1.call-done.weights_ref
  154.3 0.0 copy-done.5
  154.3 12.7 %shard_map.137 = bf16[8,96,256]{2,1,0:T(8,128)(2,1)S(1)} custom-call(bf16[8,96,256]{2,1,0:T(8,128)(2,1)S(1)} %all_to_all.27.mid_ref, f32[8,1,256]{2,1,0:T(1,128)S(1)} %bitcast.17, bf16[2048,4224]{1,0:T(8,128)(2,1)} %all-gather.2.cloned.1.call-done.weights_ref), custom_call_target="tpu_custom_call" | custom-call | flops 1700000000 | bytes 18000000 | tf_op jit(solution)/shard_map/pallas_call | solution.py:218
  167.0 15.6 %all_to_all.28 = bf16[8,96,256]{2,1,0:T(8,128)(2,1)S(1)} all-to-all(bf16[8,96,256]{2,1,0:T(8,128)(2,1)S(1)} %shard_map.137), channel_id=1, replica_groups=mesh['head'=8,'z'=8,'x'=4,'core'=2] {'head'}, dimensions={0} | all-to-all | bytes 786432 | tf_op jit(solution)/shard_map/all_to_all | solution.py:244
  182.6 0.7 add_convert_fusion
  (10 shorter events, 0.2 us)
Async XLA Ops:
  6.5 9.2 %copy-start = (bf16[1,16,2048]{2,1,0:T(8,128)(2,1)S(1)}, bf16[1,16,2048]{2,1,0:T(8,128)(2,1)}, u32[]{:S(2)}) copy-start(bf16[1,16,2048]{2,1,0:T(8,128)(2,1)} %param.23) | copy-start | bytes 196612
  6.5 147.8 %all-gather.2.cloned.1.call-start = ((), (), s32[]{:S(2)}) async-start(), calls=%async_computation.5 | async-start | bytes 17571840 | tf_op jit(solution)/shard_map/all_gather | solution.py:289
  7.5 6.5 %collective-permute-start.1 = (bf16[32,2112]{1,0:T(8,128)(2,1)S(1)}, bf16[32,2112]{1,0:T(8,128)(2,1)S(1)}, u32[]{:S(2)}, u32[]{:S(2)}) collective-permute-start(bf16[32,2112]{1,0:T(8,128)(2,1)S(1)} %concatenate.20), channel_id=1, source_target_pairs={{0,64},{64,0},{128,192},{192,128},{256,320},{320,256},{384,448},{4... | collective-permute-start | bytes 405512 | tf_op jit(solution)/shard_map/ppermute | solution.py:288
  48.5 42.5 %copy-start.9 = (s32[192,1]{0,1:T(1,128)S(1)}, s32[192,1]{0,1:T(1,128)}, u32[]{:S(2)}) copy-start(s32[192,1]{0,1:T(1,128)} %param.16) | copy-start | bytes 2308
  48.6 46.5 %copy-start.2 = (bf16[192,2048]{1,0:T(8,128)(2,1)S(1)}, bf16[192,2048]{1,0:T(8,128)(2,1)}, u32[]{:S(2)}) copy-start(bf16[192,2048]{1,0:T(8,128)(2,1)} %residual_ref.1) | copy-start | bytes 2359300
  48.6 46.5 %copy-start.4 = (f32[2048]{0:T(1024)S(1)}, f32[2048]{0:T(1024)}, u32[]{:S(2)}) copy-start(f32[2048]{0:T(1024)} %param.17) | copy-start | bytes 24580
  48.6 46.5 %copy-start.6 = (s32[1,6]{1,0:T(1,128)S(1)}, s32[1,6]{1,0:T(1,128)}, u32[]{:S(2)}) copy-start(s32[1,6]{1,0:T(1,128)} %lengths_ref.1) | copy-start | bytes 76
  79.6 15.4 %collective-permute-start = (bf16[4,8,32,1280]{3,2,1,0:T(8,128)(2,1)S(1)}, bf16[4,8,32,1280]{3,2,1,0:T(8,128)(2,1)}, u32[]{:S(2)}, u32[]{:S(2)}) collective-permute-start(bf16[4,8,32,1280]{3,2,1,0:T(8,128)(2,1)S(1)} %all_to_all.26.mine_ref), channel_id=1, source_target_pairs={{0,1},{1,0},{2,3},{3,2},{4,5},{5,4},{6,7},{7,6},{8,9},{9,8},{10,11... | collective-permute-start | bytes 7864328 | tf_op jit(solution)/shard_map/ppermute | solution.py:252
  95.1 0.9 copy-start.3
  100.9 0.9 copy-start.1
  101.8 0.8 copy-start.7
  102.6 34.4 %copy-start.8 = (bf16[1024,256]{1,0:T(8,128)(2,1)S(1)}, bf16[1024,256]{1,0:T(8,128)(2,1)}, u32[]{:S(2)}) copy-start(bf16[1024,256]{1,0:T(8,128)(2,1)} %copy-done.7) | copy-start | bytes 1572868
  102.6 51.7 %copy-start.5 = (f32[2048]{0:T(1024)S(1)}, f32[2048]{0:T(1024)}, u32[]{:S(2)}) copy-start(f32[2048]{0:T(1024)} %param.24) | copy-start | bytes 24580
  102.6 34.3 %all-to-all-start.2 = ((bf16[8,224,256]{2,1,0:T(8,128)(2,1)}), bf16[8,224,256]{2,1,0:T(8,128)(2,1)S(1)}, u32[]{:S(2)}, u32[]{:S(2)}) async-start(bf16[8,224,256]{2,1,0:T(8,128)(2,1)} %copy-done.1), calls=%async_computation.2 | async-start | bytes 1835008 | tf_op jit(solution)/shard_map/all_to_all | solution.py:244
Sparse Core Ops, SparseCore 0:
  15.8 115.9 all-gather.1

commit v6 on v4

--- a/solution.py
+++ b/solution.py
@@ -40,7 +40,7 @@
 def attention_kernel(
     lengths_ref, lambda_ref, core_ref, residual_ref, gain_ref, chosen_ref, mine_ref, other_ref, sent_ref
 ):
-    slabs_x, slabs_z, rows, width = mine_ref.shape
+    slabs_x, slabs_z, rows, _ = mine_ref.shape
     tokens = residual_ref.shape[0]
     value_width = 2 * HD
     qkv_width = 4 * HD + value_width
@@ -93,12 +93,9 @@
 
         coordinates = jnp.zeros((tokens, adapters * RANK), jnp.float32)
         for half in range(2):
+            folded_rows = (half * RANK, (half + 1) * RANK)
             maps = jnp.concatenate(
-                [
-                    gather(z, out_end, width, half * RANK, (half + 1) * RANK)
-                    for z in range(slabs_z)
-                ],
-                axis=0,
+                [gather(z, out_end, out_end + HD, *folded_rows) for z in range(slabs_z)], axis=0
             )
             coordinates = coordinates + nt_dot(head_out[:, half * HD : (half + 1) * HD], maps)
         owner = lax.broadcasted_iota(jnp.int32, coordinates.shape, 1) // RANK
@@ -149,6 +146,179 @@
     )(lengths, second_weight, core, residual, gain.reshape(1, -1), chosen, mine, other)
 
 
+def middle_kernel(core_ref, chosen_ref, residual_ref, received_ref, mine_ref, other_ref, mid_ref, sent_ref):
+    slabs_x, slabs_z, _, half_width = mine_ref.shape
+    tokens = chosen_ref.shape[0]
+    part = tokens // 2
+    adapters = 2 * slabs_x * slabs_z
+
+    def body(even_ref, odd_ref):
+        total = received_ref[0].astype(jnp.float32)
+        for group in range(1, received_ref.shape[0]):
+            total = total + received_ref[group].astype(jnp.float32)
+        low_rank = (total[tokens : tokens + RANK] + total[tokens + RANK :]).astype(jnp.bfloat16)
+        lift_shape = (RANK, adapters * RANK)
+        lift = jnp.where(
+            lax.broadcasted_iota(jnp.int32, lift_shape, 1) % RANK
+            == lax.broadcasted_iota(jnp.int32, lift_shape, 0),
+            1.0,
+            0.0,
+        ).astype(jnp.bfloat16)
+        lifted = lax.dot_general(
+            low_rank, lift, (((0,), (0,)), ((), ())), preferred_element_type=jnp.float32
+        )[:tokens]
+        owner = lax.broadcasted_iota(jnp.int32, lifted.shape, 1) // RANK
+        routed = jnp.where(owner == chosen_ref[...], lifted, 0.0).astype(jnp.bfloat16)
+        for half in range(2):
+            maps = jnp.concatenate(
+                [
+                    ref[x, z, half * RANK : (half + 1) * RANK, :]
+                    for z in range(slabs_z)
+                    for x in range(slabs_x)
+                    for ref in (even_ref, odd_ref)
+                ],
+                axis=0,
+            )
+            delta = (
+                adapter_scaling * jnp.dot(routed, maps, preferred_element_type=jnp.float32)
+            ).astype(jnp.bfloat16)
+            lanes = slice(half * half_width, (half + 1) * half_width)
+            mid = residual_ref[:, lanes].astype(jnp.float32) + total[:tokens, lanes]
+            mid_ref[:, lanes] = mid + delta.astype(jnp.float32)
+        rounded = mid_ref[...].astype(jnp.bfloat16)
+        for group in range(sent_ref.shape[0]):
+            side = group % 2
+            sent_ref[group] = rounded[side * part : (side + 1) * part]
+
+    @pl.when(core_ref[0] == 0)
+    def _():
+        body(mine_ref, other_ref)
+
+    @pl.when(core_ref[0] != 0)
+    def _():
+        body(other_ref, mine_ref)
+
+
+def middle(core, chosen, residual, received, mine, other):
+    tokens, own_width = residual.shape
+    groups = received.shape[0]
+    last = mine.shape[3] // HD - 1
+    vmem = pl.BlockSpec(memory_space=pltpu.VMEM)
+    maps = pl.BlockSpec((*mine.shape[:3], HD), lambda i: (0, 0, 0, last))
+
+    def whole(array):
+        return pl.BlockSpec(array.shape, lambda i: (0,) * len(array.shape))
+
+    return pl.pallas_call(
+        middle_kernel,
+        grid=(1,),
+        out_shape=[
+            jax.ShapeDtypeStruct((tokens, own_width), jnp.float32),
+            jax.ShapeDtypeStruct((groups, tokens // 2, own_width), jnp.bfloat16),
+        ],
+        in_specs=[
+            pl.BlockSpec(memory_space=pltpu.SMEM),
+            whole(chosen),
+            whole(residual),
+            whole(received),
+            maps,
+            maps,
+        ],
+        out_specs=[
+            pl.BlockSpec((tokens, own_width), lambda i: (0, 0)),
+            pl.BlockSpec((groups, tokens // 2, own_width), lambda i: (0, 0, 0)),
+        ],
+        compiler_params=pltpu.CompilerParams(vmem_limit_bytes=32 * 1024 * 1024),
+        cost_estimate=pl.CostEstimate(
+            flops=120_000_000, bytes_accessed=3_000_000, transcendentals=0
+        ),
+    )(core, chosen, residual, received, mine, other)
+
+
+def feed_forward_kernel(mid_ref, gain_ref, weights_ref, out_ref, acts_ref, down_ref, acts_in, down_in):
+    sides, steps, owners, rows, pairs = acts_ref.shape
+    padded = down_ref.shape[4]
+    groups, _, slab = mid_ref.shape
+    units = pairs // 2
+    per_step = owners * rows // slab
+
+    def fetch(side, step, begin, count, held_ref, arrived):
+        return pltpu.make_async_copy(
+            weights_ref.at[pl.ds(step * owners, owners), side, :, pl.ds(begin, count)],
+            held_ref.at[side, step],
+            arrived.at[side, step],
+        )
+
+    acts_copies = [
+        [fetch(side, step, 0, pairs, acts_ref, acts_in) for step in range(steps)]
+        for side in range(sides)
+    ]
+    down_copies = [
+        [fetch(side, step, pairs, padded, down_ref, down_in) for side in range(sides)]
+        for step in range(steps)
+    ]
+    for row in acts_copies + down_copies:
+        for copy in row:
+            copy.start()
+    mid = mid_ref[...].astype(jnp.float32)
+    square = jnp.sum(jnp.sum(mid * mid, axis=0), axis=-1, keepdims=True) / (groups * slab)
+    normed = (mid * lax.rsqrt(square + 1e-06)[None] * gain_ref[...]).astype(jnp.bfloat16)
+
+    hidden = []
+    for side in range(sides):
+        acts = None
+        for step in range(steps):
+            left = jnp.concatenate(
+                [normed[step * per_step + i] for i in range(per_step)], axis=1
+            )
+            acts_copies[side][step].wait()
+            product = jnp.dot(
+                left,
+                acts_ref[side, step].reshape(owners * rows, pairs),
+                preferred_element_type=jnp.float32,
+            )
+            acts = product if acts is None else acts + product
+        upward = pltpu.roll(acts, units, 1)[:, :padded]
+        lane = lax.broadcasted_iota(jnp.int32, upward.shape, 1)
+        gated = jax.nn.silu(acts[:, :padded]) * upward
+        hidden.append(jnp.where(lane < units, gated, 0.0).astype(jnp.bfloat16))
+    for step in range(steps):
+        for copy in down_copies[step]:
+            copy.wait()
+        for i in range(per_step):
+            picked = slice(i * slab, (i + 1) * slab)
+            out_ref[step * per_step + i] = sum(
+                nt_dot(
+                    hidden[side], down_ref[side, step].reshape(owners * rows, padded)[picked]
+                )
+                for side in range(sides)
+            ).astype(jnp.bfloat16)
+
+
+def feed_forward(mid, gain, weights, units):
+    groups, _, slab = mid.shape
+    owners, sides, rows, columns = weights.shape
+    steps = 4
+    held = (sides, steps, owners // steps, rows)
+    vmem = pl.BlockSpec(memory_space=pltpu.VMEM)
+    return pl.pallas_call(
+        feed_forward_kernel,
+        out_shape=jax.ShapeDtypeStruct(mid.shape, jnp.bfloat16),
+        in_specs=[vmem, vmem, pl.BlockSpec(memory_space=pl.ANY)],
+        out_specs=vmem,
+        scratch_shapes=[
+            pltpu.VMEM((*held, 2 * units), jnp.bfloat16),
+            pltpu.VMEM((*held, columns - 2 * units), jnp.bfloat16),
+            pltpu.SemaphoreType.DMA((sides, steps)),
+            pltpu.SemaphoreType.DMA((sides, steps)),
+        ],
+        compiler_params=pltpu.CompilerParams(vmem_limit_bytes=40 * 1024 * 1024),
+        cost_estimate=pl.CostEstimate(
+            flops=1_700_000_000, bytes_accessed=18_000_000, transcendentals=300_000
+        ),
+    )(mid, gain.reshape(groups, 1, slab), weights)
+
+
 def exchange(blocks, axis):
     return lax.all_to_all(blocks, axis, split_axis=0, concat_axis=0, tiled=True)
 
@@ -164,11 +334,6 @@
 def fold_map(rank_rows):
     half = rank_rows.shape[1] // 2
     return jnp.concatenate([rank_rows[:, :half], rank_rows[:, half:]], axis=0)
-
-
-def unfold_map(folded, owners):
-    stacked = folded.reshape(owners, 2, RANK, folded.shape[1])
-    return [stacked[:, i].reshape(owners * RANK, folded.shape[1]) for i in range(2)]
 
 
 def per_device(
@@ -189,7 +354,6 @@
 ):
     tokens, width = residual.shape
     groups = lax.axis_size("head")
-    owners = lax.axis_size(BLK)
     own_width = width // groups
     own_begin = lax.axis_index("head") * own_width
     units = gate_weight.shape[1]
@@ -197,9 +361,12 @@
     down_map = fold_map(adapter_down_maps[0].T)
     up_map = fold_map(lax.dynamic_slice_in_dim(adapter_up_maps[0], own_begin, own_width, 1))
 
-    early = jnp.concatenate([query_key_weight, value_weight, output_weight, down_map], axis=1)
-    late_rows = jnp.concatenate([gate_weight, up_weight, up_map, down_weight], axis=1)
-    late = lax.all_gather(late_rows, BLK, axis=0, tiled=True)
+    early = jnp.concatenate([query_key_weight, value_weight, output_weight, down_map, up_map], axis=1)
+    room = jnp.zeros((gate_weight.shape[0], -units % HD), gate_weight.dtype)
+    acts_own = jnp.concatenate([gate_weight, up_weight, down_weight, room], axis=1)
+    acts_pair = lax.ppermute(acts_own, "head", [(i, i ^ 1) for i in range(groups)])
+    early, acts_pair = lax.optimization_barrier((early, acts_pair))
+    late = lax.all_gather(jnp.stack([acts_own, acts_pair]), BLK, axis=0, tiled=False)
     mine = spread(spread(early, "z"), "x")
     other = sibling(mine)
     core = lax.axis_index("core").astype(jnp.int32).reshape(1)
@@ -214,49 +381,14 @@
         other,
     )
 
-    inputs = residual.astype(jnp.float32)
-    coordinate = jnp.arange(owners * RANK, dtype=jnp.int32)
-    chosen = coordinate[None, :] // RANK == token_adapter_index
-    lift = (jnp.arange(RANK, dtype=jnp.int32)[:, None] == coordinate[None, :] % RANK)
-    total = jnp.sum(exchange(sent, "head").astype(jnp.float32), axis=0)
-    low_rank = (total[tokens : tokens + RANK, :tokens] + total[tokens + RANK :, :tokens]).astype(
-        jnp.bfloat16
+    own_residual = lax.dynamic_slice_in_dim(residual, own_begin, own_width, 1)
+    own_mid, halves = middle(
+        core, token_adapter_index, own_residual, exchange(sent, "head"), mine, other
     )
-    lifted = lax.dot_general(
-        low_rank,
-        lift.astype(jnp.bfloat16),
-        (((0,), (0,)), ((), ())),
-        preferred_element_type=jnp.float32,
-    )
-    routed = jnp.where(chosen, lifted, 0.0).astype(jnp.bfloat16)
-    up_maps = unfold_map(late[:, 2 * units : 2 * units + own_width // 2], owners)
-    delta_own = (
-        adapter_scaling
-        * jnp.concatenate(
-            [jnp.dot(routed, part, preferred_element_type=jnp.float32) for part in up_maps], axis=1
-        )
-    ).astype(jnp.bfloat16)
-    own_mid = (
-        lax.dynamic_slice_in_dim(inputs, own_begin, own_width, 1)
-        + total[:tokens]
-        + delta_own.astype(jnp.float32)
-    )
-    mid_full = spread(own_mid.astype(jnp.bfloat16), "head").transpose(1, 0, 2).reshape(tokens, width)
-    ffn_in = (rms_scale(mid_full.astype(jnp.float32), 1e-06) * feedforward_norm_gain).astype(
-        jnp.bfloat16
-    )
-    both_acts = jnp.dot(ffn_in, late[:, : 2 * units], preferred_element_type=jnp.float32)
-    hidden_units = (jax.nn.silu(both_acts[:, :units]) * both_acts[:, units:]).astype(jnp.bfloat16)
-    piece = lax.dot_general(
-        hidden_units,
-        late[:, 2 * units + own_width // 2 :],
-        (((1,), (1,)), ((), ())),
-        preferred_element_type=jnp.float32,
-    ).astype(jnp.bfloat16)
-    piece = piece.reshape(tokens, groups, own_width).transpose(1, 0, 2)
-    return (own_mid + jnp.sum(exchange(piece, "head").astype(jnp.float32), axis=0)).astype(
-        jnp.bfloat16
-    )
+    mid_full = exchange(halves, "head")
+    piece = feed_forward(mid_full, feedforward_norm_gain, late, units)
+    pieces = exchange(piece, "head").reshape(groups // 2, tokens, own_width)
+    return (own_mid + jnp.sum(pieces.astype(jnp.float32), axis=0)).astype(jnp.bfloat16)
 
 
 def solution(mesh):

time: 183 us -> 180 us (0.984)
  blocking collectives: 109 us -> 93.9 us
  Pallas kernels: 5.89 us -> 14.2 us
  starting transfers between devices: 12.7 us -> 17.4 us
  local copies, waits for them, and re-layouts: 5.19 us -> 9.39 us
  matrix products: 3.42 us -> 0 us
    all_to_all x4, blocking collectives: 109 us -> 93.9 us  [exchange(): return lax.all_to_all(blocks, axis, split_axis=0, concat_axis=0, tiled=True)]
    pallas_call x0 -> x2, Pallas kernels: none -> 9.23 us  [the longest x1 7.45 us: feed_forward(): pl.pallas_call(feed_forward_kernel, out_shape=jax.ShapeDtypeStruct(mid.sh...]
    unnamed x15 -> x24, local copies, waits for them, and re-layouts: 1.25 us -> 6.7 us
    ppermute x0 -> x1, starting transfers between devices: none -> 4.03 us  [per_device(): lax.ppermute(acts_own, 'head', [(i, i ^ 1) for i in range(groups)])]
    dot_general x5 -> x0, matrix products: 3.42 us -> none  [the longest x1 1.45 us: per_device(): jnp.dot(ffn_in, late[:, :2 * units], preferred_element_type=jnp.float32)]
  transfers between devices with their start and end apart: 3 -> 4, of which waited for: 2 -> 2; matrix products, arithmetic and copies ran while one was open for 1% -> 3% of each run, Pallas kernels for 3% -> 4%
where the time goes in v6:
time: 180 us
  blocking collectives  93.9 us (52%)
  waiting for transfers between devices  29.1 us (16%)
  starting transfers between devices  17.4 us (10%)
  Pallas kernels  14.2 us (8%)
  between operations  14.2 us (8%)
  local copies, waits for them, and re-layouts  9.39 us (5%)
    all_to_all x4, blocking collectives, exchange(): return lax.all_to_all(blocks, axis, split_axis=0, concat_axis=0, tiled=True)  93.9 us
    all_to_all x1, waiting for transfers between devices, exchange(): return lax.all_to_all(blocks, axis, split_axis=0, concat_axis=0, tiled=True)  25.8 us
    pallas_call x1, Pallas kernels, feed_forward(): pl.pallas_call(feed_forward_kernel, out_shape=jax.ShapeDtypeStruct(mid.sh...  7.45 us
    all_to_all x1, starting transfers between devices, exchange(): return lax.all_to_all(blocks, axis, split_axis=0, concat_axis=0, tiled=True)  6.8 us
    unnamed x24, local copies, waits for them, and re-layouts  6.7 us
    ppermute x1, starting transfers between devices, sibling(): return lax.ppermute(block, 'core', [(0, 1), (1, 0)])  6.57 us
    pallas_call x1, Pallas kernels, attention(): pl.pallas_call(attention_kernel, out_shape=jax.ShapeDtypeStruct((groups,...  4.93 us
    ppermute x1, starting transfers between devices, per_device(): lax.ppermute(acts_own, 'head', [(i, i ^ 1) for i in range(groups)])  4.03 us
  transfers between devices with their start and end apart: 4, of which 2 were waited for; matrix products, arithmetic and copies ran while one was open for 3% of the time, Pallas kernels for 4%

profile of v6, /device:TPU:1, one launch (start us, length us, event | category | flops | bytes accessed | tf_op | source)
XLA Modules:
  0.0 179.6 jit_solution(15068702889787452949)
XLA Ops:
  6.5 0.0 copy-start
  6.5 0.0 all-gather.3.cloned.1.call-start
  6.5 1.0 concatenate.15
  7.5 4.0 %collective-permute-start = (bf16[32,2176]{1,0:T(8,128)(2,1)S(1)}, bf16[32,2176]{1,0:T(8,128)(2,1)S(1)}, u32[]{:S(2)}, u32[]{:S(2)}) collective-permute-start(bf16[32,2176]{1,0:T(8,128)(2,1)S(1)} %concatenate.15), channel_id=1, source_target_pairs={{0,64},{64,0},{128,192},{192,128},{256,320},{320,256},{384,448},{4... | collective-permute-start | bytes 417800 | tf_op jit(solution)/shard_map/ppermute | solution.py:367
  11.6 0.8 constant_dynamic-update-slice_fusion.4
  12.3 0.7 fusion.1
  13.1 0.0 copy-done
  13.1 0.7 constant_dynamic-update-slice_fusion.3
  13.8 0.7 constant_dynamic-update-slice_fusion.2
  14.5 0.0 collective-permute-done
  14.5 0.8 pad_maximum_fusion
  15.3 0.0 all-gather.3.cloned.1.call-update
  15.4 28.1 %all_to_all.25 = bf16[8,32,1280]{2,1,0:T(8,128)(2,1)S(1)} all-to-all(bf16[8,32,1280]{2,1,0:T(8,128)(2,1)S(1)} %broadcast_in_dim.7), channel_id=1, replica_groups=mesh['head'=8,'z'=8,'x'=4,'core'=2] {'z'}, dimensions={0} | all-to-all | bytes 1310720 | tf_op jit(solution)/shard_map/all_to_all | solution.py:323
  43.4 0.3 broadcast_in_dim.8
  43.7 0.0 copy-start.9
  43.7 0.0 copy-start.2
  43.7 0.0 copy-start.6
  43.8 0.0 copy-start.8
  43.8 33.6 %all_to_all.26.mine_ref = bf16[4,8,32,1280]{3,2,1,0:T(8,128)(2,1)S(1)} all-to-all(bf16[4,8,32,1280]{3,2,1,0:T(8,128)(2,1)S(1)} %broadcast_in_dim.8), channel_id=1, replica_groups=mesh['head'=8,'z'=8,'x'=4,'core'=2] {'x'}, dimensions={0} | all-to-all | bytes 5242880 | tf_op jit(solution)/shard_map/all_to_all | solution.py:323
  77.3 6.6 %collective-permute-start.1 = (bf16[4,8,32,1280]{3,2,1,0:T(8,128)(2,1)S(1)}, bf16[4,8,32,1280]{3,2,1,0:T(8,128)(2,1)}, u32[]{:S(2)}, u32[]{:S(2)}) collective-permute-start(bf16[4,8,32,1280]{3,2,1,0:T(8,128)(2,1)S(1)} %all_to_all.26.mine_ref), channel_id=1, source_target_pairs={{0,1},{1,0},{2,3},{3,2},{4,5},{5,4},{6,7},{7,6},{8,9},{9,8},{10,11... | collective-permute-start | bytes 7864328 | tf_op jit(solution)/shard_map/ppermute | solution.py:331
  83.9 0.0 copy-done.9
  83.9 0.8 copy.18.chosen_ref
  85.4 3.2 %collective-permute-done.1.other_ref = bf16[4,8,32,1280]{3,2,1,0:T(8,128)(2,1)} collective-permute-done((bf16[4,8,32,1280]{3,2,1,0:T(8,128)(2,1)S(1)}, bf16[4,8,32,1280]{3,2,1,0:T(8,128)(2,1)}, u32[]{:S(2)}, u32[]{:S(2)}) %collective-permute-start.1) | collective-permute-done | bytes 2621472 | tf_op jit(solution)/shard_map/ppermute | solution.py:331
  88.6 0.0 copy-done.2
  88.6 0.0 copy-done.6
  88.6 0.0 copy-done.8
  88.6 0.0 copy-start.3
  88.6 0.9 copy-done.3
  89.5 4.9 %shard_map.136 = bf16[8,224,256]{2,1,0:T(8,128)(2,1)S(1)} custom-call(s32[1,6]{1,0:T(1,128)S(1)} %copy-done.8, f32[1]{0:T(128)S(6)} %copy.23.lambda_ref, s32[1]{0:T(128)} %bitcast.core_ref, bf16[192,2048]{1,0:T(8,128)(2,1)S(1)} %copy-done.2, f32[1,2048]{1,0:T(1,128)S(1)} %bitcast.15, s32[192,1]{1,0:T(8,128)S(1)} %copy-done.3, ...), custom_call_target="tpu_custom_call" | custom-call | flops 1200000000 | bytes 8000000 | tf_op jit(solution)/shard_map/pallas_call | solution.py:137
  94.4 0.0 copy-start.1
  94.4 1.0 copy-done.1
  95.4 6.8 %all-to-all-start.2 = ((bf16[8,224,256]{2,1,0:T(8,128)(2,1)}), bf16[8,224,256]{2,1,0:T(8,128)(2,1)}, u32[]{:S(2)}, u32[]{:S(2)}) async-start(bf16[8,224,256]{2,1,0:T(8,128)(2,1)} %copy-done.1), calls=%async_computation.2 | async-start | bytes 1835008 | tf_op jit(solution)/shard_map/all_to_all | solution.py:323
  102.2 0.7 constant_dynamic-slice_fusion.residual_ref
  102.9 25.8 %all-to-all-done.2.received_ref = bf16[8,224,256]{2,1,0:T(8,128)(2,1)} async-done(((bf16[8,224,256]{2,1,0:T(8,128)(2,1)}), bf16[8,224,256]{2,1,0:T(8,128)(2,1)}, u32[]{:S(2)}, u32[]{:S(2)}) %all-to-all-start.2) | async-done | bytes 917536 | tf_op jit(solution)/shard_map/all_to_all | solution.py:323
  128.7 0.0 copy-start.4
  128.7 0.9 copy-done.4
  129.6 0.0 copy-start.5
  129.6 0.9 copy-done.5
  130.5 0.0 copy-start.7
  130.5 1.8 shard_map.137
  132.3 16.7 %all_to_all.27.mid_ref = bf16[8,96,256]{2,1,0:T(8,128)(2,1)S(1)} all-to-all(bf16[8,96,256]{2,1,0:T(8,128)(2,1)S(1)} %get-tuple-element.11), channel_id=1, replica_groups=mesh['head'=8,'z'=8,'x'=4,'core'=2] {'head'}, dimensions={0} | all-to-all | bytes 786432 | tf_op jit(solution)/shard_map/all_to_all | solution.py:323
  149.0 0.0 all-gather.3.cloned.1.call-done
  149.1 0.0 copy-done.7
  149.1 7.4 %shard_map.138 = bf16[8,96,256]{2,1,0:T(8,128)(2,1)S(1)} custom-call(bf16[8,96,256]{2,1,0:T(8,128)(2,1)S(1)} %all_to_all.27.mid_ref, f32[8,1,256]{2,1,0:T(1,128)S(1)} %bitcast.16, bf16[64,2,32,2176]{3,2,1,0:T(8,128)(2,1)} %bitcast.17), custom_call_target="tpu_custom_call" | custom-call | flops 1700000000 | bytes 18000000 | tf_op jit(solution)/shard_map/pallas_call | solution.py:304
  156.5 15.6 %all_to_all.28 = bf16[8,96,256]{2,1,0:T(8,128)(2,1)S(1)} all-to-all(bf16[8,96,256]{2,1,0:T(8,128)(2,1)S(1)} %shard_map.138), channel_id=1, replica_groups=mesh['head'=8,'z'=8,'x'=4,'core'=2] {'head'}, dimensions={0} | all-to-all | bytes 786432 | tf_op jit(solution)/shard_map/all_to_all | solution.py:323
  172.1 0.7 add_convert_fusion
  (7 shorter events, 0.1 us)
Async XLA Ops:
  6.5 6.5 %copy-start = (bf16[1,16,2048]{2,1,0:T(8,128)(2,1)S(1)}, bf16[1,16,2048]{2,1,0:T(8,128)(2,1)}, u32[]{:S(2)}) copy-start(bf16[1,16,2048]{2,1,0:T(8,128)(2,1)} %param.23) | copy-start | bytes 196612
  6.5 142.5 %all-gather.3.cloned.1.call-start = ((), (), s32[]{:S(2)}) async-start(), calls=%async_computation.5 | async-start | bytes 18104320 | tf_op jit(solution)/shard_map/all_gather | solution.py:369
  7.5 7.0 %collective-permute-start = (bf16[32,2176]{1,0:T(8,128)(2,1)S(1)}, bf16[32,2176]{1,0:T(8,128)(2,1)S(1)}, u32[]{:S(2)}, u32[]{:S(2)}) collective-permute-start(bf16[32,2176]{1,0:T(8,128)(2,1)S(1)} %concatenate.15), channel_id=1, source_target_pairs={{0,64},{64,0},{128,192},{192,128},{256,320},{320,256},{384,448},{4... | collective-permute-start | bytes 417800 | tf_op jit(solution)/shard_map/ppermute | solution.py:367
  43.7 40.2 %copy-start.9 = (s32[192,1]{0,1:T(1,128)S(1)}, s32[192,1]{0,1:T(1,128)}, u32[]{:S(2)}) copy-start(s32[192,1]{0,1:T(1,128)} %param.16) | copy-start | bytes 2308
  43.7 44.8 %copy-start.2 = (bf16[192,2048]{1,0:T(8,128)(2,1)S(1)}, bf16[192,2048]{1,0:T(8,128)(2,1)}, u32[]{:S(2)}) copy-start(bf16[192,2048]{1,0:T(8,128)(2,1)} %residual_ref.1) | copy-start | bytes 2359300
  43.7 44.8 %copy-start.6 = (f32[2048]{0:T(1024)S(1)}, f32[2048]{0:T(1024)}, u32[]{:S(2)}) copy-start(f32[2048]{0:T(1024)} %param.17) | copy-start | bytes 24580
  43.8 44.8 %copy-start.8 = (s32[1,6]{1,0:T(1,128)S(1)}, s32[1,6]{1,0:T(1,128)}, u32[]{:S(2)}) copy-start(s32[1,6]{1,0:T(1,128)} %lengths_ref.1) | copy-start | bytes 76
  77.3 11.2 %collective-permute-start.1 = (bf16[4,8,32,1280]{3,2,1,0:T(8,128)(2,1)S(1)}, bf16[4,8,32,1280]{3,2,1,0:T(8,128)(2,1)}, u32[]{:S(2)}, u32[]{:S(2)}) collective-permute-start(bf16[4,8,32,1280]{3,2,1,0:T(8,128)(2,1)S(1)} %all_to_all.26.mine_ref), channel_id=1, source_target_pairs={{0,1},{1,0},{2,3},{3,2},{4,5},{5,4},{6,7},{7,6},{8,9},{9,8},{10,11... | collective-permute-start | bytes 7864328 | tf_op jit(solution)/shard_map/ppermute | solution.py:331
  88.6 0.9 copy-start.3
  94.4 1.0 copy-start.1
  95.4 33.3 %all-to-all-start.2 = ((bf16[8,224,256]{2,1,0:T(8,128)(2,1)}), bf16[8,224,256]{2,1,0:T(8,128)(2,1)}, u32[]{:S(2)}, u32[]{:S(2)}) async-start(bf16[8,224,256]{2,1,0:T(8,128)(2,1)} %copy-done.1), calls=%async_computation.2 | async-start | bytes 1835008 | tf_op jit(solution)/shard_map/all_to_all | solution.py:323
  128.7 0.9 copy-start.4
  129.6 0.9 copy-start.5
  130.5 18.5 %copy-start.7 = (f32[2048]{0:T(1024)S(1)}, f32[2048]{0:T(1024)}, u32[]{:S(2)}) copy-start(f32[2048]{0:T(1024)} %param.24) | copy-start | bytes 24580
Sparse Core Ops, SparseCore 0:
  15.4 115.7 all-gather.2

commit v7 on v6

--- a/solution.py
+++ b/solution.py
@@ -37,8 +37,16 @@
     return raised / jnp.sum(raised, axis=-1, keepdims=True)
 
 
+def rank_lift(adapters):
+    shape = (RANK, adapters * RANK)
+    rank = lax.broadcasted_iota(jnp.int32, shape, 1) % RANK
+    return jnp.where(rank == lax.broadcasted_iota(jnp.int32, shape, 0), 1.0, 0.0).astype(
+        jnp.bfloat16
+    )
+
+
 def attention_kernel(
-    lengths_ref, lambda_ref, core_ref, residual_ref, gain_ref, chosen_ref, mine_ref, other_ref, sent_ref
+    lengths_ref, lambda_ref, place_ref, residual_ref, gain_ref, chosen_ref, mine_ref, other_ref, sent_ref
 ):
     slabs_x, slabs_z, rows, _ = mine_ref.shape
     tokens = residual_ref.shape[0]
@@ -91,45 +99,46 @@
         )
         head_out = (rms_scale(attended, 1e-05) * head_shrink).astype(jnp.bfloat16)
 
-        coordinates = jnp.zeros((tokens, adapters * RANK), jnp.float32)
+        room = jnp.zeros((value_width - tokens, value_width), jnp.bfloat16)
+        padded = jnp.concatenate([head_out, room], axis=0)
+        coordinates = jnp.zeros((adapters * RANK, value_width), jnp.float32)
         for half in range(2):
-            folded_rows = (half * RANK, (half + 1) * RANK)
             maps = jnp.concatenate(
-                [gather(z, out_end, out_end + HD, *folded_rows) for z in range(slabs_z)], axis=0
-            )
-            coordinates = coordinates + nt_dot(head_out[:, half * HD : (half + 1) * HD], maps)
-        owner = lax.broadcasted_iota(jnp.int32, coordinates.shape, 1) // RANK
+                [
+                    gather(z, out_end, out_end + HD, half * RANK, (half + 1) * RANK)
+                    for z in range(slabs_z)
+                ],
+                axis=0,
+            )
+            coordinates = coordinates + nt_dot(maps, padded[:, half * HD : (half + 1) * HD])
+        owner = lax.broadcasted_iota(jnp.int32, coordinates.shape, 0) // RANK
         kept = jnp.where(owner == chosen_ref[...], coordinates, 0.0)
-        room = jnp.zeros((value_width - tokens, adapters * RANK), jnp.float32)
-        kept = jnp.concatenate([kept, room], axis=0)
         high = kept.astype(jnp.bfloat16)
         low = (kept - high.astype(jnp.float32)).astype(jnp.bfloat16)
-        lift_shape = (RANK, adapters * RANK)
-        lift = jnp.where(
-            lax.broadcasted_iota(jnp.int32, lift_shape, 1) % RANK
-            == lax.broadcasted_iota(jnp.int32, lift_shape, 0),
-            1.0,
-            0.0,
+        lift = rank_lift(adapters)
+        low_rows = jnp.concatenate(
+            [
+                jnp.dot(lift, high, preferred_element_type=jnp.float32),
+                jnp.dot(lift, low, preferred_element_type=jnp.float32),
+            ],
+            axis=0,
         ).astype(jnp.bfloat16)
-        low_rows = jnp.concatenate([nt_dot(lift, high), nt_dot(lift, low)], axis=0).astype(
-            jnp.bfloat16
-        )
         for z in range(slabs_z):
             sent_ref[z, :tokens, :] = nt_dot(head_out, gather(z, qkv_width, out_end)).astype(
                 jnp.bfloat16
             )
             sent_ref[z, tokens:, :] = low_rows
 
-    @pl.when(core_ref[0] == 0)
+    @pl.when(place_ref[0] == 0)
     def _():
         body(mine_ref, other_ref)
 
-    @pl.when(core_ref[0] != 0)
+    @pl.when(place_ref[0] != 0)
     def _():
         body(other_ref, mine_ref)
 
 
-def attention(lengths, second_weight, core, residual, gain, chosen, mine, other):
+def attention(lengths, second_weight, place, residual, gain, chosen, mine, other):
     tokens = residual.shape[0]
     groups = mine.shape[1]
     smem = pl.BlockSpec(memory_space=pltpu.SMEM)
@@ -143,12 +152,12 @@
         cost_estimate=pl.CostEstimate(
             flops=1_200_000_000, bytes_accessed=8_000_000, transcendentals=80_000
         ),
-    )(lengths, second_weight, core, residual, gain.reshape(1, -1), chosen, mine, other)
-
-
-def middle_kernel(core_ref, chosen_ref, residual_ref, received_ref, mine_ref, other_ref, mid_ref, sent_ref):
+    )(lengths, second_weight, place, residual, gain.reshape(1, -1), chosen, mine, other)
+
+
+def middle_kernel(place_ref, chosen_ref, residual_ref, received_ref, mine_ref, other_ref, mid_ref, sent_ref):
     slabs_x, slabs_z, _, half_width = mine_ref.shape
-    tokens = chosen_ref.shape[0]
+    tokens = residual_ref.shape[0]
     part = tokens // 2
     adapters = 2 * slabs_x * slabs_z
 
@@ -157,17 +166,13 @@
         for group in range(1, received_ref.shape[0]):
             total = total + received_ref[group].astype(jnp.float32)
         low_rank = (total[tokens : tokens + RANK] + total[tokens + RANK :]).astype(jnp.bfloat16)
-        lift_shape = (RANK, adapters * RANK)
-        lift = jnp.where(
-            lax.broadcasted_iota(jnp.int32, lift_shape, 1) % RANK
-            == lax.broadcasted_iota(jnp.int32, lift_shape, 0),
-            1.0,
-            0.0,
-        ).astype(jnp.bfloat16)
         lifted = lax.dot_general(
-            low_rank, lift, (((0,), (0,)), ((), ())), preferred_element_type=jnp.float32
-        )[:tokens]
-        owner = lax.broadcasted_iota(jnp.int32, lifted.shape, 1) // RANK
+            rank_lift(adapters),
+            low_rank,
+            (((0,), (0,)), ((), ())),
+            preferred_element_type=jnp.float32,
+        )
+        owner = lax.broadcasted_iota(jnp.int32, lifted.shape, 0) // RANK
         routed = jnp.where(owner == chosen_ref[...], lifted, 0.0).astype(jnp.bfloat16)
         for half in range(2):
             maps = jnp.concatenate(
@@ -179,9 +184,10 @@
                 ],
                 axis=0,
             )
-            delta = (
-                adapter_scaling * jnp.dot(routed, maps, preferred_element_type=jnp.float32)
-            ).astype(jnp.bfloat16)
+            product = lax.dot_general(
+                routed, maps, (((0,), (0,)), ((), ())), preferred_element_type=jnp.float32
+            )
+            delta = (adapter_scaling * product[:tokens]).astype(jnp.bfloat16)
             lanes = slice(half * half_width, (half + 1) * half_width)
             mid = residual_ref[:, lanes].astype(jnp.float32) + total[:tokens, lanes]
             mid_ref[:, lanes] = mid + delta.astype(jnp.float32)
@@ -190,49 +196,49 @@
             side = group % 2
             sent_ref[group] = rounded[side * part : (side + 1) * part]
 
-    @pl.when(core_ref[0] == 0)
+    @pl.when(place_ref[0] == 0)
     def _():
         body(mine_ref, other_ref)
 
-    @pl.when(core_ref[0] != 0)
+    @pl.when(place_ref[0] != 0)
     def _():
         body(other_ref, mine_ref)
 
 
-def middle(core, chosen, residual, received, mine, other):
-    tokens, own_width = residual.shape
-    groups = received.shape[0]
+def middle(place, chosen, residual, received, mine, other):
+    tokens = residual.shape[0]
+    groups, _, own_width = received.shape
     last = mine.shape[3] // HD - 1
-    vmem = pl.BlockSpec(memory_space=pltpu.VMEM)
-    maps = pl.BlockSpec((*mine.shape[:3], HD), lambda i: (0, 0, 0, last))
-
-    def whole(array):
-        return pl.BlockSpec(array.shape, lambda i: (0,) * len(array.shape))
-
+    maps = pl.BlockSpec((*mine.shape[:3], HD), lambda i, place_ref: (0, 0, 0, last))
+
+    def whole(shape):
+        return pl.BlockSpec(shape, lambda i, place_ref: (0,) * len(shape))
+
+    mid_shape = (tokens, own_width)
+    sent_shape = (groups, tokens // 2, own_width)
     return pl.pallas_call(
         middle_kernel,
-        grid=(1,),
+        grid_spec=pltpu.PrefetchScalarGridSpec(
+            num_scalar_prefetch=1,
+            grid=(1,),
+            in_specs=[
+                whole(chosen.shape),
+                pl.BlockSpec(mid_shape, lambda i, place_ref: (0, place_ref[1])),
+                whole(received.shape),
+                maps,
+                maps,
+            ],
+            out_specs=[whole(mid_shape), whole(sent_shape)],
+        ),
         out_shape=[
-            jax.ShapeDtypeStruct((tokens, own_width), jnp.float32),
-            jax.ShapeDtypeStruct((groups, tokens // 2, own_width), jnp.bfloat16),
-        ],
-        in_specs=[
-            pl.BlockSpec(memory_space=pltpu.SMEM),
-            whole(chosen),
-            whole(residual),
-            whole(received),
-            maps,
-            maps,
-        ],
-        out_specs=[
-            pl.BlockSpec((tokens, own_width), lambda i: (0, 0)),
-            pl.BlockSpec((groups, tokens // 2, own_width), lambda i: (0, 0, 0)),
+            jax.ShapeDtypeStruct(mid_shape, jnp.float32),
+            jax.ShapeDtypeStruct(sent_shape, jnp.bfloat16),
         ],
         compiler_params=pltpu.CompilerParams(vmem_limit_bytes=32 * 1024 * 1024),
         cost_estimate=pl.CostEstimate(
             flops=120_000_000, bytes_accessed=3_000_000, transcendentals=0
         ),
-    )(core, chosen, residual, received, mine, other)
+    )(place, chosen, residual, received, mine, other)
 
 
 def feed_forward_kernel(mid_ref, gain_ref, weights_ref, out_ref, acts_ref, down_ref, acts_in, down_in):
@@ -369,22 +375,14 @@
     late = lax.all_gather(jnp.stack([acts_own, acts_pair]), BLK, axis=0, tiled=False)
     mine = spread(spread(early, "z"), "x")
     other = sibling(mine)
-    core = lax.axis_index("core").astype(jnp.int32).reshape(1)
+    place = jnp.stack([lax.axis_index("core"), lax.axis_index("head")]).astype(jnp.int32)
+    chosen = jnp.pad(
+        token_adapter_index.reshape(1, tokens), ((0, 0), (0, own_width - tokens)), constant_values=-1
+    )
     sent = attention(
-        lengths,
-        head_second_weight,
-        core,
-        residual,
-        attention_norm_gain,
-        token_adapter_index,
-        mine,
-        other,
+        lengths, head_second_weight, place, residual, attention_norm_gain, chosen, mine, other
     )
-
-    own_residual = lax.dynamic_slice_in_dim(residual, own_begin, own_width, 1)
-    own_mid, halves = middle(
-        core, token_adapter_index, own_residual, exchange(sent, "head"), mine, other
-    )
+    own_mid, halves = middle(place, chosen, residual, exchange(sent, "head"), mine, other)
     mid_full = exchange(halves, "head")
     piece = feed_forward(mid_full, feedforward_norm_gain, late, units)
     pieces = exchange(piece, "head").reshape(groups // 2, tokens, own_width)

time: 180 us -> 176 us (0.978); the launches traced: 180 us -> 173 us
  blocking collectives: 93.9 us -> 123 us
  waiting for transfers between devices: 29.1 us -> 3.92 us
  starting transfers between devices: 17.4 us -> 10.6 us
  local copies, waits for them, and re-layouts: 9.39 us -> 4.95 us
    all_to_all x4 -> x5, blocking collectives: 93.9 us -> 123 us  [exchange(): return lax.all_to_all(blocks, axis, split_axis=0, concat_axis=0, tiled=True)]
    all_to_all x1 -> x0, waiting for transfers between devices: 25.8 us -> none  [exchange(): return lax.all_to_all(blocks, axis, split_axis=0, concat_axis=0, tiled=True)]
    all_to_all x1 -> x0, starting transfers between devices: 6.8 us -> none  [exchange(): return lax.all_to_all(blocks, axis, split_axis=0, concat_axis=0, tiled=True)]
    unnamed x24 -> x19, local copies, waits for them, and re-layouts: 6.7 us -> 2.91 us
  transfers between devices with their start and end apart: 4 -> 3, of which waited for: 2 -> 1; matrix products, arithmetic and copies ran while one was open for 3% -> 2% of each run, Pallas kernels for 4% -> 5%
where the time goes in v7:
time: 176 us; the launch traced here: 173 us
  blocking collectives  123 us (70%)
  Pallas kernels  15.3 us (9%)
  between operations  14.2 us (8%)
  starting transfers between devices  10.6 us (6%)
  local copies, waits for them, and re-layouts  4.95 us (3%)
  waiting for transfers between devices  3.92 us (2%)
    all_to_all x5, blocking collectives, exchange(): return lax.all_to_all(blocks, axis, split_axis=0, concat_axis=0, tiled=True)  123 us
    pallas_call x1, Pallas kernels, feed_forward(): pl.pallas_call(feed_forward_kernel, out_shape=jax.ShapeDtypeStruct(mid.sh...  7.5 us
    ppermute x1, starting transfers between devices, sibling(): return lax.ppermute(block, 'core', [(0, 1), (1, 0)])  6.57 us
    pallas_call x1, Pallas kernels, attention(): pl.pallas_call(attention_kernel, out_shape=jax.ShapeDtypeStruct((groups,...  5.36 us
    ppermute x1, starting transfers between devices, per_device(): lax.ppermute(acts_own, 'head', [(i, i ^ 1) for i in range(groups)])  4.03 us
    ppermute x1, waiting for transfers between devices, sibling(): return lax.ppermute(block, 'core', [(0, 1), (1, 0)])  3.9 us
  transfers between devices with their start and end apart: 3, of which 1 were waited for; matrix products, arithmetic and copies ran while one was open for 2% of the time, Pallas kernels for 5%

profile of v7, /device:TPU:1, one launch (start us, length us, event | category | flops | bytes accessed | tf_op | source)
XLA Modules:
  0.0 173.2 jit_solution(11718845641719705190)
XLA Ops:
  6.5 0.0 copy-start
  6.5 0.0 all-gather.3.cloned.1.call-start
  6.5 1.0 concatenate.15
  7.5 4.0 %collective-permute-start = (bf16[32,2176]{1,0:T(8,128)(2,1)S(1)}, bf16[32,2176]{1,0:T(8,128)(2,1)S(1)}, u32[]{:S(2)}, u32[]{:S(2)}) collective-permute-start(bf16[32,2176]{1,0:T(8,128)(2,1)S(1)} %concatenate.15), channel_id=1, source_target_pairs={{0,64},{64,0},{128,192},{192,128},{256,320},{320,256},{384,448},{4... | collective-permute-start | bytes 417800 | tf_op jit(solution)/shard_map/ppermute | solution.py:373
  11.6 0.8 constant_dynamic-update-slice_fusion.4
  12.3 0.7 fusion.1
  13.1 0.0 copy-done
  13.1 0.7 constant_dynamic-update-slice_fusion.3
  13.8 0.7 constant_dynamic-update-slice_fusion.2
  14.5 0.0 collective-permute-done
  14.5 0.8 pad_maximum_fusion
  15.3 0.0 all-gather.3.cloned.1.call-update
  15.4 28.1 %all_to_all.25 = bf16[8,32,1280]{2,1,0:T(8,128)(2,1)S(1)} all-to-all(bf16[8,32,1280]{2,1,0:T(8,128)(2,1)S(1)} %broadcast_in_dim.7), channel_id=1, replica_groups=mesh['head'=8,'z'=8,'x'=4,'core'=2] {'z'}, dimensions={0} | all-to-all | bytes 1310720 | tf_op jit(solution)/shard_map/all_to_all | solution.py:329
  43.4 0.3 broadcast_in_dim.8
  43.7 0.0 copy-start.7
  43.7 0.0 copy-start.1
  43.7 0.0 copy-start.4
  43.8 0.0 copy-start.6
  43.8 33.6 %all_to_all.26.mine_ref = bf16[4,8,32,1280]{3,2,1,0:T(8,128)(2,1)S(1)} all-to-all(bf16[4,8,32,1280]{3,2,1,0:T(8,128)(2,1)S(1)} %broadcast_in_dim.8), channel_id=1, replica_groups=mesh['head'=8,'z'=8,'x'=4,'core'=2] {'x'}, dimensions={0} | all-to-all | bytes 5242880 | tf_op jit(solution)/shard_map/all_to_all | solution.py:329
  77.3 6.6 %collective-permute-start.1 = (bf16[4,8,32,1280]{3,2,1,0:T(8,128)(2,1)S(1)}, bf16[4,8,32,1280]{3,2,1,0:T(8,128)(2,1)}, u32[]{:S(2)}, u32[]{:S(2)}) collective-permute-start(bf16[4,8,32,1280]{3,2,1,0:T(8,128)(2,1)S(1)} %all_to_all.26.mine_ref), channel_id=1, source_target_pairs={{0,1},{1,0},{2,3},{3,2},{4,5},{5,4},{6,7},{7,6},{8,9},{9,8},{10,11... | collective-permute-start | bytes 7864328 | tf_op jit(solution)/shard_map/ppermute | solution.py:337
  84.6 0.0 copy-done.7
  84.6 0.1 pad_add_fusion.place_ref
  84.7 3.9 %collective-permute-done.1.other_ref = bf16[4,8,32,1280]{3,2,1,0:T(8,128)(2,1)} collective-permute-done((bf16[4,8,32,1280]{3,2,1,0:T(8,128)(2,1)S(1)}, bf16[4,8,32,1280]{3,2,1,0:T(8,128)(2,1)}, u32[]{:S(2)}, u32[]{:S(2)}) %collective-permute-start.1) | collective-permute-done | bytes 2621472 | tf_op jit(solution)/shard_map/ppermute | solution.py:337
  88.6 0.0 copy-done.1
  88.6 0.0 copy-done.4
  88.6 0.0 copy-done.6
  88.6 5.4 %shard_map.136 = bf16[8,224,256]{2,1,0:T(8,128)(2,1)S(1)} custom-call(s32[1,6]{1,0:T(1,128)S(1)} %copy-done.6, f32[1]{0:T(128)S(6)} %copy.19.lambda_ref, s32[2]{0:T(128)S(1)} %pad_add_fusion.place_ref, bf16[192,2048]{1,0:T(8,128)(2,1)S(1)} %copy-done.1, f32[1,2048]{1,0:T(1,128)S(1)} %bitcast.17, s32[1,256]{1,0:T(1,128)S(1)} %pad.4.chosen_ref, ...), custom_call_target="tpu_custom_call" | custom-call | flops 1200000000 | bytes 8000000 | tf_op jit(solution)/shard_map/pallas_call | solution.py:146
  93.9 31.4 %all_to_all.27.received_ref = bf16[8,224,256]{2,1,0:T(8,128)(2,1)S(1)} all-to-all(bf16[8,224,256]{2,1,0:T(8,128)(2,1)S(1)} %shard_map.136), channel_id=1, replica_groups=mesh['head'=8,'z'=8,'x'=4,'core'=2] {'head'}, dimensions={0} | all-to-all | bytes 1835008 | tf_op jit(solution)/shard_map/all_to_all | solution.py:329
  125.4 0.0 copy-start.5
  125.4 2.5 %shard_map.137 = (f32[192,256]{1,0:T(8,128)S(1)}, bf16[8,96,256]{2,1,0:T(8,128)(2,1)S(1)}) custom-call(s32[2]{0:T(128)S(1)} %pad_add_fusion.place_ref, s32[1,256]{1,0:T(1,128)S(1)} %pad.4.chosen_ref, bf16[192,2048]{1,0:T(8,128)(2,1)S(1)} %copy-done.1, bf16[8,224,256]{2,1,0:T(8,128)(2,1)S(1)} %all_to_all.27.received_ref, ...), custom_call_target="tpu_custom_call" | custom-call | flops 120000000 | bytes 3000000 | tf_op jit(solution)/shard_map/pallas_call | solution.py:219
  127.9 0.0 copy-start.2
  127.9 0.7 copy-done.2
  128.5 14.7 %all_to_all.28.mid_ref = bf16[8,96,256]{2,1,0:T(8,128)(2,1)S(1)} all-to-all(bf16[8,96,256]{2,1,0:T(8,128)(2,1)S(1)} %get-tuple-element.11), channel_id=1, replica_groups=mesh['head'=8,'z'=8,'x'=4,'core'=2] {'head'}, dimensions={0} | all-to-all | bytes 786432 | tf_op jit(solution)/shard_map/all_to_all | solution.py:329
  143.2 0.0 all-gather.3.cloned.1.call-done
  143.2 0.0 copy-done.5
  143.2 0.0 copy-start.3
  143.2 7.5 %shard_map.138 = bf16[8,96,256]{2,1,0:T(8,128)(2,1)S(1)} custom-call(bf16[8,96,256]{2,1,0:T(8,128)(2,1)S(1)} %all_to_all.28.mid_ref, f32[8,1,256]{2,1,0:T(1,128)S(1)} %bitcast.18, bf16[64,2,32,2176]{3,2,1,0:T(8,128)(2,1)} %bitcast.19), custom_call_target="tpu_custom_call" | custom-call | flops 1700000000 | bytes 18000000 | tf_op jit(solution)/shard_map/pallas_call | solution.py:310
  150.7 15.0 %all_to_all.29 = bf16[8,96,256]{2,1,0:T(8,128)(2,1)S(1)} all-to-all(bf16[8,96,256]{2,1,0:T(8,128)(2,1)S(1)} %shard_map.138), channel_id=1, replica_groups=mesh['head'=8,'z'=8,'x'=4,'core'=2] {'head'}, dimensions={0} | all-to-all | bytes 786432 | tf_op jit(solution)/shard_map/all_to_all | solution.py:329
  165.7 0.0 copy-done.3
  165.7 0.7 add_convert_fusion
  (8 shorter events, 0.1 us)
Async XLA Ops:
  6.5 6.5 %copy-start = (bf16[1,16,2048]{2,1,0:T(8,128)(2,1)S(1)}, bf16[1,16,2048]{2,1,0:T(8,128)(2,1)}, u32[]{:S(2)}) copy-start(bf16[1,16,2048]{2,1,0:T(8,128)(2,1)} %param.23) | copy-start | bytes 196612
  6.5 136.7 %all-gather.3.cloned.1.call-start = ((), (), s32[]{:S(2)}) async-start(), calls=%async_computation.5 | async-start | bytes 18104320 | tf_op jit(solution)/shard_map/all_gather | solution.py:375
  7.5 7.0 %collective-permute-start = (bf16[32,2176]{1,0:T(8,128)(2,1)S(1)}, bf16[32,2176]{1,0:T(8,128)(2,1)S(1)}, u32[]{:S(2)}, u32[]{:S(2)}) collective-permute-start(bf16[32,2176]{1,0:T(8,128)(2,1)S(1)} %concatenate.15), channel_id=1, source_target_pairs={{0,64},{64,0},{128,192},{192,128},{256,320},{320,256},{384,448},{4... | collective-permute-start | bytes 417800 | tf_op jit(solution)/shard_map/ppermute | solution.py:373
  43.7 40.9 %copy-start.7 = (s32[192,1]{0,1:T(1,128)S(1)}, s32[192,1]{0,1:T(1,128)}, u32[]{:S(2)}) copy-start(s32[192,1]{0,1:T(1,128)} %param.16) | copy-start | bytes 2308
  43.7 44.8 %copy-start.1 = (bf16[192,2048]{1,0:T(8,128)(2,1)S(1)}, bf16[192,2048]{1,0:T(8,128)(2,1)}, u32[]{:S(2)}) copy-start(bf16[192,2048]{1,0:T(8,128)(2,1)} %residual_ref.3) | copy-start | bytes 2359300
  43.7 44.8 %copy-start.4 = (f32[2048]{0:T(1024)S(1)}, f32[2048]{0:T(1024)}, u32[]{:S(2)}) copy-start(f32[2048]{0:T(1024)} %param.17) | copy-start | bytes 24580
  43.8 44.8 %copy-start.6 = (s32[1,6]{1,0:T(1,128)S(1)}, s32[1,6]{1,0:T(1,128)}, u32[]{:S(2)}) copy-start(s32[1,6]{1,0:T(1,128)} %lengths_ref.1) | copy-start | bytes 76
  77.3 11.2 %collective-permute-start.1 = (bf16[4,8,32,1280]{3,2,1,0:T(8,128)(2,1)S(1)}, bf16[4,8,32,1280]{3,2,1,0:T(8,128)(2,1)}, u32[]{:S(2)}, u32[]{:S(2)}) collective-permute-start(bf16[4,8,32,1280]{3,2,1,0:T(8,128)(2,1)S(1)} %all_to_all.26.mine_ref), channel_id=1, source_target_pairs={{0,1},{1,0},{2,3},{3,2},{4,5},{5,4},{6,7},{7,6},{8,9},{9,8},{10,11... | collective-permute-start | bytes 7864328 | tf_op jit(solution)/shard_map/ppermute | solution.py:337
  125.4 17.8 %copy-start.5 = (f32[2048]{0:T(1024)S(1)}, f32[2048]{0:T(1024)}, u32[]{:S(2)}) copy-start(f32[2048]{0:T(1024)} %param.24) | copy-start | bytes 24580
  127.9 0.7 copy-start.2
  143.2 22.5 %copy-start.3 = (f32[192,256]{1,0:T(8,128)S(1)}, f32[192,256]{1,0:T(8,128)}, u32[]{:S(2)}) copy-start(f32[192,256]{1,0:T(8,128)} %copy-done.2) | copy-start | bytes 589828
Sparse Core Ops, SparseCore 0:
  15.4 115.9 all-gather.2

commit v8 on v7

--- a/solution.py
+++ b/solution.py
@@ -46,7 +46,17 @@
 
 
 def attention_kernel(
-    lengths_ref, lambda_ref, place_ref, residual_ref, gain_ref, chosen_ref, mine_ref, other_ref, sent_ref
+    lengths_ref,
+    lambda_ref,
+    place_ref,
+    residual_ref,
+    gain_ref,
+    chosen_ref,
+    mine_ref,
+    sibling_ref,
+    sent_ref,
+    other_ref,
+    arrived,
 ):
     slabs_x, slabs_z, rows, _ = mine_ref.shape
     tokens = residual_ref.shape[0]
@@ -54,6 +64,17 @@
     qkv_width = 4 * HD + value_width
     out_end = qkv_width + value_width
     adapters = 2 * slabs_x * slabs_z
+    copies = [
+        pltpu.make_async_copy(sibling_ref.at[x], other_ref.at[x], arrived.at[x])
+        for x in range(slabs_x)
+    ]
+    for copy in copies:
+        copy.start()
+    normed = (rms_scale(residual_ref[...].astype(jnp.float32), 1e-06) * gain_ref[...]).astype(
+        jnp.bfloat16
+    )
+    for copy in copies:
+        copy.wait()
 
     def body(even_ref, odd_ref):
         def gather(z, begin, end, first_row=0, last_row=rows):
@@ -67,9 +88,6 @@
             )
 
         slab = 2 * slabs_x * rows
-        normed = (rms_scale(residual_ref[...].astype(jnp.float32), 1e-06) * gain_ref[...]).astype(
-            jnp.bfloat16
-        )
         qkv = jnp.zeros((tokens, qkv_width), jnp.float32)
         for z in range(slabs_z):
             qkv = qkv + jnp.dot(
@@ -113,15 +131,8 @@
             coordinates = coordinates + nt_dot(maps, padded[:, half * HD : (half + 1) * HD])
         owner = lax.broadcasted_iota(jnp.int32, coordinates.shape, 0) // RANK
         kept = jnp.where(owner == chosen_ref[...], coordinates, 0.0)
-        high = kept.astype(jnp.bfloat16)
-        low = (kept - high.astype(jnp.float32)).astype(jnp.bfloat16)
-        lift = rank_lift(adapters)
-        low_rows = jnp.concatenate(
-            [
-                jnp.dot(lift, high, preferred_element_type=jnp.float32),
-                jnp.dot(lift, low, preferred_element_type=jnp.float32),
-            ],
-            axis=0,
+        low_rows = jnp.dot(
+            rank_lift(adapters), kept.astype(jnp.bfloat16), preferred_element_type=jnp.float32
         ).astype(jnp.bfloat16)
         for z in range(slabs_z):
             sent_ref[z, :tokens, :] = nt_dot(head_out, gather(z, qkv_width, out_end)).astype(
@@ -145,9 +156,13 @@
     vmem = pl.BlockSpec(memory_space=pltpu.VMEM)
     return pl.pallas_call(
         attention_kernel,
-        out_shape=jax.ShapeDtypeStruct((groups, tokens + 2 * RANK, 2 * HD), jnp.bfloat16),
-        in_specs=[smem] * 3 + [vmem] * 5,
+        out_shape=jax.ShapeDtypeStruct((groups, tokens + RANK, 2 * HD), jnp.bfloat16),
+        in_specs=[smem] * 3 + [vmem] * 4 + [pl.BlockSpec(memory_space=pl.ANY)],
         out_specs=vmem,
+        scratch_shapes=[
+            pltpu.VMEM(other.shape, other.dtype),
+            pltpu.SemaphoreType.DMA((mine.shape[0],)),
+        ],
         compiler_params=pltpu.CompilerParams(vmem_limit_bytes=48 * 1024 * 1024),
         cost_estimate=pl.CostEstimate(
             flops=1_200_000_000, bytes_accessed=8_000_000, transcendentals=80_000
@@ -165,7 +180,7 @@
         total = received_ref[0].astype(jnp.float32)
         for group in range(1, received_ref.shape[0]):
             total = total + received_ref[group].astype(jnp.float32)
-        low_rank = (total[tokens : tokens + RANK] + total[tokens + RANK :]).astype(jnp.bfloat16)
+        low_rank = total[tokens:].astype(jnp.bfloat16)
         lifted = lax.dot_general(
             rank_lift(adapters),
             low_rank,

time: 176 us -> 175 us (level)
  no operation moved by 1% of the time
where the time goes in v8:
time: 175 us; the launch traced here: 172 us
  blocking collectives  122 us (70%)
  Pallas kernels  15.5 us (9%)
  between operations  14.2 us (8%)
  starting transfers between devices  10.6 us (6%)
  local copies, waits for them, and re-layouts  4.95 us (3%)
  waiting for transfers between devices  3.92 us (2%)
    all_to_all x5, blocking collectives, exchange(): return lax.all_to_all(blocks, axis, split_axis=0, concat_axis=0, tiled=True)  122 us
    pallas_call x1, Pallas kernels, feed_forward(): pl.pallas_call(feed_forward_kernel, out_shape=jax.ShapeDtypeStruct(mid.sh...  7.5 us
    ppermute x1, starting transfers between devices, sibling(): return lax.ppermute(block, 'core', [(0, 1), (1, 0)])  6.57 us
    pallas_call x1, Pallas kernels, attention(): pl.pallas_call(attention_kernel, out_shape=jax.ShapeDtypeStruct((groups,...  5.58 us
    ppermute x1, starting transfers between devices, per_device(): lax.ppermute(acts_own, 'head', [(i, i ^ 1) for i in range(groups)])  4.03 us
    ppermute x1, waiting for transfers between devices, sibling(): return lax.ppermute(block, 'core', [(0, 1), (1, 0)])  3.9 us
  transfers between devices with their start and end apart: 3, of which 1 were waited for; matrix products, arithmetic and copies ran while one was open for 2% of the time, Pallas kernels for 5%

profile of v8, /device:TPU:1, one launch (start us, length us, event | category | flops | bytes accessed | tf_op | source)
XLA Modules:
  0.0 172.4 jit_solution(11346266849547175115)
XLA Ops:
  6.5 0.0 copy-start
  6.5 0.0 all-gather.3.cloned.1.call-start
  6.5 1.0 concatenate.15
  7.5 4.0 %collective-permute-start = (bf16[32,2176]{1,0:T(8,128)(2,1)S(1)}, bf16[32,2176]{1,0:T(8,128)(2,1)S(1)}, u32[]{:S(2)}, u32[]{:S(2)}) collective-permute-start(bf16[32,2176]{1,0:T(8,128)(2,1)S(1)} %concatenate.15), channel_id=1, source_target_pairs={{0,64},{64,0},{128,192},{192,128},{256,320},{320,256},{384,448},{4... | collective-permute-start | bytes 417800 | tf_op jit(solution)/shard_map/ppermute | solution.py:388
  11.6 0.8 constant_dynamic-update-slice_fusion.4
  12.3 0.7 fusion.1
  13.1 0.0 copy-done
  13.1 0.7 constant_dynamic-update-slice_fusion.3
  13.8 0.7 constant_dynamic-update-slice_fusion.2
  14.5 0.0 collective-permute-done
  14.5 0.8 pad_maximum_fusion
  15.3 0.0 all-gather.3.cloned.1.call-update
  15.4 28.1 %all_to_all.25 = bf16[8,32,1280]{2,1,0:T(8,128)(2,1)S(1)} all-to-all(bf16[8,32,1280]{2,1,0:T(8,128)(2,1)S(1)} %broadcast_in_dim.7), channel_id=1, replica_groups=mesh['head'=8,'z'=8,'x'=4,'core'=2] {'z'}, dimensions={0} | all-to-all | bytes 1310720 | tf_op jit(solution)/shard_map/all_to_all | solution.py:344
  43.4 0.3 broadcast_in_dim.8
  43.7 0.0 copy-start.7
  43.7 0.0 copy-start.1
  43.7 0.0 copy-start.4
  43.8 0.0 copy-start.6
  43.8 33.6 %all_to_all.26.mine_ref = bf16[4,8,32,1280]{3,2,1,0:T(8,128)(2,1)S(1)} all-to-all(bf16[4,8,32,1280]{3,2,1,0:T(8,128)(2,1)S(1)} %broadcast_in_dim.8), channel_id=1, replica_groups=mesh['head'=8,'z'=8,'x'=4,'core'=2] {'x'}, dimensions={0} | all-to-all | bytes 5242880 | tf_op jit(solution)/shard_map/all_to_all | solution.py:344
  77.3 6.6 %collective-permute-start.1 = (bf16[4,8,32,1280]{3,2,1,0:T(8,128)(2,1)S(1)}, bf16[4,8,32,1280]{3,2,1,0:T(8,128)(2,1)}, u32[]{:S(2)}, u32[]{:S(2)}) collective-permute-start(bf16[4,8,32,1280]{3,2,1,0:T(8,128)(2,1)S(1)} %all_to_all.26.mine_ref), channel_id=1, source_target_pairs={{0,1},{1,0},{2,3},{3,2},{4,5},{5,4},{6,7},{7,6},{8,9},{9,8},{10,11... | collective-permute-start | bytes 7864328 | tf_op jit(solution)/shard_map/ppermute | solution.py:352
  84.6 0.0 copy-done.7
  84.6 0.1 pad_add_fusion.place_ref
  84.7 3.9 %collective-permute-done.1.sibling_ref.other_ref = bf16[4,8,32,1280]{3,2,1,0:T(8,128)(2,1)} collective-permute-done((bf16[4,8,32,1280]{3,2,1,0:T(8,128)(2,1)S(1)}, bf16[4,8,32,1280]{3,2,1,0:T(8,128)(2,1)}, u32[]{:S(2)}, u32[]{:S(2)}) %collective-permute-start.1) | collective-permute-done | bytes 2621472 | tf_op jit(solution)/shard_map/ppermute | solution.py:352
  88.6 0.0 copy-done.1
  88.6 0.0 copy-done.4
  88.6 0.0 copy-done.6
  88.6 5.6 %shard_map.136 = bf16[8,208,256]{2,1,0:T(8,128)(2,1)S(1)} custom-call(s32[1,6]{1,0:T(1,128)S(1)} %copy-done.6, f32[1]{0:T(128)S(6)} %copy.19.lambda_ref, s32[2]{0:T(128)S(1)} %pad_add_fusion.place_ref, bf16[192,2048]{1,0:T(8,128)(2,1)S(1)} %copy-done.1, f32[1,2048]{1,0:T(1,128)S(1)} %bitcast.17, s32[1,256]{1,0:T(1,128)S(1)} %pad.4.chosen_ref, ...), custom_call_target="tpu_custom_call" | custom-call | flops 1200000000 | bytes 8000000 | tf_op jit(solution)/shard_map/pallas_call | solution.py:157
  94.2 30.6 %all_to_all.27.received_ref = bf16[8,208,256]{2,1,0:T(8,128)(2,1)S(1)} all-to-all(bf16[8,208,256]{2,1,0:T(8,128)(2,1)S(1)} %shard_map.136), channel_id=1, replica_groups=mesh['head'=8,'z'=8,'x'=4,'core'=2] {'head'}, dimensions={0} | all-to-all | bytes 1703936 | tf_op jit(solution)/shard_map/all_to_all | solution.py:344
  124.7 0.0 copy-start.5
  124.7 2.4 %shard_map.137 = (f32[192,256]{1,0:T(8,128)S(1)}, bf16[8,96,256]{2,1,0:T(8,128)(2,1)S(1)}) custom-call(s32[2]{0:T(128)S(1)} %pad_add_fusion.place_ref, s32[1,256]{1,0:T(1,128)S(1)} %pad.4.chosen_ref, bf16[192,2048]{1,0:T(8,128)(2,1)S(1)} %copy-done.1, bf16[8,208,256]{2,1,0:T(8,128)(2,1)S(1)} %all_to_all.27.received_ref, ...), custom_call_target="tpu_custom_call" | custom-call | flops 120000000 | bytes 3000000 | tf_op jit(solution)/shard_map/pallas_call | solution.py:234
  127.1 0.0 copy-start.2
  127.1 0.7 copy-done.2
  127.8 15.4 %all_to_all.28.mid_ref = bf16[8,96,256]{2,1,0:T(8,128)(2,1)S(1)} all-to-all(bf16[8,96,256]{2,1,0:T(8,128)(2,1)S(1)} %get-tuple-element.11), channel_id=1, replica_groups=mesh['head'=8,'z'=8,'x'=4,'core'=2] {'head'}, dimensions={0} | all-to-all | bytes 786432 | tf_op jit(solution)/shard_map/all_to_all | solution.py:344
  143.2 0.0 all-gather.3.cloned.1.call-done
  143.2 0.0 copy-done.5
  143.2 0.0 copy-start.3
  143.2 7.5 %shard_map.138 = bf16[8,96,256]{2,1,0:T(8,128)(2,1)S(1)} custom-call(bf16[8,96,256]{2,1,0:T(8,128)(2,1)S(1)} %all_to_all.28.mid_ref, f32[8,1,256]{2,1,0:T(1,128)S(1)} %bitcast.18, bf16[64,2,32,2176]{3,2,1,0:T(8,128)(2,1)} %bitcast.19), custom_call_target="tpu_custom_call" | custom-call | flops 1700000000 | bytes 18000000 | tf_op jit(solution)/shard_map/pallas_call | solution.py:325
  150.7 14.1 %all_to_all.29 = bf16[8,96,256]{2,1,0:T(8,128)(2,1)S(1)} all-to-all(bf16[8,96,256]{2,1,0:T(8,128)(2,1)S(1)} %shard_map.138), channel_id=1, replica_groups=mesh['head'=8,'z'=8,'x'=4,'core'=2] {'head'}, dimensions={0} | all-to-all | bytes 786432 | tf_op jit(solution)/shard_map/all_to_all | solution.py:344
  164.8 0.0 copy-done.3
  164.8 0.7 add_convert_fusion
  (8 shorter events, 0.1 us)
Async XLA Ops:
  6.5 6.5 %copy-start = (bf16[1,16,2048]{2,1,0:T(8,128)(2,1)S(1)}, bf16[1,16,2048]{2,1,0:T(8,128)(2,1)}, u32[]{:S(2)}) copy-start(bf16[1,16,2048]{2,1,0:T(8,128)(2,1)} %param.23) | copy-start | bytes 196612
  6.5 136.7 %all-gather.3.cloned.1.call-start = ((), (), s32[]{:S(2)}) async-start(), calls=%async_computation.5 | async-start | bytes 18104320 | tf_op jit(solution)/shard_map/all_gather | solution.py:390
  7.5 7.0 %collective-permute-start = (bf16[32,2176]{1,0:T(8,128)(2,1)S(1)}, bf16[32,2176]{1,0:T(8,128)(2,1)S(1)}, u32[]{:S(2)}, u32[]{:S(2)}) collective-permute-start(bf16[32,2176]{1,0:T(8,128)(2,1)S(1)} %concatenate.15), channel_id=1, source_target_pairs={{0,64},{64,0},{128,192},{192,128},{256,320},{320,256},{384,448},{4... | collective-permute-start | bytes 417800 | tf_op jit(solution)/shard_map/ppermute | solution.py:388
  43.7 40.9 %copy-start.7 = (s32[192,1]{0,1:T(1,128)S(1)}, s32[192,1]{0,1:T(1,128)}, u32[]{:S(2)}) copy-start(s32[192,1]{0,1:T(1,128)} %param.16) | copy-start | bytes 2308
  43.7 44.8 %copy-start.1 = (bf16[192,2048]{1,0:T(8,128)(2,1)S(1)}, bf16[192,2048]{1,0:T(8,128)(2,1)}, u32[]{:S(2)}) copy-start(bf16[192,2048]{1,0:T(8,128)(2,1)} %residual_ref.3) | copy-start | bytes 2359300
  43.7 44.8 %copy-start.4 = (f32[2048]{0:T(1024)S(1)}, f32[2048]{0:T(1024)}, u32[]{:S(2)}) copy-start(f32[2048]{0:T(1024)} %param.17) | copy-start | bytes 24580
  43.8 44.8 %copy-start.6 = (s32[1,6]{1,0:T(1,128)S(1)}, s32[1,6]{1,0:T(1,128)}, u32[]{:S(2)}) copy-start(s32[1,6]{1,0:T(1,128)} %lengths_ref.1) | copy-start | bytes 76
  77.3 11.2 %collective-permute-start.1 = (bf16[4,8,32,1280]{3,2,1,0:T(8,128)(2,1)S(1)}, bf16[4,8,32,1280]{3,2,1,0:T(8,128)(2,1)}, u32[]{:S(2)}, u32[]{:S(2)}) collective-permute-start(bf16[4,8,32,1280]{3,2,1,0:T(8,128)(2,1)S(1)} %all_to_all.26.mine_ref), channel_id=1, source_target_pairs={{0,1},{1,0},{2,3},{3,2},{4,5},{5,4},{6,7},{7,6},{8,9},{9,8},{10,11... | collective-permute-start | bytes 7864328 | tf_op jit(solution)/shard_map/ppermute | solution.py:352
  124.7 18.5 %copy-start.5 = (f32[2048]{0:T(1024)S(1)}, f32[2048]{0:T(1024)}, u32[]{:S(2)}) copy-start(f32[2048]{0:T(1024)} %param.24) | copy-start | bytes 24580
  127.1 0.7 copy-start.2
  143.2 21.6 %copy-start.3 = (f32[192,256]{1,0:T(8,128)S(1)}, f32[192,256]{1,0:T(8,128)}, u32[]{:S(2)}) copy-start(f32[192,256]{1,0:T(8,128)} %copy-done.2) | copy-start | bytes 589828
Sparse Core Ops, SparseCore 0:
  15.4 115.9 all-gather.2

commit v9 on v8

--- a/solution.py
+++ b/solution.py
@@ -53,10 +53,8 @@
     gain_ref,
     chosen_ref,
     mine_ref,
-    sibling_ref,
+    other_ref,
     sent_ref,
-    other_ref,
-    arrived,
 ):
     slabs_x, slabs_z, rows, _ = mine_ref.shape
     tokens = residual_ref.shape[0]
@@ -64,17 +62,9 @@
     qkv_width = 4 * HD + value_width
     out_end = qkv_width + value_width
     adapters = 2 * slabs_x * slabs_z
-    copies = [
-        pltpu.make_async_copy(sibling_ref.at[x], other_ref.at[x], arrived.at[x])
-        for x in range(slabs_x)
-    ]
-    for copy in copies:
-        copy.start()
     normed = (rms_scale(residual_ref[...].astype(jnp.float32), 1e-06) * gain_ref[...]).astype(
         jnp.bfloat16
     )
-    for copy in copies:
-        copy.wait()
 
     def body(even_ref, odd_ref):
         def gather(z, begin, end, first_row=0, last_row=rows):
@@ -88,13 +78,15 @@
             )
 
         slab = 2 * slabs_x * rows
-        qkv = jnp.zeros((tokens, qkv_width), jnp.float32)
-        for z in range(slabs_z):
-            qkv = qkv + jnp.dot(
-                normed[:, z * slab : (z + 1) * slab],
-                gather(z, 0, qkv_width),
+        depth = slabs_z // 2
+        qkv = sum(
+            jnp.dot(
+                normed[:, z * slab : (z + depth) * slab],
+                jnp.concatenate([gather(z + i, 0, qkv_width) for i in range(depth)], axis=0),
                 preferred_element_type=jnp.float32,
             )
+            for z in range(0, slabs_z, depth)
+        )
         row_at = lax.broadcasted_iota(jnp.int32, (tokens, tokens), 0)
         column_at = lax.broadcasted_iota(jnp.int32, (tokens, tokens), 1)
         row_request = jnp.zeros((tokens, tokens), jnp.int32)
@@ -157,12 +149,8 @@
     return pl.pallas_call(
         attention_kernel,
         out_shape=jax.ShapeDtypeStruct((groups, tokens + RANK, 2 * HD), jnp.bfloat16),
-        in_specs=[smem] * 3 + [vmem] * 4 + [pl.BlockSpec(memory_space=pl.ANY)],
+        in_specs=[smem] * 3 + [vmem] * 5,
         out_specs=vmem,
-        scratch_shapes=[
-            pltpu.VMEM(other.shape, other.dtype),
-            pltpu.SemaphoreType.DMA((mine.shape[0],)),
-        ],
         compiler_params=pltpu.CompilerParams(vmem_limit_bytes=48 * 1024 * 1024),
         cost_estimate=pl.CostEstimate(
             flops=1_200_000_000, bytes_accessed=8_000_000, transcendentals=80_000

time: 175 us -> 175 us (level)
  transfers between devices with their start and end apart: 3 -> 3, of which waited for: 1 -> 1; matrix products, arithmetic and copies ran while one was open for 2% -> 2% of each run, Pallas kernels for 5% -> 4%
where the time goes in v9:
time: 175 us; the launch traced here: 172 us
  blocking collectives  122 us (70%)
  Pallas kernels  15.2 us (9%)
  between operations  14.2 us (8%)
  starting transfers between devices  10.6 us (6%)
  local copies, waits for them, and re-layouts  4.95 us (3%)
  waiting for transfers between devices  3.92 us (2%)
    all_to_all x5, blocking collectives, exchange(): return lax.all_to_all(blocks, axis, split_axis=0, concat_axis=0, tiled=True)  122 us
    pallas_call x1, Pallas kernels, feed_forward(): pl.pallas_call(feed_forward_kernel, out_shape=jax.ShapeDtypeStruct(mid.sh...  7.5 us
    ppermute x1, starting transfers between devices, sibling(): return lax.ppermute(block, 'core', [(0, 1), (1, 0)])  6.57 us
    pallas_call x1, Pallas kernels, attention(): pl.pallas_call(attention_kernel, out_shape=jax.ShapeDtypeStruct((groups,...  5.29 us
    ppermute x1, starting transfers between devices, per_device(): lax.ppermute(acts_own, 'head', [(i, i ^ 1) for i in range(groups)])  4.03 us
    ppermute x1, waiting for transfers between devices, sibling(): return lax.ppermute(block, 'core', [(0, 1), (1, 0)])  3.9 us
  transfers between devices with their start and end apart: 3, of which 1 were waited for; matrix products, arithmetic and copies ran while one was open for 2% of the time, Pallas kernels for 4%

profile of v9, /device:TPU:1, one launch (start us, length us, event | category | flops | bytes accessed | tf_op | source)
XLA Modules:
  0.0 172.0 jit_solution(10836704797579838634)
XLA Ops:
  6.5 0.0 copy-start
  6.5 0.0 all-gather.3.cloned.1.call-start
  6.5 1.0 concatenate.15
  7.5 4.0 %collective-permute-start = (bf16[32,2176]{1,0:T(8,128)(2,1)S(1)}, bf16[32,2176]{1,0:T(8,128)(2,1)S(1)}, u32[]{:S(2)}, u32[]{:S(2)}) collective-permute-start(bf16[32,2176]{1,0:T(8,128)(2,1)S(1)} %concatenate.15), channel_id=1, source_target_pairs={{0,64},{64,0},{128,192},{192,128},{256,320},{320,256},{384,448},{4... | collective-permute-start | bytes 417800 | tf_op jit(solution)/shard_map/ppermute | solution.py:376
  11.6 0.8 constant_dynamic-update-slice_fusion.4
  12.3 0.7 fusion.1
  13.1 0.0 copy-done
  13.1 0.7 constant_dynamic-update-slice_fusion.3
  13.8 0.7 constant_dynamic-update-slice_fusion.2
  14.5 0.0 collective-permute-done
  14.5 0.8 pad_maximum_fusion
  15.3 0.0 all-gather.3.cloned.1.call-update
  15.4 28.1 %all_to_all.25 = bf16[8,32,1280]{2,1,0:T(8,128)(2,1)S(1)} all-to-all(bf16[8,32,1280]{2,1,0:T(8,128)(2,1)S(1)} %broadcast_in_dim.7), channel_id=1, replica_groups=mesh['head'=8,'z'=8,'x'=4,'core'=2] {'z'}, dimensions={0} | all-to-all | bytes 1310720 | tf_op jit(solution)/shard_map/all_to_all | solution.py:332
  43.4 0.3 broadcast_in_dim.8
  43.7 0.0 copy-start.7
  43.7 0.0 copy-start.1
  43.7 0.0 copy-start.4
  43.8 0.0 copy-start.6
  43.8 33.6 %all_to_all.26.mine_ref = bf16[4,8,32,1280]{3,2,1,0:T(8,128)(2,1)S(1)} all-to-all(bf16[4,8,32,1280]{3,2,1,0:T(8,128)(2,1)S(1)} %broadcast_in_dim.8), channel_id=1, replica_groups=mesh['head'=8,'z'=8,'x'=4,'core'=2] {'x'}, dimensions={0} | all-to-all | bytes 5242880 | tf_op jit(solution)/shard_map/all_to_all | solution.py:332
  77.3 6.6 %collective-permute-start.1 = (bf16[4,8,32,1280]{3,2,1,0:T(8,128)(2,1)S(1)}, bf16[4,8,32,1280]{3,2,1,0:T(8,128)(2,1)}, u32[]{:S(2)}, u32[]{:S(2)}) collective-permute-start(bf16[4,8,32,1280]{3,2,1,0:T(8,128)(2,1)S(1)} %all_to_all.26.mine_ref), channel_id=1, source_target_pairs={{0,1},{1,0},{2,3},{3,2},{4,5},{5,4},{6,7},{7,6},{8,9},{9,8},{10,11... | collective-permute-start | bytes 7864328 | tf_op jit(solution)/shard_map/ppermute | solution.py:340
  84.6 0.0 copy-done.7
  84.6 0.1 pad_add_fusion.place_ref
  84.7 3.9 %collective-permute-done.1.other_ref = bf16[4,8,32,1280]{3,2,1,0:T(8,128)(2,1)} collective-permute-done((bf16[4,8,32,1280]{3,2,1,0:T(8,128)(2,1)S(1)}, bf16[4,8,32,1280]{3,2,1,0:T(8,128)(2,1)}, u32[]{:S(2)}, u32[]{:S(2)}) %collective-permute-start.1) | collective-permute-done | bytes 2621472 | tf_op jit(solution)/shard_map/ppermute | solution.py:340
  88.6 0.0 copy-done.1
  88.6 0.0 copy-done.4
  88.6 0.0 copy-done.6
  88.6 5.3 %shard_map.136 = bf16[8,208,256]{2,1,0:T(8,128)(2,1)S(1)} custom-call(s32[1,6]{1,0:T(1,128)S(1)} %copy-done.6, f32[1]{0:T(128)S(6)} %copy.19.lambda_ref, s32[2]{0:T(128)S(1)} %pad_add_fusion.place_ref, bf16[192,2048]{1,0:T(8,128)(2,1)S(1)} %copy-done.1, f32[1,2048]{1,0:T(1,128)S(1)} %bitcast.17, s32[1,256]{1,0:T(1,128)S(1)} %pad.4.chosen_ref, ...), custom_call_target="tpu_custom_call" | custom-call | flops 1200000000 | bytes 8000000 | tf_op jit(solution)/shard_map/pallas_call | solution.py:149
  93.9 30.5 %all_to_all.27.received_ref = bf16[8,208,256]{2,1,0:T(8,128)(2,1)S(1)} all-to-all(bf16[8,208,256]{2,1,0:T(8,128)(2,1)S(1)} %shard_map.136), channel_id=1, replica_groups=mesh['head'=8,'z'=8,'x'=4,'core'=2] {'head'}, dimensions={0} | all-to-all | bytes 1703936 | tf_op jit(solution)/shard_map/all_to_all | solution.py:332
  124.4 0.0 copy-start.5
  124.4 2.4 %shard_map.137 = (f32[192,256]{1,0:T(8,128)S(1)}, bf16[8,96,256]{2,1,0:T(8,128)(2,1)S(1)}) custom-call(s32[2]{0:T(128)S(1)} %pad_add_fusion.place_ref, s32[1,256]{1,0:T(1,128)S(1)} %pad.4.chosen_ref, bf16[192,2048]{1,0:T(8,128)(2,1)S(1)} %copy-done.1, bf16[8,208,256]{2,1,0:T(8,128)(2,1)S(1)} %all_to_all.27.received_ref, ...), custom_call_target="tpu_custom_call" | custom-call | flops 120000000 | bytes 3000000 | tf_op jit(solution)/shard_map/pallas_call | solution.py:222
  126.8 0.0 copy-start.2
  126.8 0.7 copy-done.2
  127.5 15.4 %all_to_all.28.mid_ref = bf16[8,96,256]{2,1,0:T(8,128)(2,1)S(1)} all-to-all(bf16[8,96,256]{2,1,0:T(8,128)(2,1)S(1)} %get-tuple-element.11), channel_id=1, replica_groups=mesh['head'=8,'z'=8,'x'=4,'core'=2] {'head'}, dimensions={0} | all-to-all | bytes 786432 | tf_op jit(solution)/shard_map/all_to_all | solution.py:332
  142.8 0.0 all-gather.3.cloned.1.call-done
  142.8 0.0 copy-done.5
  142.8 0.0 copy-start.3
  142.8 7.5 %shard_map.138 = bf16[8,96,256]{2,1,0:T(8,128)(2,1)S(1)} custom-call(bf16[8,96,256]{2,1,0:T(8,128)(2,1)S(1)} %all_to_all.28.mid_ref, f32[8,1,256]{2,1,0:T(1,128)S(1)} %bitcast.18, bf16[64,2,32,2176]{3,2,1,0:T(8,128)(2,1)} %bitcast.19), custom_call_target="tpu_custom_call" | custom-call | flops 1700000000 | bytes 18000000 | tf_op jit(solution)/shard_map/pallas_call | solution.py:313
  150.3 14.1 %all_to_all.29 = bf16[8,96,256]{2,1,0:T(8,128)(2,1)S(1)} all-to-all(bf16[8,96,256]{2,1,0:T(8,128)(2,1)S(1)} %shard_map.138), channel_id=1, replica_groups=mesh['head'=8,'z'=8,'x'=4,'core'=2] {'head'}, dimensions={0} | all-to-all | bytes 786432 | tf_op jit(solution)/shard_map/all_to_all | solution.py:332
  164.5 0.0 copy-done.3
  164.5 0.7 add_convert_fusion
  (8 shorter events, 0.1 us)
Async XLA Ops:
  6.5 6.5 %copy-start = (bf16[1,16,2048]{2,1,0:T(8,128)(2,1)S(1)}, bf16[1,16,2048]{2,1,0:T(8,128)(2,1)}, u32[]{:S(2)}) copy-start(bf16[1,16,2048]{2,1,0:T(8,128)(2,1)} %param.23) | copy-start | bytes 196612
  6.5 136.3 %all-gather.3.cloned.1.call-start = ((), (), s32[]{:S(2)}) async-start(), calls=%async_computation.5 | async-start | bytes 18104320 | tf_op jit(solution)/shard_map/all_gather | solution.py:378
  7.5 7.0 %collective-permute-start = (bf16[32,2176]{1,0:T(8,128)(2,1)S(1)}, bf16[32,2176]{1,0:T(8,128)(2,1)S(1)}, u32[]{:S(2)}, u32[]{:S(2)}) collective-permute-start(bf16[32,2176]{1,0:T(8,128)(2,1)S(1)} %concatenate.15), channel_id=1, source_target_pairs={{0,64},{64,0},{128,192},{192,128},{256,320},{320,256},{384,448},{4... | collective-permute-start | bytes 417800 | tf_op jit(solution)/shard_map/ppermute | solution.py:376
  43.7 40.9 %copy-start.7 = (s32[192,1]{0,1:T(1,128)S(1)}, s32[192,1]{0,1:T(1,128)}, u32[]{:S(2)}) copy-start(s32[192,1]{0,1:T(1,128)} %param.16) | copy-start | bytes 2308
  43.7 44.8 %copy-start.1 = (bf16[192,2048]{1,0:T(8,128)(2,1)S(1)}, bf16[192,2048]{1,0:T(8,128)(2,1)}, u32[]{:S(2)}) copy-start(bf16[192,2048]{1,0:T(8,128)(2,1)} %residual_ref.3) | copy-start | bytes 2359300
  43.7 44.8 %copy-start.4 = (f32[2048]{0:T(1024)S(1)}, f32[2048]{0:T(1024)}, u32[]{:S(2)}) copy-start(f32[2048]{0:T(1024)} %param.17) | copy-start | bytes 24580
  43.8 44.8 %copy-start.6 = (s32[1,6]{1,0:T(1,128)S(1)}, s32[1,6]{1,0:T(1,128)}, u32[]{:S(2)}) copy-start(s32[1,6]{1,0:T(1,128)} %lengths_ref.1) | copy-start | bytes 76
  77.3 11.2 %collective-permute-start.1 = (bf16[4,8,32,1280]{3,2,1,0:T(8,128)(2,1)S(1)}, bf16[4,8,32,1280]{3,2,1,0:T(8,128)(2,1)}, u32[]{:S(2)}, u32[]{:S(2)}) collective-permute-start(bf16[4,8,32,1280]{3,2,1,0:T(8,128)(2,1)S(1)} %all_to_all.26.mine_ref), channel_id=1, source_target_pairs={{0,1},{1,0},{2,3},{3,2},{4,5},{5,4},{6,7},{7,6},{8,9},{9,8},{10,11... | collective-permute-start | bytes 7864328 | tf_op jit(solution)/shard_map/ppermute | solution.py:340
  124.4 18.4 %copy-start.5 = (f32[2048]{0:T(1024)S(1)}, f32[2048]{0:T(1024)}, u32[]{:S(2)}) copy-start(f32[2048]{0:T(1024)} %param.24) | copy-start | bytes 24580
  126.8 0.7 copy-start.2
  142.8 21.7 %copy-start.3 = (f32[192,256]{1,0:T(8,128)S(1)}, f32[192,256]{1,0:T(8,128)}, u32[]{:S(2)}) copy-start(f32[192,256]{1,0:T(8,128)} %copy-done.2) | copy-start | bytes 589828
Sparse Core Ops, SparseCore 0:
  15.4 115.9 all-gather.2
